TPU v7x, 32 devices: a whole 2x2x4 slice. The times are simulated.
32 devices in a mesh: gx: 4 (over y, x), vert: 8 (over z, core).
Axes of the slice: x: 2, y: 2, z: 4, core: 2. Of those that a mesh axis runs over, the one named last changes fastest.
Arguments:
- dist: float32 [2, 4096, 24576], P(None, 'vert', 'gx'), may hold values from -6 to 6
- factors: float32 [2, 4096, 128], P(None, 'vert', 'gx'), may hold values from 0.95 to 0.999
- velocity: float32 [3, 2, 4096], P(None, None, 'vert'), may hold values from -3 to 3
- weights: float32 [13, 2, 4096], P(None, None, 'vert'), may hold values from -0.0625 to 0.0625
- relax: float32 [2, 4096], P(None, 'vert'), may hold values from 0.1 to 0.9
Outputs:
- updated: float32 [2, 4096, 24576], P(None, 'vert', 'gx')
- macro: float32 [13, 24576], P(None, 'gx')
All inputs are finite; a program needn't handle non-finite values.
Results may differ from a plain program's by a relative error of at most 0.000071.
Values sent between devices are 32-bit elements; how exact they have to be, the bound alone decides.
No kernel may reach another device: no remote copies, remote signals or barrier semaphores. Data moves between devices by JAX's collectives and lax.ppermute only.
A program may use at most 192 MiB of HBM per device.

v0:
```python
import jax
import jax.numpy as jnp
from jax import lax
from jax.sharding import PartitionSpec as P

SMOOTH = 4


smooth_rate = 0.24


def padded_2(cells, sides, width):
    for axis, dim in sides:
        count = lax.axis_size(axis)
        ends = count - 1
        head = lax.slice_in_dim(cells, 0, width, axis=dim)
        tail = lax.slice_in_dim(cells, cells.shape[dim] - width, cells.shape[dim], axis=dim)
        cells = jnp.concatenate(
            [
                lax.ppermute(tail, axis, [(i, (i + 1) % count) for i in range(ends)]),
                cells,
                lax.ppermute(head, axis, [((i + 1) % count, i) for i in range(ends)]),
            ],
            axis=dim,
        )
    return cells


def shifted(value, axis, steps):
    count = lax.axis_size(axis)
    leading, last = (max(0, -steps), min(count, count - steps))
    return lax.ppermute(value, axis, [(source, source + steps) for source in range(leading, last)])


def equilibrium(moments, speed_x, speed_y, speed_z):
    density = 1.0 + 0.5 * jnp.tanh(moments[0])
    flow_x = 0.5 * jnp.tanh(moments[1])
    flow_y = 0.5 * jnp.tanh(moments[2])
    flow_z = 0.5 * jnp.tanh(moments[3])
    temper = 1.0 + 0.5 * jnp.tanh(moments[4])
    stress = 0.2 * jnp.tanh(moments[5:10])
    fluxes = 0.2 * jnp.tanh(moments[10:13])
    rel_x = speed_x - flow_x
    rel_y = speed_y - flow_y
    rel_z = speed_z - flow_z
    square = rel_x * rel_x + rel_y * rel_y + rel_z * rel_z
    inverse = 1.0 / temper
    shape_term = (
        stress[0] * rel_x * rel_y
        + stress[1] * rel_x * rel_z
        + stress[2] * rel_y * rel_z
        + 0.5 * stress[3] * (rel_x * rel_x - rel_z * rel_z)
        + 0.5 * stress[4] * (rel_y * rel_y - rel_z * rel_z)
    )
    heat_term = (fluxes[0] * rel_x + fluxes[1] * rel_y + fluxes[2] * rel_z) * (
        0.5 * square * inverse - 2.5
    )
    return (
        density
        * inverse
        * jnp.sqrt(inverse)
        * jnp.exp(-0.5 * square * inverse)
        * (1.0 + (shape_term + heat_term) * inverse)
    )


def smooth_step(moments, padded):
    coef = 1.0 / (1.0 + moments[0] * moments[0])
    return moments + smooth_rate * coef * (padded[:, 2:] - 2.0 * moments + padded[:, :-2])


def smooth_margin(padded, cells):
    depth = SMOOTH
    total_cells = cells * lax.axis_size("gx")
    first = lax.axis_index("gx") * cells - depth
    for step in range(depth):
        inner = smooth_step(padded[:, 1:-1], padded)
        width = inner.shape[1]
        places = first + step + 1 + lax.broadcasted_iota(jnp.int32, (1, width, 1), 1)
        inside = (places >= 0) & (places < total_cells)
        padded = jnp.where(inside, inner, 0.0)
    return padded


def smooth_whole(moments):
    padded = padded_2(moments, (("gx", 1),), SMOOTH)
    moments = smooth_margin(padded, moments.shape[1])
    return moments


def per_device(dist, factors, velocity, weights, relax):
    cells = factors.shape[2]
    vel_dev = dist.shape[1]
    plane = dist.shape[2] // cells
    grid = dist.reshape(2, vel_dev, cells, plane)
    source = jnp.sqrt(1.0 - factors * factors)[..., None] * grid
    logs = jnp.log(factors)
    forward_sum = jnp.cumsum(logs[0], axis=-1)
    backward_sum = jnp.cumsum(logs[1][:, ::-1], axis=-1)[:, ::-1]
    totals = jnp.stack([forward_sum, backward_sum])
    positions = lax.broadcasted_iota(jnp.int32, (cells, cells), 0)
    columns = lax.broadcasted_iota(jnp.int32, (cells, cells), 1)
    lower = positions >= columns
    mask = jnp.stack([lower, columns >= positions])[:, None]
    spread = totals[..., :, None] - totals[..., None, :]
    transfer = jnp.where(mask, jnp.exp(jnp.where(mask, spread, 0.0)), 0.0)
    local = jnp.einsum("dvij,dvjc->dvic", transfer, source, precision=lax.Precision.HIGHEST)
    reach = jnp.exp(totals)
    pass_forward = reach[0][:, -1]
    pass_backward = reach[1][:, 0]
    leave_forward = local[0][:, -1, :]
    leave_backward = local[1][:, 0, :]
    length = lax.axis_size("gx")
    enter_forward = jnp.zeros_like(leave_forward)
    enter_backward = jnp.zeros_like(leave_backward)
    for step in range(length - 1):
        enter_forward = shifted(pass_forward[:, None] * enter_forward + leave_forward, "gx", 1)
        enter_backward = shifted(pass_backward[:, None] * enter_backward + leave_backward, "gx", -1)
    incoming = jnp.stack([enter_forward, enter_backward])
    swept = local + reach[..., None] * incoming[:, :, None, :]
    partial_moments = jnp.einsum("kdv,dvxc->kxc", weights, swept, precision=lax.Precision.HIGHEST)
    moments = lax.psum(partial_moments, "vert")
    moments = smooth_whole(moments)
    equil = equilibrium(
        moments,
        velocity[0][:, :, None, None],
        velocity[1][:, :, None, None],
        velocity[2][:, :, None, None],
    )
    updated = swept + relax[:, :, None, None] * (equil - swept)
    return (
        updated.reshape(2, vel_dev, cells * plane),
        moments.reshape(moments.shape[0], cells * plane),
    )


def solution(mesh):
    return jax.shard_map(
        per_device,
        mesh=mesh,
        in_specs=(
            P(None, "vert", "gx"),
            P(None, "vert", "gx"),
            P(None, None, "vert"),
            P(None, None, "vert"),
            P(None, "vert"),
        ),
        out_specs=(P(None, "vert", "gx"), P(None, "gx")),
        check_vma=False,
    )
```

profile of v0, /device:TPU:0, one launch (start us, length us, event | category | flops | bytes accessed | tf_op | source)
XLA Modules:
  0.0 462.0 jit_solution(15354596710435988809)
XLA Ops:
  7.2 1.0 fusion.85
  8.2 0.1 rev.6
  8.3 0.1 reduce_window_sum.18
  8.4 0.1 rev.7
  8.5 0.1 reduce_window_sum.17
  8.6 0.2 copy.38
  8.8 24.7 %copy.40 = f32[2,512,6144]{1,2,0:T(8,128)} copy(f32[2,512,6144]{2,1,0:T(8,128)} %param.5) | data formatting | bytes 50331648 | tf_op args[0]
  33.5 18.4 %broadcast_multiply_fusion = f32[2,512,32,192]{1,3,2,0:T(8,128)} fusion(f32[2,512,32,192]{1,3,2,0:T(8,128)} %bitcast.99, f32[2,512,32]{1,2,0:T(8,128)S(1)} %get-tuple-element.29), kind=kLoop, calls=%fused_computation.47 | loop fusion | flops 6291456 | bytes 50462720 | tf_op jit(solution)/shard_map/mul | solution.py:96
  51.9 35.3 %copy.41 = f32[2,512,32,192]{3,2,1,0:T(8,128)} copy(f32[2,512,32,192]{1,3,2,0:T(8,128)} %broadcast_multiply_fusion) | data formatting | bytes 50331648 | tf_op jit(solution)/shard_map/mul | solution.py:96
  87.2 39.0 %fusion.27 = f32[2,512,32,192]{3,2,1,0:T(8,128)} fusion(f32[2,512,32,192]{3,2,1,0:T(8,128)} %copy.41, f32[2,512,32]{2,1,0:T(8,128)S(1)} %copy.38, pred[2,32,32]{2,1,0:T(8,128)(4,1)S(1)} %pad_add_fusion), kind=kOutput, calls=%fused_computation.42 | convolution fusion | flops 2419064832 | bytes 50464768 | tf_op jit(solution)/shard_map/dvij,dvjc->dvic/dot_general | solution.py:107
  126.2 17.0 %slice_bitcast_fusion.1 = (f32[512,32,192]{2,1,0:T(8,128)S(1)}, f32[512,32,192]{2,1,0:T(8,128)}) fusion(f32[2,512,32,192]{3,2,1,0:T(8,128)} %fusion.27), kind=kLoop, calls=%fused_computation.41 | loop fusion | bytes 50331648 | tf_op jit(solution)/shard_map/squeeze | solution.py:111
  143.2 0.5 slice.197
  143.8 0.3 copy.43
  144.2 5.0 %collective-permute-start = (f32[512,192]{0,1:T(8,128)S(1)}, f32[512,192]{0,1:T(8,128)S(1)}, u32[]{:S(2)}, u32[]{:S(2)}) collective-permute-start(f32[512,192]{0,1:T(8,128)S(1)} %bitcast_add_fusion.5), channel_id=1, source_target_pairs={{0,8},{8,16},{16,24},{1,9},{9,17},{17,25},{2,10},{10,18},{18,26},{... | collective-permute-start | bytes 1179656 | tf_op jit(solution)/shard_map/ppermute | solution.py:32
  149.3 2.5 slice.201
  151.7 0.3 copy.44
  152.1 1.3 collective-permute-start.3
  153.4 4.2 collective-permute-done
  157.7 4.6 collective-permute-start.1
  162.2 6.9 %collective-permute-done.3 = f32[512,192]{0,1:T(8,128)S(1)} collective-permute-done((f32[512,192]{0,1:T(8,128)S(1)}, f32[512,192]{0,1:T(8,128)S(1)}, u32[]{:S(2)}, u32[]{:S(2)}) %collective-permute-start.3) | collective-permute-done | bytes 393248 | tf_op jit(solution)/shard_map/ppermute | solution.py:32
  169.1 0.1 bitcast_add_fusion.1
  169.2 1.3 collective-permute-start.4
  170.6 8.5 %collective-permute-start.2 = (f32[512,192]{0,1:T(8,128)S(1)}, f32[512,192]{0,1:T(8,128)S(1)}, u32[]{:S(2)}, u32[]{:S(2)}) collective-permute-start(f32[512,192]{0,1:T(8,128)S(1)} %bitcast_add_fusion.3), channel_id=1, source_target_pairs={{0,8},{8,16},{16,24},{1,9},{9,17},{17,25},{2,10},{10,18},{18,26},{... | collective-permute-start | bytes 1179656 | tf_op jit(solution)/shard_map/ppermute | solution.py:32
  179.1 6.9 %collective-permute-done.4 = f32[512,192]{0,1:T(8,128)S(1)} collective-permute-done((f32[512,192]{0,1:T(8,128)S(1)}, f32[512,192]{0,1:T(8,128)S(1)}, u32[]{:S(2)}, u32[]{:S(2)}) %collective-permute-start.4) | collective-permute-done | bytes 393248 | tf_op jit(solution)/shard_map/ppermute | solution.py:32
  186.0 1.3 collective-permute-start.5
  187.3 0.2 copy.42
  187.6 14.1 %collective-permute-done.5 = f32[512,192]{0,1:T(8,128)S(1)} collective-permute-done((f32[512,192]{0,1:T(8,128)S(1)}, f32[512,192]{0,1:T(8,128)S(1)}, u32[]{:S(2)}, u32[]{:S(2)}) %collective-permute-start.5) | collective-permute-done | bytes 393248 | tf_op jit(solution)/shard_map/ppermute | solution.py:32
  201.7 0.3 copy.45
  202.1 23.5 %multiply_add_fusion = f32[2,512,32,192]{3,2,1,0:T(8,128)} fusion(f32[2,512,32,192]{3,2,1,0:T(8,128)} %fusion.27, f32[2,512,192]{2,1,0:T(8,128)S(1)} %copy.45, f32[2,512,32]{2,1,0:T(8,128)S(1)} %copy.42), kind=kLoop, calls=%fused_computation.39 | loop fusion | flops 12582912 | bytes 51249152 | tf_op jit(solution)/shard_map/add | solution.py:120
  225.5 43.6 %fusion.36 = f32[13,32,192]{2,0,1:T(8,128)} fusion(f32[2,512,32,192]{3,2,1,0:T(8,128)} %multiply_add_fusion, f32[13,2,512]{2,1,0:T(2,128)S(1)} %copy-done), kind=kOutput, calls=%fused_computation.52 | convolution fusion | flops 981467136 | bytes 25538560 | tf_op jit(solution)/shard_map/kdv,dvxc->kxc/dot_general | solution.py:121
  269.2 56.5 %all-reduce.2.cloned.1.call-done = f32[13,32,192]{2,0,1:T(8,128)} async-done(((f32[13,32,192]{2,0,1:T(8,128)}), f32[13,32,192]{2,0,1:T(8,128)}) %all-reduce.2.cloned.1.call-update) | async-done | bytes 319504 | tf_op jit(solution)/shard_map/psum | solution.py:122
  325.7 0.9 fusion.81
  326.6 3.4 collective-permute-start.6
  330.0 1.5 collective-permute-start.7
  331.5 0.3 collective-permute-done.6
  331.8 1.1 constant_dynamic-update-slice_fusion.1
  332.9 3.2 collective-permute-done.7
  336.2 0.1 fusion.41
  336.4 0.1 fusion.44
  336.6 0.1 fusion.47
  336.8 0.1 fusion.50
  336.9 0.3 copy.49
  337.2 0.2 fusion.66
  337.5 0.9 reshape.188
  338.5 0.1 fusion.82
  338.8 56.1 %fusion.24 = f32[2,512,32,192]{3,2,1,0:T(8,128)} fusion(f32[32,192]{1,0:T(8,128)S(1)} %bitcast.107, f32[32,192]{1,0:T(8,128)S(1)} %get-tuple-element.32, f32[32,192]{1,0:T(8,128)S(1)} %bitcast.113, f32[32,192]{1,0:T(8,128)S(1)} %bitcast.114, f32[32,192]{1,0:T(8,128)S(1)} %bitcast.115, f32[32,192]{1,0:T(8,128)S(1)} %bitcast.108, f32[32,192]{1,0:T(8,128)S(1)} %bitcast.109, ...), kind=kLoop, calls=%fused_computation.36 | loop fusion | flops 257949696 | bytes 51634176 | tf_op jit(solution)/shard_map/add | solution.py:130
  394.9 35.6 %copy.53 = f32[2,512,32,192]{1,3,2,0:T(8,128)} copy(f32[2,512,32,192]{3,2,1,0:T(8,128)} %fusion.24) | data formatting | bytes 50331648 | tf_op jit(solution)/shard_map/add | solution.py:130
  430.5 24.7 %copy.55 = f32[2,512,6144]{2,1,0:T(8,128)} copy(f32[2,512,6144]{1,2,0:T(8,128)} %bitcast.100) | data formatting | bytes 50331648
  (56 shorter events, 0.9 us)
Async XLA Ops:
  7.2 318.5 %all-reduce.2.cloned.1.call-start = ((), (), s32[]{:S(2)}) async-start(), calls=%async_computation | async-start | bytes 1048576 | tf_op jit(solution)/shard_map/psum | solution.py:122
  126.2 61.3 %copy-start.1 = (f32[3,2,512]{2,1,0:T(2,128)S(1)}, f32[3,2,512]{2,1,0:T(2,128)}, u32[]{:S(2)}) copy-start(f32[3,2,512]{2,1,0:T(2,128)} %param.7) | copy-start | bytes 36868
  144.2 13.4 %collective-permute-start = (f32[512,192]{0,1:T(8,128)S(1)}, f32[512,192]{0,1:T(8,128)S(1)}, u32[]{:S(2)}, u32[]{:S(2)}) collective-permute-start(f32[512,192]{0,1:T(8,128)S(1)} %bitcast_add_fusion.5), channel_id=1, source_target_pairs={{0,8},{8,16},{16,24},{1,9},{9,17},{17,25},{2,10},{10,18},{18,26},{... | collective-permute-start | bytes 1179656 | tf_op jit(solution)/shard_map/ppermute | solution.py:32
  152.1 17.0 %collective-permute-start.3 = (f32[512,192]{0,1:T(8,128)S(1)}, f32[512,192]{0,1:T(8,128)S(1)}, u32[]{:S(2)}, u32[]{:S(2)}) collective-permute-start(f32[512,192]{0,1:T(8,128)S(1)} %bitcast_add_fusion.2), channel_id=1, source_target_pairs={{8,0},{16,8},{24,16},{9,1},{17,9},{25,17},{10,2},{18,10},{26,18},{... | collective-permute-start | bytes 1179656 | tf_op jit(solution)/shard_map/ppermute | solution.py:32
  157.7 12.8 %collective-permute-start.1 = (f32[512,192]{0,1:T(8,128)S(1)}, f32[512,192]{0,1:T(8,128)S(1)}, u32[]{:S(2)}, u32[]{:S(2)}) collective-permute-start(f32[512,192]{0,1:T(8,128)S(1)} %bitcast_add_fusion.4), channel_id=1, source_target_pairs={{0,8},{8,16},{16,24},{1,9},{9,17},{17,25},{2,10},{10,18},{18,26},{... | collective-permute-start | bytes 1179656 | tf_op jit(solution)/shard_map/ppermute | solution.py:32
  169.2 16.8 %collective-permute-start.4 = (f32[512,192]{0,1:T(8,128)S(1)}, f32[512,192]{0,1:T(8,128)S(1)}, u32[]{:S(2)}, u32[]{:S(2)}) collective-permute-start(f32[512,192]{0,1:T(8,128)S(1)} %bitcast_add_fusion.1), channel_id=1, source_target_pairs={{8,0},{16,8},{24,16},{9,1},{17,9},{25,17},{10,2},{18,10},{26,18},{... | collective-permute-start | bytes 1179656 | tf_op jit(solution)/shard_map/ppermute | solution.py:32
  170.6 17.0 %collective-permute-start.2 = (f32[512,192]{0,1:T(8,128)S(1)}, f32[512,192]{0,1:T(8,128)S(1)}, u32[]{:S(2)}, u32[]{:S(2)}) collective-permute-start(f32[512,192]{0,1:T(8,128)S(1)} %bitcast_add_fusion.3), channel_id=1, source_target_pairs={{0,8},{8,16},{16,24},{1,9},{9,17},{17,25},{2,10},{10,18},{18,26},{... | collective-permute-start | bytes 1179656 | tf_op jit(solution)/shard_map/ppermute | solution.py:32
  186.0 15.6 %collective-permute-start.5 = (f32[512,192]{0,1:T(8,128)S(1)}, f32[512,192]{0,1:T(8,128)S(1)}, u32[]{:S(2)}, u32[]{:S(2)}) collective-permute-start(f32[512,192]{0,1:T(8,128)S(1)} %bitcast_add_fusion), channel_id=1, source_target_pairs={{8,0},{16,8},{24,16},{9,1},{17,9},{25,17},{10,2},{18,10},{26,18},{... | collective-permute-start | bytes 1179656 | tf_op jit(solution)/shard_map/ppermute | solution.py:32
  202.1 23.5 %copy-start = (f32[13,2,512]{2,1,0:T(2,128)S(1)}, f32[13,2,512]{2,1,0:T(2,128)}, u32[]{:S(2)}) copy-start(f32[13,2,512]{2,1,0:T(2,128)} %param.8) | copy-start | bytes 159748
  225.5 113.3 %copy-start.2 = (f32[2,512]{1,0:T(2,128)S(1)}, f32[2,512]{1,0:T(2,128)}, u32[]{:S(2)}) copy-start(f32[2,512]{1,0:T(2,128)} %param.9) | copy-start | bytes 12292
  326.6 5.3 %collective-permute-start.6 = (f32[13,4,192]{2,0,1:T(8,128)S(1)}, f32[13,4,192]{2,0,1:T(8,128)S(1)}, u32[]{:S(2)}, u32[]{:S(2)}) collective-permute-start(f32[13,4,192]{2,0,1:T(8,128)S(1)} %get-tuple-element.13), channel_id=1, source_target_pairs={{0,8},{8,16},{16,24},{1,9},{9,17},{17,25},{2,10},{10,18},{18,26},{... | collective-permute-start | bytes 119816 | tf_op jit(solution)/shard_map/ppermute | solution.py:20
  330.0 6.2 %collective-permute-start.7 = (f32[13,4,192]{2,0,1:T(8,128)S(1)}, f32[13,4,192]{2,0,1:T(8,128)S(1)}, u32[]{:S(2)}, u32[]{:S(2)}) collective-permute-start(f32[13,4,192]{2,0,1:T(8,128)S(1)} %get-tuple-element.12), channel_id=1, source_target_pairs={{8,0},{16,8},{24,16},{9,1},{17,9},{25,17},{10,2},{18,10},{26,18},{... | collective-permute-start | bytes 119816 | tf_op jit(solution)/shard_map/ppermute | solution.py:22
Sparse Core Ops, SparseCore 0:
  269.2 56.3 all-reduce.1
where the time goes:
time: 465 us; the launch traced here: 462 us
  local copies, waits for them, and re-layouts  145 us (31%)
  other arithmetic  101 us (22%)
  waiting for transfers between devices  92.1 us (20%)
  matrix products  82.6 us (18%)
  starting transfers between devices  26.9 us (6%)
  between operations  14.6 us (3%)
    psum x1, waiting for transfers between devices, per_device(): moments = lax.psum(partial_moments, 'vert')  56.5 us
    add x1, other arithmetic, per_device(): updated = swept + relax[:, :, None, None] * (equil - swept)  56.1 us
    unnamed x25, local copies, waits for them, and re-layouts  50.6 us
    dot_general x1, matrix products, per_device(): jnp.einsum('kdv,dvxc->kxc', weights, swept, precision=lax.Precision.HIGHEST)  43.6 us
    dot_general x1, matrix products, per_device(): jnp.einsum('dvij,dvjc->dvic', transfer, source, precision=lax.Precision.H...  39 us
    add x1, local copies, waits for them, and re-layouts, per_device(): updated = swept + relax[:, :, None, None] * (equil - swept)  35.6 us
    mul x1, local copies, waits for them, and re-layouts, per_device(): source = jnp.sqrt(1.0 - factors * factors)[..., None] * grid  35.3 us
    ppermute x6, waiting for transfers between devices, shifted(): lax.ppermute(value, axis, [(source, source + steps) for source in range(l...  32 us
  transfers between devices with their start and end apart: 9, of which 7 were waited for; matrix products, arithmetic and copies ran while one was open for 1% of the time, Pallas kernels for 0%

commit v1 on v0

v1 whole, which is shorter than its diff:
```python
import jax
import jax.numpy as jnp
from jax import lax
from jax.experimental import pallas as pl
from jax.experimental.pallas import tpu as pltpu
from jax.sharding import PartitionSpec as P

SMOOTH = 4
RATE = 0.24
LANES = 128
PARTS = 2
SUB = 32
MIB = 2**20

f32 = jnp.float32
bf16 = jnp.bfloat16


def dot(a, b):
    return jnp.dot(a, b, preferred_element_type=f32)


def halves(x):
    high = x.astype(bf16)
    return high, (x - high.astype(f32)).astype(bf16)


def thirds(x):
    high = x.astype(bf16)
    rest = x - high.astype(f32)
    middle = rest.astype(bf16)
    return high, middle, (rest - middle.astype(f32)).astype(bf16)


def rounded(x):
    return lax.reduce_precision(x, 8, 7)


def outside_thirds(x):
    high = rounded(x)
    middle = rounded(x - high)
    return high.astype(bf16), middle.astype(bf16), rounded(x - high - middle).astype(bf16)


def low_half(rows):
    return lax.broadcasted_iota(jnp.int32, (rows, LANES), 1) < LANES // 2


def turn(x):
    return pltpu.roll(x, LANES // 2, 1)


def swap_cells(pair, whole, low):
    tiles = len(pair)
    turned = [turn(t) for t in pair]
    return [
        jnp.where(low, turned[(t + whole) % tiles], turned[(t + whole + 1) % tiles])
        for t in range(tiles)
    ]


def by_cell(first, second, tiles, whole, low):
    mixed = jnp.where(low, first, second)
    return [first if t < whole else mixed if t == whole else second for t in range(tiles)]


def sweep_rows(rows, load, store, gain, reach, backward, pairs, plane):
    tiles, whole = 2 * plane // LANES, plane // LANES
    low = low_half(rows)
    zero = jnp.zeros((rows, LANES), f32)
    sums, late = [zero] * tiles, [zero] * tiles
    for step in range(pairs):
        p = pairs - 1 - step if backward else step
        spread = lambda c: jnp.broadcast_to(c, (rows, LANES))
        g = by_cell(spread(gain[:, 2 * p : 2 * p + 1]), spread(gain[:, 2 * p + 1 : 2 * p + 2]), tiles, whole, low)
        r = by_cell(spread(reach[:, 2 * p : 2 * p + 1]), spread(reach[:, 2 * p + 1 : 2 * p + 2]), tiles, whole, low)
        term = [g[t] * load(p, t) for t in range(tiles)]
        early = []
        total = []
        for t in range(tiles):
            if t == whole:
                now, then = (term[t], late[t]) if not backward else (late[t], term[t])
                early.append(sums[t] + jnp.where(low, now, then))
                total.append(jnp.where(low, 0.0, term[t]) if not backward else jnp.where(low, term[t], 0.0))
            elif (t < whole) != backward:
                early.append(sums[t] + term[t])
                total.append(None)
            else:
                early.append(sums[t] + late[t])
                total.append(term[t])
        sums, late = early, term
        crossed = swap_cells(sums, whole, low)
        values = []
        for t in range(tiles):
            value = sums[t] + crossed[t]
            if total[t] is not None:
                value = value + total[t]
            values.append(r[t] * value)
            store(p, t, values[t])
    return values


def packed_last(values, backward, whole, low):
    tiles = len(values)
    if backward:
        return values[:whole], values[whole]
    turned = [turn(v) for v in values[whole:]]
    full = [jnp.where(low, turned[i], turned[i + 1]) for i in range(whole)]
    return full, turned[whole]


def sweep_kernel(part, block, plane, dist, coef, *rest):
    others = len(rest) - 1
    swept, sent = rest[0], rest[1:]
    count = others + 1
    me = lax.axis_index("gx")
    vel = swept.shape[1]
    cells = swept.shape[2] // plane
    pairs = cells // 2
    tiles, whole = 2 * plane // LANES, plane // LANES
    width = 2 * plane
    offset = part * (vel // block)

    def body(ahead, back):
        step = pl.program_id(0)
        for sub in range(block // SUB):
            here = slice(sub * SUB, (sub + 1) * SUB)
            row = pl.multiple_of(step * block + sub * SUB, SUB)
            leaving = []
            for d, ref in enumerate((ahead, back)):
                table = coef[d, pl.ds(pl.multiple_of(part * vel + row, SUB), SUB), :]

                def load(p, t):
                    return ref[here, p * width + t * LANES : p * width + (t + 1) * LANES]

                def store(p, t, value):
                    swept[d, pl.ds(row, SUB), p * width + t * LANES : p * width + (t + 1) * LANES] = value

                values = sweep_rows(
                    SUB, load, store, table[:, :cells], table[:, cells : 2 * cells], d == 1, pairs, plane
                )
                low = low_half(SUB)
                full, half = packed_last(values, d == 1, whole, low)
                both = jnp.where(low[: SUB // 2], half[: SUB // 2], turn(half[SUB // 2 :]))
                leaving.append((full, both))
            half_row = pl.multiple_of(whole * vel + row // 2, SUB // 2)
            for s in range(1, count):
                forward = (me ^ s) > me
                out = sent[s - 1]
                for w in range(whole):
                    out[pl.ds(pl.multiple_of(w * vel + row, SUB), SUB), :] = jnp.where(
                        forward, leaving[0][0][w], leaving[1][0][w]
                    )
                out[pl.ds(half_row, SUB // 2), :] = jnp.where(forward, leaving[0][1], leaving[1][1])

    pltpu.emit_pipeline(
        body,
        grid=(vel // block,),
        in_specs=[
            pl.BlockSpec((None, block, dist.shape[2]), lambda i: (0, i + offset, 0)),
            pl.BlockSpec((None, block, dist.shape[2]), lambda i: (1, i + offset, 0)),
        ],
    )(dist, dist)
    lane = lax.broadcasted_iota(jnp.int32, (8, LANES), 1)
    passed = []
    for d in range(2):
        last = (cells if d == 1 else 2 * cells - 1)
        tile = jnp.zeros((8, LANES), f32)
        for j in range(vel // 8):
            at = part * vel + 8 * j
            tile = jnp.where(lane == j, jnp.broadcast_to(coef[d, at : at + 8, last : last + 1], (8, LANES)), tile)
        passed.append(tile)
    tail = whole * vel + vel // 2
    for s in range(1, count):
        sent[s - 1][tail : tail + 8, :] = jnp.where((me ^ s) > me, passed[0], passed[1])


def moment_kernel(weight, *refs):
    parts, out = refs[:-1], refs[-1]
    vel, lanes = parts[0].shape[1], parts[0].shape[2]
    chunk = 4 * LANES
    k = out.shape[0]

    @pl.loop(0, lanes // chunk)
    def _(i):
        at = pl.ds(pl.multiple_of(i * chunk, chunk), chunk)
        total = jnp.zeros((k, chunk), f32)
        for d in range(2):
            for c, part in enumerate(parts):
                high, rest = halves(part[d, :, at])
                both = weight[d, :, c * vel : (c + 1) * vel]
                first = dot(both, high)
                total += first[:k] + first[k:] + dot(both[:k], rest)
        out[:, at] = total


def correct_kernel(plane, parts, moments, first_lhs, second_lhs, *refs):
    count = lax.axis_size("gx")
    got = refs[: parts * (count - 1)]
    entering, mine, other, work = refs[parts * (count - 1) :]
    me = lax.axis_index("gx")
    core = lax.axis_index("vert") % 2
    tiles, whole = 2 * plane // LANES, plane // LANES
    vel = entering.shape[1] // parts
    k = moments.shape[0]
    pairs = moments.shape[1] // (2 * plane)
    low = low_half(SUB)
    tail = whole * vel + vel // 2
    for c in range(parts):
        refs_c = got[c * (count - 1) : (c + 1) * (count - 1)]
        passed = [r[tail : tail + 8, :] for r in refs_c]
        scale = []
        for s in range(1, count):
            q = me ^ s
            product = jnp.ones((8, LANES), f32)
            for z in range(1, count):
                if z != s:
                    h = me ^ z
                    between = ((q < h) & (h < me)) | ((me < h) & (h < q))
                    product = product * jnp.where(between, passed[z - 1], 1.0)
            scale.append((jnp.where(q < me, product, 0.0), jnp.where(q > me, product, 0.0)))
        for sub in range(vel // SUB):
            row = sub * SUB
            full = [[jnp.zeros((SUB, LANES), f32)] * whole for _ in range(2)]
            half = [jnp.zeros((SUB, LANES), f32) for _ in range(2)]
            for s in range(1, count):
                ref = refs_c[s - 1]
                packed = ref[whole * vel + row // 2 : whole * vel + (row + SUB) // 2, :]
                ends = jnp.concatenate([packed, turn(packed)], axis=0)
                for d in range(2):
                    by = jnp.concatenate(
                        [
                            jnp.broadcast_to(scale[s - 1][d][:, j : j + 1], (8, LANES))
                            for j in range(row // 8, (row + SUB) // 8)
                        ],
                        axis=0,
                    )
                    full[d] = [full[d][w] + by * ref[w * vel + row : w * vel + row + SUB, :] for w in range(whole)]
                    half[d] = half[d] + by * ends
            for d in range(2):
                cell = full[d] + [half[d]]
                turned = [turn(x) for x in cell]
                pair = full[d] + [jnp.where(low, half[d], turned[0])]
                for w in range(whole):
                    pair.append(jnp.where(low, turned[w], turned[w + 1]))
                for t in range(tiles):
                    entering[d, c * vel + row : c * vel + row + SUB, t * LANES : (t + 1) * LANES] = pair[t]
    width = 2 * plane
    place = lax.broadcasted_iota(jnp.int32, (first_lhs.shape[1] // 3, width), 1)
    total = jnp.zeros(place.shape, f32)
    rows = place.shape[0]
    for d in range(2):
        high, rest = halves(entering[d])
        a, b = first_lhs[d], second_lhs[d]
        even = dot(a[:rows], high) + dot(a[rows : 2 * rows], high) + dot(a[:rows], rest)
        odd = dot(b[:rows], high) + dot(b[rows : 2 * rows], high) + dot(b[:rows], rest)
        total += jnp.where(place < plane, even, odd)
    work[...] = total
    for p in range(pairs):
        at = slice(p * width, (p + 1) * width)
        value = moments[:, at] + work[p * k : (p + 1) * k, :]
        half_pairs = pairs // 2
        inner = slice((p % half_pairs) * width, (p % half_pairs + 1) * width)

        @pl.when(core == p // half_pairs)
        def _():
            mine[:, inner] = value

        @pl.when(core != p // half_pairs)
        def _():
            other[:, inner] = value


def fit_rows(m):
    density = 1.0 + 0.5 * jnp.tanh(m[0:1])
    u = [0.5 * jnp.tanh(m[j : j + 1]) for j in (1, 2, 3)]
    inverse = 1.0 / (1.0 + 0.5 * jnp.tanh(m[4:5]))
    s = [0.2 * jnp.tanh(m[j : j + 1]) for j in range(5, 10)]
    q = [0.2 * jnp.tanh(m[j : j + 1]) for j in range(10, 13)]
    h = 0.5 * inverse
    uu = u[0] * u[0] + u[1] * u[1] + u[2] * u[2]
    qu = q[0] * u[0] + q[1] * u[1] + q[2] * u[2]
    e = h * 1.4426950408889634
    zero = jnp.zeros_like(e)
    exponent = [-e * uu, 2.0 * e * u[0], 2.0 * e * u[1], 2.0 * e * u[2], -e, -e, -e]
    exponent = exponent + [zero] * (16 - len(exponent))
    a = h * uu - 2.5
    xx, yy, zz = 0.5 * s[3], 0.5 * s[4], -0.5 * (s[3] + s[4])
    xy, xz, yz = s[0], s[1], s[2]
    gx = xx * u[0] + 0.5 * (xy * u[1] + xz * u[2])
    gy = yy * u[1] + 0.5 * (xy * u[0] + yz * u[2])
    gz = zz * u[2] + 0.5 * (xz * u[0] + yz * u[1])
    form = gx * u[0] + gy * u[1] + gz * u[2]
    two = 2.0 * h
    scale = density * inverse * jnp.sqrt(inverse)
    by = scale * inverse
    square = qu * h
    terms = [
        scale + by * (form - qu * a),
        by * (a * q[0] + two * qu * u[0] - 2.0 * gx),
        by * (a * q[1] + two * qu * u[1] - 2.0 * gy),
        by * (a * q[2] + two * qu * u[2] - 2.0 * gz),
        by * (xx - two * q[0] * u[0] - square),
        by * (yy - two * q[1] * u[1] - square),
        by * (zz - two * q[2] * u[2] - square),
        by * (xy - two * (q[0] * u[1] + q[1] * u[0])),
        by * (xz - two * (q[0] * u[2] + q[2] * u[0])),
        by * (yz - two * (q[1] * u[2] + q[2] * u[1])),
        by * (h * q[0]),
        by * (h * q[1]),
        by * (h * q[2]),
    ]
    terms = terms + [zero] * (16 - len(terms))
    return jnp.concatenate(exponent, axis=0), jnp.concatenate(terms, axis=0)


def stacked_right(x):
    a, b, c = thirds(x)
    return jnp.concatenate([a, b, a, c, b, a], axis=0)


def stacked_left(x):
    a, b, c = outside_thirds(x)
    return jnp.concatenate([a, a, b, a, b, c], axis=-1)


def finish_kernel(plane, parts, *refs):
    swept = refs[:parts]
    entering, coef, left_e, left_p, mine, other, edge_a, edge_b = refs[parts : parts + 8]
    updated, macro, wide, right_e, right_p = refs[parts + 8 :]
    me, count = lax.axis_index("gx"), lax.axis_size("gx")
    core = lax.axis_index("vert") % 2
    lanes = macro.shape[1]
    cells = lanes // plane
    margin = SMOOTH * plane
    half = lanes // 2
    k = wide.shape[0]
    width = 2 * plane
    pairs = cells // 2

    @pl.when(core == 0)
    def _():
        wide[:, :margin] = edge_b[...]
        wide[:, margin : margin + half] = mine[...]
        wide[:, margin + half : margin + lanes] = other[...]
        wide[:, margin + lanes :] = edge_a[...]

    @pl.when(core != 0)
    def _():
        wide[:, :margin] = edge_a[...]
        wide[:, margin : margin + half] = other[...]
        wide[:, margin + half : margin + lanes] = mine[...]
        wide[:, margin + lanes :] = edge_b[...]

    value = wide[...]
    total = value.shape[1]
    place = lax.broadcasted_iota(jnp.int32, (1, total), 1) + (me * lanes - margin)
    inside = (place >= 0) & (place < count * lanes)
    for _ in range(SMOOTH):
        rate = RATE / (1.0 + value[0:1] * value[0:1])
        rate = jnp.where(inside, rate, 0.0)
        value = value + rate * (pltpu.roll(value, plane, 1) + pltpu.roll(value, total - plane, 1) - 2.0 * value)
    value = value[:, margin : margin + lanes]
    wide[:, :lanes] = value
    macro[...] = value[: macro.shape[0]]

    @pl.loop(0, lanes // (2 * width))
    def _(i):
        at = pl.ds(pl.multiple_of(i * 2 * width, 2 * width), 2 * width)
        exponent, terms = fit_rows(wide[:, at])
        right_e[:, at] = stacked_right(exponent)
        right_p[:, at] = stacked_right(terms)

    vel = swept[0].shape[1]
    block = min(vel, 2 * LANES)
    tiles, whole = 2 * plane // LANES, plane // LANES
    low = low_half(SUB)

    def body(*outs):
        p = pl.program_id(0)
        at = pl.ds(pl.multiple_of(p * width, width), width)
        be, bp = right_e[:, at], right_p[:, at]
        for d in range(2):
            for c in range(parts):
                for row in range(0, vel, block):
                    there = slice(c * vel + row, c * vel + row + block)
                    equil = jnp.exp2(dot(left_e[d, there, :], be)) * dot(left_p[d, there, :], bp)
                    for sub in range(0, block, SUB):
                        line = slice(c * vel + row + sub, c * vel + row + sub + SUB)
                        table = coef[d, line, :]
                        kept = jnp.broadcast_to(table[:, 3 * cells : 3 * cells + 1], (SUB, LANES))
                        table = pltpu.roll(table, 4 * LANES - 2 * cells - 2 * p, 1)
                        first = jnp.broadcast_to(table[:, 0:1], (SUB, LANES))
                        second = jnp.broadcast_to(table[:, 1:2], (SUB, LANES))
                        reach = by_cell(first, second, tiles, whole, low)
                        for t in range(tiles):
                            tile = slice(t * LANES, (t + 1) * LANES)
                            here = pl.ds(pl.multiple_of(p * width + t * LANES, LANES), LANES)
                            outs[d][line, tile] = (
                                kept * swept[c][d, row + sub : row + sub + SUB, here]
                                + reach[t] * entering[d, line, tile]
                                + equil[sub : sub + SUB, tile]
                            )

    spec = lambda d: pl.BlockSpec((None, updated.shape[1], width), lambda i: (d, 0, i))
    pltpu.emit_pipeline(body, grid=(pairs,), out_specs=[spec(0), spec(1)])(updated, updated)


def in_vmem(x):
    return pltpu.with_memory_space_constraint(x, pltpu.VMEM)


def per_device(dist, factors, velocity, weights, relax):
    _, vel, lanes = dist.shape
    cells = factors.shape[2]
    plane = lanes // cells
    count = lax.axis_size("gx")
    moments_n = weights.shape[0]
    k = 16
    pairs = cells // 2
    tiles, whole = 2 * plane // LANES, plane // LANES
    width = 2 * plane
    vel_part = vel // PARTS
    vmem = pl.BlockSpec(memory_space=pltpu.VMEM)
    anywhere = pl.BlockSpec(memory_space=pl.ANY)
    params = lambda mib: pltpu.CompilerParams(vmem_limit_bytes=mib * MIB)

    reach = jnp.stack(
        [jnp.cumprod(factors[0], axis=-1), jnp.cumprod(factors[1][:, ::-1], axis=-1)[:, ::-1]]
    )
    gain = jnp.sqrt(1.0 - factors * factors) / reach
    kept = 1.0 - relax
    coef = jnp.concatenate(
        [gain, reach, reach * kept[..., None], kept[..., None], jnp.zeros((2, vel, LANES - 3 * cells - 1), f32)],
        axis=-1,
    )

    payload = whole * vel_part + vel_part // 2 + 8
    swept, sent = [], []
    for part in range(PARTS):
        out = pl.pallas_call(
            lambda *refs, part=part: sweep_kernel(part, min(SUB, vel_part), plane, *refs),
            out_shape=[pltpu.VMEM((2, vel_part, lanes), f32)]
            + [jax.ShapeDtypeStruct((payload, LANES), f32)] * (count - 1),
            in_specs=[anywhere, vmem],
            out_specs=[vmem] * count,
            compiler_params=params(16),
            name="sweep",
        )(dist, coef)
        swept.append(in_vmem(out[0]))
        sent.append(out[1:])

    got = []
    for part in range(PARTS):
        for s in range(1, count):
            got.append(lax.ppermute(sent[part][s - 1], "gx", [(i, i ^ s) for i in range(count)]))

    padded = jnp.pad(jnp.moveaxis(weights, 1, 0), ((0, 0), (0, k - moments_n), (0, 0)))
    w_high = rounded(padded)
    w_rest = rounded(padded - w_high)
    both = jnp.concatenate([w_high, w_rest], axis=1).astype(bf16)
    moments = pl.pallas_call(
        moment_kernel,
        out_shape=jax.ShapeDtypeStruct((k, lanes), f32),
        in_specs=[vmem] * (1 + PARTS),
        out_specs=vmem,
        compiler_params=params(16),
        name="moments",
    )(both, *swept)

    by_cells = jnp.moveaxis(reach, 2, 1)
    product = by_cells[:, :, None, :] * padded[:, None, :, :]
    product = product.reshape(2, pairs, 2, k, vel)
    product = jnp.moveaxis(product, 2, 0).reshape(2, 2, pairs * k, vel)
    p_high = rounded(product)
    p_rest = rounded(product - p_high)
    lhs = jnp.concatenate([p_high, p_rest, jnp.zeros_like(p_rest)], axis=2).astype(bf16)
    entering, mine, other = pl.pallas_call(
        lambda *refs: correct_kernel(plane, PARTS, *refs),
        out_shape=[
            pltpu.VMEM((2, vel, width), f32),
            jax.ShapeDtypeStruct((k, lanes // 2), f32),
            jax.ShapeDtypeStruct((k, lanes // 2), f32),
        ],
        in_specs=[vmem] * (3 + len(got)),
        out_specs=[vmem] * 3,
        scratch_shapes=[pltpu.VMEM((pairs * k, width), f32)],
        compiler_params=params(24),
        name="correct",
    )(moments, lhs[0], lhs[1], *got)

    size = lax.axis_size("vert")
    core = lax.axis_index("vert") % 2
    total = mine + lax.ppermute(other, "vert", [(i, i ^ 1) for i in range(size)])
    step = 2
    while step < size:
        total = total + lax.ppermute(total, "vert", [(i, i ^ step) for i in range(size)])
        step *= 2
    rest = lax.ppermute(total, "vert", [(i, i ^ 1) for i in range(size)])
    margin = SMOOTH * plane
    edge = jnp.where(core == 0, total[:, :margin], total[:, -margin:])
    near, far = [], []
    for g in range(count):
        for v in range(size):
            to = g - 1 if v % 2 == 0 else g + 1
            if 0 <= to < count:
                near.append((g * size + v, to * size + v))
                far.append((g * size + v, to * size + (v ^ 1)))
    edge_a = lax.ppermute(edge, ("gx", "vert"), near)
    edge_b = lax.ppermute(edge, ("gx", "vert"), far)

    vx, vy, vz = velocity[0], velocity[1], velocity[2]
    xx, yy, zz = vx * vx, vy * vy, vz * vz
    vv = xx + yy + zz
    one = jnp.ones_like(vx)
    zero = jnp.zeros_like(vx)
    base = [one, vx, vy, vz, xx, yy, zz]
    left_e = stacked_left(jnp.stack(base + [zero] * (k - len(base)), axis=-1))
    base = base + [vx * vy, vx * vz, vy * vz, vx * vv, vy * vv, vz * vv]
    left_p = stacked_left(jnp.stack(base + [zero] * (k - len(base)), axis=-1) * relax[..., None])

    depth = left_e.shape[-1]
    updated, macro = pl.pallas_call(
        lambda *refs: finish_kernel(plane, PARTS, *refs),
        out_shape=[jax.ShapeDtypeStruct(dist.shape, f32), jax.ShapeDtypeStruct((moments_n, lanes), f32)],
        in_specs=[vmem] * (PARTS + 8),
        out_specs=[anywhere, vmem],
        scratch_shapes=[
            pltpu.VMEM((k, lanes + 2 * margin), f32),
            pltpu.VMEM((depth, lanes), bf16),
            pltpu.VMEM((depth, lanes), bf16),
        ],
        compiler_params=params(24),
        name="finish",
    )(*swept, in_vmem(entering), coef, left_e, left_p, total, rest, edge_a, edge_b)
    return updated, macro


def solution(mesh):
    return jax.shard_map(
        per_device,
        mesh=mesh,
        in_specs=(
            P(None, "vert", "gx"),
            P(None, "vert", "gx"),
            P(None, None, "vert"),
            P(None, None, "vert"),
            P(None, "vert"),
        ),
        out_specs=(P(None, "vert", "gx"), P(None, "gx")),
        check_vma=False,
    )
```

time: 465 us -> 208 us (0.45)
  Pallas kernels: 0 us -> 104 us
  other arithmetic: 101 us -> 7.49 us
  local copies, waits for them, and re-layouts: 145 us -> 61.8 us
  matrix products: 82.6 us -> 0 us
  waiting for transfers between devices: 92.1 us -> 14.8 us
  between operations: 14.6 us -> 1.16 us
  starting transfers between devices: 26.9 us -> 18.2 us
    pallas_call x0 -> x5, Pallas kernels: none -> 104 us  [the longest x1 48.5 us: per_device(): pl.pallas_call(lambda *refs: finish_kernel(plane, PARTS, *refs), out_shap...]
    dot_general x2 -> x0, matrix products: 82.6 us -> none  [the longest x1 43.6 us: per_device(): jnp.einsum('kdv,dvxc->kxc', weights, swept, precision=lax.Precision.HIGHEST)]
    add x8 -> x3, other arithmetic: 79.9 us -> 1 us  [the longest x1 0.95 us: per_device(): mine + lax.ppermute(other, 'vert', [(i, i ^ 1) for i in range(size)])]
    psum x1 -> x0, waiting for transfers between devices: 56.5 us -> none  [per_device(): moments = lax.psum(partial_moments, 'vert')]
    add x1 -> x0, local copies, waits for them, and re-layouts: 35.6 us -> none  [per_device(): updated = swept + relax[:, :, None, None] * (equil - swept)]
    mul x1 -> x13, local copies, waits for them, and re-layouts: 35.3 us -> 8.48 us  [the longest x6 3.77 us: per_device(): base = base + [vx * vy, vx * vz, vy * vz, vx * vv, vy * vv, vz * vv]]
    ppermute x8 -> x12, waiting for transfers between devices: 35.6 us -> 14.8 us  [the longest x2 8.48 us: per_device(): lax.ppermute(total, 'vert', [(i, i ^ step) for i in range(size)])]
    mul x11 -> x4, other arithmetic: 18.8 us -> 1.82 us  [the longest x2 1.6 us: per_device(): base = base + [vx * vy, vx * vz, vy * vz, vx * vv, vy * vv, vz * vv]]
  transfers between devices with their start and end apart: 9 -> 12, of which waited for: 7 -> 2; matrix products, arithmetic and copies ran while one was open for 1% -> 13% of each run, Pallas kernels for 0% -> 14%
where the time goes in v1:
time: 208 us; the launch traced here: 207 us
  Pallas kernels  104 us (50%)
  local copies, waits for them, and re-layouts  61.8 us (30%)
  starting transfers between devices  18.2 us (9%)
  waiting for transfers between devices  14.8 us (7%)
  other arithmetic  7.49 us (4%)
    pallas_call x1, Pallas kernels, per_device(): pl.pallas_call(lambda *refs: finish_kernel(plane, PARTS, *refs), out_shap...  48.5 us
    pallas_call x2, Pallas kernels, per_device(): pl.pallas_call(lambda *refs, part=part: sweep_kernel(part, min(SUB, vel_p...  46.7 us
    unnamed x34, local copies, waits for them, and re-layouts  37.5 us
    ppermute x2, waiting for transfers between devices, per_device(): lax.ppermute(total, 'vert', [(i, i ^ step) for i in range(size)])  8.48 us
    ppermute x6, starting transfers between devices, per_device(): lax.ppermute(sent[part][s - 1], 'gx', [(i, i ^ s) for i in range(count)])  8.02 us
    another operation x9, local copies, waits for them, and re-layouts, per_device(): left_e = stacked_left(jnp.stack(base + [zero] * (k - len(base)), axis=-1))  7.95 us
    ppermute x6, waiting for transfers between devices, per_device(): lax.ppermute(sent[part][s - 1], 'gx', [(i, i ^ s) for i in range(count)])  6.32 us
    pallas_call x1, Pallas kernels, per_device(): pl.pallas_call(moment_kernel, out_shape=jax.ShapeDtypeStruct((k, lanes),...  5.62 us
  transfers between devices with their start and end apart: 12, of which 2 were waited for; matrix products, arithmetic and copies ran while one was open for 13% of the time, Pallas kernels for 14%

profile of v1, /device:TPU:0, one launch (start us, length us, event | category | flops | bytes accessed | tf_op | source)
XLA Modules:
  0.0 207.1 jit_solution(10310193260855270600)
XLA Ops:
  0.6 0.9 fusion.17
  1.5 1.1 copy.102
  2.6 0.7 fusion.11
  4.4 1.0 concatenate.17.refs_1_.refs_3_
  5.4 8.1 %copy-done = f32[2,512,6144]{2,1,0:T(8,128)S(1)} copy-done((f32[2,512,6144]{2,1,0:T(8,128)S(1)}, f32[2,512,6144]{2,1,0:T(8,128)}, u32[]{:S(2)}) %copy-start) | copy-done | bytes 25165848
  13.5 23.4 %sweep.3 = (f32[2,256,6144]{2,1,0:T(8,128)S(1)}, f32[392,128]{1,0:T(8,128)S(1)}, f32[392,128]{1,0:T(8,128)S(1)}, f32[392,128]{1,0:T(8,128)S(1)}) custom-call(f32[2,512,6144]{2,1,0:T(8,128)S(1)} %copy-done, f32[2,512,128]{2,1,0:T(8,128)S(1)} %concatenate.17.refs_1_.refs_3_), custom_call_target="tpu_custom_call" | custom-call | tf_op jit(solution)/shard_map/sweep/pallas_call | solution.py:441
  36.9 4.5 %copy-done.1 = f32[2,256,6144]{2,1,0:T(8,128)} copy-done((f32[2,256,6144]{2,1,0:T(8,128)}, f32[2,256,6144]{2,1,0:T(8,128)S(1)}, u32[]{:S(2)}) %copy-start.1) | copy-done | bytes 12582936
  41.4 2.9 %collective-permute-start.3 = (f32[392,128]{1,0:T(8,128)S(1)}, f32[392,128]{1,0:T(8,128)S(1)}, u32[]{:S(2)}, u32[]{:S(2)}) collective-permute-start(f32[392,128]{1,0:T(8,128)S(1)} %get-tuple-element.18), channel_id=1, source_target_pairs={{0,8},{8,0},{16,24},{24,16},{1,9},{9,1},{17,25},{25,17},{2,10},{10... | collective-permute-start | bytes 602120 | tf_op jit(solution)/shard_map/ppermute | solution.py:456
  44.3 1.5 collective-permute-start.4
  45.9 23.4 %sweep.2 = (f32[2,256,6144]{2,1,0:T(8,128)S(1)}, f32[392,128]{1,0:T(8,128)S(1)}, f32[392,128]{1,0:T(8,128)S(1)}, f32[392,128]{1,0:T(8,128)S(1)}) custom-call(f32[2,512,6144]{2,1,0:T(8,128)S(1)} %copy-done, f32[2,512,128]{2,1,0:T(8,128)S(1)} %concatenate.17.refs_1_.refs_3_), custom_call_target="tpu_custom_call" | custom-call | tf_op jit(solution)/shard_map/sweep/pallas_call | solution.py:441
  69.2 4.8 %copy-done.4 = f32[2,256,6144]{2,1,0:T(8,128)} copy-done((f32[2,256,6144]{2,1,0:T(8,128)}, f32[2,256,6144]{2,1,0:T(8,128)S(1)}, u32[]{:S(2)}) %copy-start.4) | copy-done | bytes 12582936
  74.0 2.0 collective-permute-start
  76.0 1.5 collective-permute-start.1
  77.5 1.0 copy.119
  78.6 1.0 copy.117
  79.6 1.0 copy.116
  80.7 1.0 copy.118
  82.5 4.6 %copy-done.2 = f32[2,256,6144]{2,1,0:T(8,128)S(1)} copy-done((f32[2,256,6144]{2,1,0:T(8,128)S(1)}, f32[2,256,6144]{2,1,0:T(8,128)}, u32[]{:S(2)}) %copy-start.2) | copy-done | bytes 12582936
  87.0 4.6 %copy-done.5 = f32[2,256,6144]{2,1,0:T(8,128)S(1)} copy-done((f32[2,256,6144]{2,1,0:T(8,128)S(1)}, f32[2,256,6144]{2,1,0:T(8,128)}, u32[]{:S(2)}) %copy-start.5) | copy-done | bytes 12582936
  91.6 5.6 %moments.1.refs_0_ = f32[16,6144]{1,0:T(8,128)S(1)} custom-call(bf16[2,32,512]{2,1,0:T(8,128)(2,1)S(1)} %pad_maximum_fusion.1.weight, f32[2,256,6144]{2,1,0:T(8,128)S(1)} %copy-done.5, f32[2,256,6144]{2,1,0:T(8,128)S(1)} %copy-done.2), custom_call_target="tpu_custom_call" | custom-call | tf_op jit(solution)/shard_map/moments/pallas_call | solution.py:462
  98.1 6.3 %collective-permute-done.2.refs_5_ = f32[392,128]{1,0:T(8,128)S(1)} collective-permute-done((f32[392,128]{1,0:T(8,128)S(1)}, f32[392,128]{1,0:T(8,128)S(1)}, u32[]{:S(2)}, u32[]{:S(2)}) %collective-permute-start.2) | collective-permute-done | bytes 200736 | tf_op jit(solution)/shard_map/ppermute | solution.py:456
  104.4 2.7 %correct.1 = (f32[2,512,384]{2,1,0:T(8,128)S(1)}, f32[16,3072]{1,0:T(8,128)S(1)}, f32[16,3072]{1,0:T(8,128)S(1)}) custom-call(f32[16,6144]{1,0:T(8,128)S(1)} %moments.1.refs_0_, bf16[2,768,512]{2,1,0:T(8,128)(2,1)S(1)} %get-tuple-element.25.refs_1_, bf16[2,768,512]{2,1,0:T(8,128)(2,1)S(1)} %get-tuple-element.24.refs_2_, ...), custom_call_target="tpu_custom_call" | custom-call | tf_op jit(solution)/shard_map/correct/pallas_call | solution.py:478
  107.2 1.6 fusion.6
  108.8 1.3 copy.136
  110.1 1.2 copy.134
  111.4 1.2 copy.135
  112.6 1.2 copy.129
  113.8 1.2 copy.130
  115.2 0.7 copy-done.12
  115.9 1.0 add.53
  116.9 1.6 collective-permute-start.7
  118.5 1.0 copy.138
  119.5 0.8 broadcast.21
  120.4 0.8 stack.14
  121.2 0.8 broadcast.22
  122.0 4.0 %stack.15 = f32[2,512,16]{2,1,0:T(8,128)S(1)} concatenate(f32[2,512,1]{2,1,0:T(8,128)} %broadcast.21, f32[2,512,1]{2,1,0:T(8,128)} %copy.116, f32[2,512,1]{2,1,0:T(8,128)} %copy.117, f32[2,512,1]{2,1,0:T(8,128)} %copy.118, f32[2,512,1]{2,1,0:T(8,128)S(1)} %copy-done.8, f32[2,512,1]{2,1,0:T(8,128)} %get-tuple-element.31, f32[2,512,1]{2,1,0:T(8,128)} %get-tuple-element.32, ...), dimensions={2} | concatenate | bytes 131072 | tf_op jit(solution)/shard_map/stack | solution.py:518
  126.1 2.7 %collective-permute-start.8 = (f32[16,3072]{1,0:T(8,128)S(1)}, f32[16,3072]{1,0:T(8,128)S(1)}, u32[]{:S(2)}, u32[]{:S(2)}) collective-permute-start(f32[16,3072]{1,0:T(8,128)S(1)} %add.54), channel_id=1, source_target_pairs={{0,4},{1,5},{2,6},{3,7},{4,0},{5,1},{6,2},{7,3},{8,12},{9,13},{10,... | collective-permute-start | bytes 589832 | tf_op jit(solution)/shard_map/ppermute | solution.py:497
  128.8 0.9 fusion.3
  129.7 8.5 %collective-permute-done.8 = f32[16,3072]{1,0:T(8,128)S(1)} collective-permute-done((f32[16,3072]{1,0:T(8,128)S(1)}, f32[16,3072]{1,0:T(8,128)S(1)}, u32[]{:S(2)}, u32[]{:S(2)}) %collective-permute-start.8) | collective-permute-done | bytes 196640 | tf_op jit(solution)/shard_map/ppermute | solution.py:497
  138.2 0.7 collective-permute-start.11
  138.9 1.5 collective-permute-start.10
  140.4 3.7 %collective-permute-start.9 = (f32[16,3072]{1,0:T(8,128)S(1)}, f32[16,3072]{1,0:T(8,128)S(1)}, u32[]{:S(2)}, u32[]{:S(2)}) collective-permute-start(f32[16,3072]{1,0:T(8,128)S(1)} %add.55.refs_6_), channel_id=1, source_target_pairs={{0,1},{1,0},{2,3},{3,2},{4,5},{5,4},{6,7},{7,6},{8,9},{9,8},{10,11... | collective-permute-start | bytes 589832 | tf_op jit(solution)/shard_map/ppermute | solution.py:499
  144.1 2.0 fusion.5
  146.1 1.6 concatenate.20.refs_4_
  147.7 1.7 concatenate.21.refs_5_
  149.4 4.6 %copy-done.3 = f32[2,256,6144]{2,1,0:T(8,128)S(1)} copy-done((f32[2,256,6144]{2,1,0:T(8,128)S(1)}, f32[2,256,6144]{2,1,0:T(8,128)}, u32[]{:S(2)}) %copy-start.3) | copy-done | bytes 12582936
  154.0 4.6 %copy-done.6 = f32[2,256,6144]{2,1,0:T(8,128)S(1)} copy-done((f32[2,256,6144]{2,1,0:T(8,128)S(1)}, f32[2,256,6144]{2,1,0:T(8,128)}, u32[]{:S(2)}) %copy-start.6) | copy-done | bytes 12582936
  158.6 48.5 %finish.1 = (f32[2,512,6144]{2,1,0:T(8,128)}, f32[13,6144]{1,0:T(8,128)}) custom-call(f32[2,256,6144]{2,1,0:T(8,128)S(1)} %copy-done.6, f32[2,256,6144]{2,1,0:T(8,128)S(1)} %copy-done.3, f32[2,512,384]{2,1,0:T(8,128)S(1)} %get-tuple-element.21.refs_2_, f32[2,512,128]{2,1,0:T(8,128)S(1)} %concatenate.17.refs_1_.refs_3_, ...), custom_call_target="tpu_custom_call" | custom-call | tf_op jit(solution)/shard_map/finish/pallas_call | solution.py:523
  (74 shorter events, 2.9 us)
Async XLA Ops:
  5.3 8.2 %copy-start = (f32[2,512,6144]{2,1,0:T(8,128)S(1)}, f32[2,512,6144]{2,1,0:T(8,128)}, u32[]{:S(2)}) copy-start(f32[2,512,6144]{2,1,0:T(8,128)} %refs_0_.3) | copy-start | bytes 75497472
  36.9 4.5 %copy-start.1 = (f32[2,256,6144]{2,1,0:T(8,128)}, f32[2,256,6144]{2,1,0:T(8,128)S(1)}, u32[]{:S(2)}) copy-start(f32[2,256,6144]{2,1,0:T(8,128)S(1)} %get-tuple-element.14.refs_1_) | copy-start | bytes 37748740
  41.4 56.3 %collective-permute-start.3 = (f32[392,128]{1,0:T(8,128)S(1)}, f32[392,128]{1,0:T(8,128)S(1)}, u32[]{:S(2)}, u32[]{:S(2)}) collective-permute-start(f32[392,128]{1,0:T(8,128)S(1)} %get-tuple-element.18), channel_id=1, source_target_pairs={{0,8},{8,0},{16,24},{24,16},{1,9},{9,1},{17,25},{25,17},{2,10},{10... | collective-permute-start | bytes 602120 | tf_op jit(solution)/shard_map/ppermute | solution.py:456
  44.3 53.7 %collective-permute-start.4 = (f32[392,128]{1,0:T(8,128)S(1)}, f32[392,128]{1,0:T(8,128)S(1)}, u32[]{:S(2)}, u32[]{:S(2)}) collective-permute-start(f32[392,128]{1,0:T(8,128)S(1)} %get-tuple-element.19), channel_id=1, source_target_pairs={{0,16},{8,24},{16,0},{24,8},{1,17},{9,25},{17,1},{25,9},{2,18},{10... | collective-permute-start | bytes 602120 | tf_op jit(solution)/shard_map/ppermute | solution.py:456
  45.9 31.6 %copy-start.14 = (f32[3,2,512]{2,1,0:T(2,128)S(1)}, f32[3,2,512]{2,1,0:T(2,128)}, u32[]{:S(2)}) copy-start(f32[3,2,512]{2,1,0:T(2,128)} %param.7) | copy-start | bytes 36868
  45.9 35.8 %copy-start.13 = (f32[13,2,512]{2,1,0:T(2,128)S(1)}, f32[13,2,512]{2,1,0:T(2,128)}, u32[]{:S(2)}) copy-start(f32[13,2,512]{2,1,0:T(2,128)} %param.8) | copy-start | bytes 159748
  45.9 52.2 %collective-permute-start.5 = (f32[392,128]{1,0:T(8,128)S(1)}, f32[392,128]{1,0:T(8,128)S(1)}, u32[]{:S(2)}, u32[]{:S(2)}) collective-permute-start(f32[392,128]{1,0:T(8,128)S(1)} %get-tuple-element.20), channel_id=1, source_target_pairs={{0,24},{8,16},{16,8},{24,0},{1,25},{9,17},{17,9},{25,1},{2,26},{10... | collective-permute-start | bytes 602120 | tf_op jit(solution)/shard_map/ppermute | solution.py:456
  69.2 4.8 %copy-start.4 = (f32[2,256,6144]{2,1,0:T(8,128)}, f32[2,256,6144]{2,1,0:T(8,128)S(1)}, u32[]{:S(2)}) copy-start(f32[2,256,6144]{2,1,0:T(8,128)S(1)} %get-tuple-element.13.refs_0_) | copy-start | bytes 37748740
  74.0 24.1 %collective-permute-start = (f32[392,128]{1,0:T(8,128)S(1)}, f32[392,128]{1,0:T(8,128)S(1)}, u32[]{:S(2)}, u32[]{:S(2)}) collective-permute-start(f32[392,128]{1,0:T(8,128)S(1)} %get-tuple-element.15), channel_id=1, source_target_pairs={{0,8},{8,0},{16,24},{24,16},{1,9},{9,1},{17,25},{25,17},{2,10},{10... | collective-permute-start | bytes 602120 | tf_op jit(solution)/shard_map/ppermute | solution.py:456
  76.0 22.1 %collective-permute-start.1 = (f32[392,128]{1,0:T(8,128)S(1)}, f32[392,128]{1,0:T(8,128)S(1)}, u32[]{:S(2)}, u32[]{:S(2)}) collective-permute-start(f32[392,128]{1,0:T(8,128)S(1)} %get-tuple-element.16), channel_id=1, source_target_pairs={{0,16},{8,24},{16,0},{24,8},{1,17},{9,25},{17,1},{25,9},{2,18},{10... | collective-permute-start | bytes 602120 | tf_op jit(solution)/shard_map/ppermute | solution.py:456
  82.5 4.6 %copy-start.2 = (f32[2,256,6144]{2,1,0:T(8,128)S(1)}, f32[2,256,6144]{2,1,0:T(8,128)}, u32[]{:S(2)}) copy-start(f32[2,256,6144]{2,1,0:T(8,128)} %copy-done.1) | copy-start | bytes 37748740
  87.0 4.6 %copy-start.5 = (f32[2,256,6144]{2,1,0:T(8,128)S(1)}, f32[2,256,6144]{2,1,0:T(8,128)}, u32[]{:S(2)}) copy-start(f32[2,256,6144]{2,1,0:T(8,128)} %copy-done.4) | copy-start | bytes 37748740
  97.7 6.7 %collective-permute-start.2 = (f32[392,128]{1,0:T(8,128)S(1)}, f32[392,128]{1,0:T(8,128)S(1)}, u32[]{:S(2)}, u32[]{:S(2)}) collective-permute-start(f32[392,128]{1,0:T(8,128)S(1)} %get-tuple-element.17), channel_id=1, source_target_pairs={{0,24},{8,16},{16,8},{24,0},{1,25},{9,17},{17,9},{25,1},{2,26},{10... | collective-permute-start | bytes 602120 | tf_op jit(solution)/shard_map/ppermute | solution.py:456
  98.0 9.2 %copy-start.7 = (f32[2,512,1]{2,1,0:T(8,128)S(1)}, f32[2,512,1]{2,1,0:T(8,128)}, u32[]{:S(2)}) copy-start(f32[2,512,1]{2,1,0:T(8,128)} %copy.119) | copy-start | bytes 12292
  98.0 9.2 %copy-start.9 = (f32[2,512,1]{2,1,0:T(8,128)S(1)}, f32[2,512,1]{2,1,0:T(8,128)}, u32[]{:S(2)}) copy-start(f32[2,512,1]{2,1,0:T(8,128)} %copy.117) | copy-start | bytes 12292
  98.0 9.2 %copy-start.10 = (f32[2,512,1]{2,1,0:T(8,128)S(1)}, f32[2,512,1]{2,1,0:T(8,128)}, u32[]{:S(2)}) copy-start(f32[2,512,1]{2,1,0:T(8,128)} %copy.116) | copy-start | bytes 12292
  98.1 9.2 %copy-start.11 = (f32[2,512,1]{2,1,0:T(8,128)S(1)}, f32[2,512,1]{2,1,0:T(8,128)}, u32[]{:S(2)}) copy-start(f32[2,512,1]{2,1,0:T(8,128)} %copy.118) | copy-start | bytes 12292
  107.1 11.4 %copy-start.15 = (f32[2,512]{1,0:T(2,128)S(1)}, f32[2,512]{1,0:T(2,128)}, u32[]{:S(2)}) copy-start(f32[2,512]{1,0:T(2,128)} %param.9) | copy-start | bytes 12292
  107.1 8.1 %collective-permute-start.6 = (f32[16,3072]{1,0:T(8,128)S(1)}, f32[16,3072]{1,0:T(8,128)S(1)}, u32[]{:S(2)}, u32[]{:S(2)}) collective-permute-start(f32[16,3072]{1,0:T(8,128)S(1)} %get-tuple-element.23), channel_id=1, source_target_pairs={{0,1},{1,0},{2,3},{3,2},{4,5},{5,4},{6,7},{7,6},{8,9},{9,8},{10,11... | collective-permute-start | bytes 589832 | tf_op jit(solution)/shard_map/ppermute | solution.py:494
  108.8 13.2 %copy-start.8 = (f32[2,512,1]{2,1,0:T(8,128)S(1)}, f32[2,512,1]{2,1,0:T(8,128)}, u32[]{:S(2)}) copy-start(f32[2,512,1]{2,1,0:T(8,128)} %copy.119) | copy-start | bytes 12292
  115.2 0.7 copy-start.12
  116.9 9.2 %collective-permute-start.7 = (f32[16,3072]{1,0:T(8,128)S(1)}, f32[16,3072]{1,0:T(8,128)S(1)}, u32[]{:S(2)}, u32[]{:S(2)}) collective-permute-start(f32[16,3072]{1,0:T(8,128)S(1)} %add.53), channel_id=1, source_target_pairs={{0,2},{1,3},{2,0},{3,1},{4,6},{5,7},{6,4},{7,5},{8,10},{9,11},{10,... | collective-permute-start | bytes 589832 | tf_op jit(solution)/shard_map/ppermute | solution.py:497
  126.1 12.1 %collective-permute-start.8 = (f32[16,3072]{1,0:T(8,128)S(1)}, f32[16,3072]{1,0:T(8,128)S(1)}, u32[]{:S(2)}, u32[]{:S(2)}) collective-permute-start(f32[16,3072]{1,0:T(8,128)S(1)} %add.54), channel_id=1, source_target_pairs={{0,4},{1,5},{2,6},{3,7},{4,0},{5,1},{6,2},{7,3},{8,12},{9,13},{10,... | collective-permute-start | bytes 589832 | tf_op jit(solution)/shard_map/ppermute | solution.py:497
  138.2 11.2 %collective-permute-start.11 = (f32[16,768]{1,0:T(8,128)S(1)}, f32[16,768]{1,0:T(8,128)S(1)}, u32[]{:S(2)}, u32[]{:S(2)}) collective-permute-start(f32[16,768]{1,0:T(8,128)S(1)} %slice_select_fusion), channel_id=1, source_target_pairs={{1,8},{3,10},{5,12},{7,14},{8,1},{9,16},{10,3},{11,18},{12,5},{13,... | collective-permute-start | bytes 147464 | tf_op jit(solution)/shard_map/ppermute | solution.py:510
  138.9 10.5 %collective-permute-start.10 = (f32[16,768]{1,0:T(8,128)S(1)}, f32[16,768]{1,0:T(8,128)S(1)}, u32[]{:S(2)}, u32[]{:S(2)}) collective-permute-start(f32[16,768]{1,0:T(8,128)S(1)} %slice_select_fusion), channel_id=1, source_target_pairs={{1,9},{3,11},{5,13},{7,15},{8,0},{9,17},{10,2},{11,19},{12,4},{13,... | collective-permute-start | bytes 147464 | tf_op jit(solution)/shard_map/ppermute | solution.py:509
  140.4 9.1 %collective-permute-start.9 = (f32[16,3072]{1,0:T(8,128)S(1)}, f32[16,3072]{1,0:T(8,128)S(1)}, u32[]{:S(2)}, u32[]{:S(2)}) collective-permute-start(f32[16,3072]{1,0:T(8,128)S(1)} %add.55.refs_6_), channel_id=1, source_target_pairs={{0,1},{1,0},{2,3},{3,2},{4,5},{5,4},{6,7},{7,6},{8,9},{9,8},{10,11... | collective-permute-start | bytes 589832 | tf_op jit(solution)/shard_map/ppermute | solution.py:499
  149.4 4.6 %copy-start.3 = (f32[2,256,6144]{2,1,0:T(8,128)S(1)}, f32[2,256,6144]{2,1,0:T(8,128)}, u32[]{:S(2)}) copy-start(f32[2,256,6144]{2,1,0:T(8,128)} %copy-done.1) | copy-start | bytes 37748740
  154.0 4.6 %copy-start.6 = (f32[2,256,6144]{2,1,0:T(8,128)S(1)}, f32[2,256,6144]{2,1,0:T(8,128)}, u32[]{:S(2)}) copy-start(f32[2,256,6144]{2,1,0:T(8,128)} %copy-done.4) | copy-start | bytes 37748740

commit v2 on v1

v2 whole, which is shorter than its diff:
```python
import jax
import jax.numpy as jnp
from jax import lax
from jax.experimental import pallas as pl
from jax.experimental.pallas import tpu as pltpu
from jax.sharding import PartitionSpec as P

SMOOTH = 4
RATE = 0.24
LANES = 128
PARTS = 2
BLOCK = 128
SUB = 32
ROWS = 64
GROUP = 4
MIB = 2**20

f32 = jnp.float32
bf16 = jnp.bfloat16


def dot(a, b):
    return jnp.dot(a, b, preferred_element_type=f32)


def halves(x):
    high = x.astype(bf16)
    return high, (x - high.astype(f32)).astype(bf16)


def thirds(x):
    high = x.astype(bf16)
    rest = x - high.astype(f32)
    middle = rest.astype(bf16)
    return high, middle, (rest - middle.astype(f32)).astype(bf16)


def low_half(rows):
    return lax.broadcasted_iota(jnp.int32, (rows, LANES), 1) < LANES // 2


def turn(x):
    return pltpu.roll(x, LANES // 2, 1)


def swap_cells(pair, whole, low):
    tiles = len(pair)
    turned = [turn(t) for t in pair]
    return [
        jnp.where(low, turned[(t + whole) % tiles], turned[(t + whole + 1) % tiles])
        for t in range(tiles)
    ]


def seen_before(new, old, backward, whole, low):
    first, second = (old, new) if backward else (new, old)
    return first[:whole] + [jnp.where(low, first[whole], second[whole])] + second[whole + 1 :]


def sweep_rows(rows, load, store, gains, backward, pairs, plane):
    tiles, whole = 2 * plane // LANES, plane // LANES
    low = low_half(rows)
    sums = [jnp.zeros((rows, LANES), f32)] * tiles
    for step in range(pairs):
        p = pairs - 1 - step if backward else step
        gain = gains(p)
        old = sums
        sums = [old[t] + gain[:, t * LANES : (t + 1) * LANES] * load(p, t) for t in range(tiles)]
        for t in range(tiles):
            store(p, t, sums[t])
    crossed = swap_cells(seen_before(sums, old, backward, whole, low), whole, low)
    return [sums[t] + crossed[t] for t in range(tiles)]


def packed_last(values, backward, whole, low):
    tiles = len(values)
    if backward:
        return values[:whole], values[whole]
    turned = [turn(v) for v in values[whole:]]
    full = [jnp.where(low, turned[i], turned[i + 1]) for i in range(whole)]
    return full, turned[whole]


def prepare_kernel(plane, parts, factors, reach, gain, ends, spread):
    cells, vel = factors.shape[1], factors.shape[2]
    depth = spread.shape[0]
    lane = lax.broadcasted_iota(jnp.int32, (8, LANES), 1)
    for d in range(2):
        value = factors[d]
        rows = [value[i : i + 1] for i in range(cells)]
        order = range(cells - 1, -1, -1) if d == 1 else range(cells)
        product = None
        for i in order:
            product = rows[i] if product is None else product * rows[i]
            reach[d, i : i + 1, :] = product
        whole = reach[d]
        gain[d, :, :] = turned_thirds(jnp.sqrt(1.0 - value * value) / whole, depth)
        column = jnp.concatenate([whole[i : i + 1] for i in order][-1:] * 8, axis=0)
        column = column.T
        for c in range(parts):
            tile = jnp.zeros((8, LANES), f32)
            for j in range(vel // parts // 8):
                at = c * (vel // parts) + 8 * j
                tile = jnp.where(lane == j, jnp.broadcast_to(column[at : at + 8, 0:1], (8, LANES)), tile)
            ends[2 * c + d, :, :] = tile
    row = lax.broadcasted_iota(jnp.int32, (cells, 4 * LANES), 0) * plane
    for at in range(0, spread.shape[1], 4 * LANES):
        place = lax.broadcasted_iota(jnp.int32, (cells, 4 * LANES), 1) + at
        own = jnp.where((place >= row) & (place < row + plane), 1.0, 0.0).astype(bf16)
        for i in range(3):
            spread[i * cells : (i + 1) * cells, at : at + 4 * LANES] = own
        if depth > 3 * cells:
            spread[3 * cells :, at : at + 4 * LANES] = jnp.zeros((depth - 3 * cells, 4 * LANES), bf16)


def turned_thirds(x, depth):
    terms = [t.astype(f32) for t in thirds(x)]
    rest = depth - 3 * x.shape[0]
    if rest:
        terms.append(jnp.zeros((rest, x.shape[1]), f32))
    return jnp.concatenate(terms, axis=0).T.astype(bf16)


def sweep_kernel(part, rows, plane, dist, gain, ends, spread, *rest):
    swept, sent = rest[0], rest[1:]
    count = len(sent) + 1
    me = lax.axis_index("gx")
    vel = swept.shape[1]
    pairs = swept.shape[2] // plane // 2
    whole = plane // LANES
    width = 2 * plane
    offset = part * (vel // rows)
    low = low_half(rows)
    some = min(ROWS, rows)

    def body(ref):
        step = pl.program_id(0)
        row = pl.multiple_of(step // 2 * rows, rows)

        def one(d):
            table = gain[d, pl.ds(pl.multiple_of(part * vel + row, rows), rows), :]

            def gains(p):
                return dot(table, spread[:, p * width : (p + 1) * width])

            def load(p, t):
                return ref[:, p * width + t * LANES : p * width + (t + 1) * LANES]

            def store(p, t, value):
                swept[d, pl.ds(row, rows), p * width + t * LANES : p * width + (t + 1) * LANES] = value

            values = sweep_rows(rows, load, store, gains, d == 1, pairs, plane)
            full, half = packed_last(values, d == 1, whole, low)
            both = [
                jnp.where(low[: some // 2], half[n : n + some // 2], turn(half[n + some // 2 : n + some]))
                for n in range(0, rows, some)
            ]
            for s in range(1, count):
                out = sent[s - 1]

                @pl.when(((me ^ s) > me) == (d == 0))
                def _():
                    for w in range(whole):
                        out[pl.ds(pl.multiple_of(w * vel + row, rows), rows), :] = full[w]
                    for n, packed in enumerate(both):
                        out[pl.ds(pl.multiple_of(whole * vel + (row + n * some) // 2, some // 2), some // 2), :] = packed

        for d in range(2):
            pl.when(step % 2 == d)(lambda d=d: one(d))

    pltpu.emit_pipeline(
        body,
        grid=(2 * vel // rows,),
        in_specs=[
            pl.BlockSpec(
                (None, rows, dist.shape[2]), lambda i: (i % 2, i // 2 + offset, 0), pipeline_mode=pl.Buffered(3)
            )
        ],
    )(dist)
    tail = whole * vel + vel // 2
    for s in range(1, count):
        sent[s - 1][tail : tail + 8, :] = jnp.where((me ^ s) > me, ends[2 * part], ends[2 * part + 1])


def moment_kernel(plane, parts, reach, weight, *refs):
    sums = refs[:parts]
    out, high_lhs, rest_lhs, next_high, next_rest = refs[parts:]
    vel = sums[0].shape[1]
    k = weight.shape[1]
    width = 2 * plane
    pairs = next_high.shape[1] // k
    whole = plane // LANES
    low = low_half(k)
    for d in range(2):
        for p in range(pairs):
            rows = [weight[d] * reach[d, 2 * p : 2 * p + 1, :], weight[d] * reach[d, 2 * p + 1 : 2 * p + 2, :]]
            both = slice(2 * p * k, 2 * (p + 1) * k)
            high_lhs[d, both, :], rest_lhs[d, both, :] = halves(jnp.concatenate(rows, axis=0))
            q = p + 1 if d == 1 else p - 1
            if 0 <= q < pairs:
                at = slice(q * k, (q + 1) * k)
                next_high[d, at, :], next_rest[d, at, :] = halves(rows[d])
        q = 0 if d == 1 else pairs - 1
        at = slice(q * k, (q + 1) * k)
        next_high[d, at, :] = jnp.zeros((k, weight.shape[2]), bf16)
        next_rest[d, at, :] = jnp.zeros((k, weight.shape[2]), bf16)
    first = lax.broadcasted_iota(jnp.int32, (k, width), 1) < plane
    out[...] = jnp.zeros(out.shape, f32)

    def exchanged(x):
        tiles = [x[:, t : t + LANES] for t in range(0, width, LANES)]
        return jnp.concatenate(swap_cells(tiles, whole, low), axis=1)

    @pl.loop(0, pairs)
    def _(p):
        at = pl.ds(pl.multiple_of(p * width, width), width)
        ahead = jnp.minimum(p + 1, pairs - 1)
        behind = jnp.maximum(p - 1, 0)
        here = jnp.zeros((k, width), f32)
        for d in range(2):
            total = jnp.zeros((3 * k, width), f32)
            for c, part in enumerate(sums):
                high, rest = halves(part[d, :, at])
                cols = slice(c * vel, (c + 1) * vel)
                own = pl.ds(pl.multiple_of(p * 2 * k, 2 * k), 2 * k)
                after = pl.ds(pl.multiple_of(p * k, k), k)
                left = [high_lhs[d, own, cols], next_high[d, after, cols], rest_lhs[d, own, cols], next_rest[d, after, cols]]
                main = dot(jnp.concatenate(left, axis=0), high)
                total += main[: 3 * k] + main[3 * k :] + dot(jnp.concatenate(left[:2], axis=0), rest)
            even, odd, after = total[:k], total[k : 2 * k], total[2 * k :]
            if d == 0:
                here += jnp.where(first, even, odd + exchanged(odd))
                moved = jnp.where(first, exchanged(after), 0.0)
                out[:, pl.ds(pl.multiple_of(ahead * width, width), width)] += moved
            else:
                here += jnp.where(first, even + exchanged(even), odd)
                moved = jnp.where(first, 0.0, exchanged(after))
                out[:, pl.ds(pl.multiple_of(behind * width, width), width)] += moved
        out[:, at] += here


def correct_kernel(plane, part, last, moments, high_lhs, rest_lhs, *refs):
    count = lax.axis_size("gx")
    refs_c, refs = refs[: count - 1], refs[count - 1 :]
    entering, outs, (natural, work) = refs[0], refs[1:-2], refs[-2:]
    me = lax.axis_index("gx")
    core = lax.axis_index("vert") % 2
    tiles, whole = 2 * plane // LANES, plane // LANES
    vel = entering.shape[1]
    k = moments.shape[0]
    pairs = moments.shape[1] // (2 * plane)
    rows = min(ROWS, vel)
    low = low_half(rows)
    tail = whole * vel + vel // 2
    passed = [r[tail : tail + 8, :] for r in refs_c]
    scale = []
    for s in range(1, count):
        q = me ^ s
        product = jnp.ones((8, LANES), f32)
        for z in range(1, count):
            if z != s:
                h = me ^ z
                between = ((q < h) & (h < me)) | ((me < h) & (h < q))
                product = product * jnp.where(between, passed[z - 1], 1.0)
        product = product * passed[s - 1]
        scale.append((jnp.where(q < me, product, 0.0), jnp.where(q > me, product, 0.0)))
    for sub in range(vel // rows):
        row = sub * rows
        full = [[jnp.zeros((rows, LANES), f32)] * whole for _ in range(2)]
        half = [jnp.zeros((rows, LANES), f32) for _ in range(2)]
        for s in range(1, count):
            ref = refs_c[s - 1]
            packed = ref[whole * vel + row // 2 : whole * vel + (row + rows) // 2, :]
            ends = jnp.concatenate([packed, turn(packed)], axis=0)
            for d in range(2):
                by = jnp.concatenate(
                    [
                        jnp.broadcast_to(scale[s - 1][d][:, j : j + 1], (8, LANES))
                        for j in range(row // 8, (row + rows) // 8)
                    ],
                    axis=0,
                )
                full[d] = [full[d][w] + by * ref[w * vel + row : w * vel + row + rows, :] for w in range(whole)]
                half[d] = half[d] + by * ends
        for d in range(2):
            cell = full[d] + [half[d]]
            for t in range(whole + 1):
                natural[d, row : row + rows, t * LANES : (t + 1) * LANES] = cell[t]
            turned = [turn(x) for x in cell]
            pair = full[d] + [jnp.where(low, half[d], turned[0])]
            for w in range(whole):
                pair.append(jnp.where(low, turned[w], turned[w + 1]))
            for t in range(tiles):
                entering[d, row : row + rows, t * LANES : (t + 1) * LANES] = pair[t]
    low = low_half(k)
    cols = slice(part * vel, (part + 1) * vel)
    for d in range(2):
        high, rest = halves(natural[d])
        total = dot(high_lhs[d, :, cols], high) + dot(rest_lhs[d, :, cols], high) + dot(high_lhs[d, :, cols], rest)
        if d == 0:
            work[...] = total
        else:
            work[...] += total
    half_pairs = pairs // 2
    width = 2 * plane
    for p in range(pairs):
        first, second = ([work[(2 * p + i) * k : (2 * p + i + 1) * k, t : t + LANES] for t in range(0, (whole + 1) * LANES, LANES)] for i in range(2))
        turned = [turn(x) for x in second]
        term = first[:whole] + [jnp.where(low, first[whole], turned[0])]
        term += [jnp.where(low, turned[w], turned[w + 1]) for w in range(whole)]
        value = moments[:, p * width : (p + 1) * width] + jnp.concatenate(term, axis=1)
        if not last:
            outs[0][:, p * width : (p + 1) * width] = value
            continue
        mine, other = outs
        inner = slice((p % half_pairs) * width, (p % half_pairs + 1) * width)

        @pl.when(core == p // half_pairs)
        def _():
            mine[:, inner] = value

        @pl.when(core != p // half_pairs)
        def _():
            other[:, inner] = value


def fit_rows(m):
    density = 1.0 + 0.5 * jnp.tanh(m[0:1])
    u = [0.5 * jnp.tanh(m[j : j + 1]) for j in (1, 2, 3)]
    inverse = 1.0 / (1.0 + 0.5 * jnp.tanh(m[4:5]))
    s = [0.2 * jnp.tanh(m[j : j + 1]) for j in range(5, 10)]
    q = [0.2 * jnp.tanh(m[j : j + 1]) for j in range(10, 13)]
    h = 0.5 * inverse
    uu = u[0] * u[0] + u[1] * u[1] + u[2] * u[2]
    qu = q[0] * u[0] + q[1] * u[1] + q[2] * u[2]
    e = h * 1.4426950408889634
    zero = jnp.zeros_like(e)
    exponent = [-e * uu, 2.0 * e * u[0], 2.0 * e * u[1], 2.0 * e * u[2], -e, -e, -e]
    exponent = exponent + [zero] * (16 - len(exponent))
    a = h * uu - 2.5
    xx, yy, zz = 0.5 * s[3], 0.5 * s[4], -0.5 * (s[3] + s[4])
    xy, xz, yz = s[0], s[1], s[2]
    gx = xx * u[0] + 0.5 * (xy * u[1] + xz * u[2])
    gy = yy * u[1] + 0.5 * (xy * u[0] + yz * u[2])
    gz = zz * u[2] + 0.5 * (xz * u[0] + yz * u[1])
    form = gx * u[0] + gy * u[1] + gz * u[2]
    two = 2.0 * h
    scale = density * inverse * jnp.sqrt(inverse)
    by = scale * inverse
    square = qu * h
    terms = [
        scale + by * (form - qu * a),
        by * (a * q[0] + two * qu * u[0] - 2.0 * gx),
        by * (a * q[1] + two * qu * u[1] - 2.0 * gy),
        by * (a * q[2] + two * qu * u[2] - 2.0 * gz),
        by * (xx - two * q[0] * u[0] - square),
        by * (yy - two * q[1] * u[1] - square),
        by * (zz - two * q[2] * u[2] - square),
        by * (xy - two * (q[0] * u[1] + q[1] * u[0])),
        by * (xz - two * (q[0] * u[2] + q[2] * u[0])),
        by * (yz - two * (q[1] * u[2] + q[2] * u[1])),
        by * (h * q[0]),
        by * (h * q[1]),
        by * (h * q[2]),
    ]
    terms = terms + [zero] * (16 - len(terms))
    return jnp.concatenate(exponent, axis=0), jnp.concatenate(terms, axis=0)


def stacked_right(x):
    a, b, c = thirds(x)
    return jnp.concatenate([a, b, a, c, b, a, jnp.zeros((LANES - 96, x.shape[1]), bf16)], axis=0)


def table_kernel(velocity, relax, reach, _, left_e, left_p, left_r):
    for d in range(2):
        fraction = relax[d]
        x, y, z = (velocity[j, d] for j in range(3))
        xx, yy, zz = x * x, y * y, z * z
        square = xx + yy + zz
        rows = [jnp.ones_like(x), x, y, z, xx, yy, zz, x * y, x * z, y * z, x * square, y * square, z * square]
        rows = jnp.concatenate(rows + [jnp.zeros_like(x)] * (16 - len(rows)), axis=0)
        for ref, value in ((left_e, rows), (left_p, rows * fraction)):
            a, b, c = (t.astype(f32) for t in thirds(value))
            stack = [a, a, b, a, b, c]
            rest = ref.shape[2] - 16 * len(stack)
            if rest:
                stack.append(jnp.zeros((rest, value.shape[1]), f32))
            ref[d, :, :] = jnp.concatenate(stack, axis=0).T.astype(bf16)
        left_r[d, :, :] = turned_thirds(reach[d] * (1.0 - fraction), left_r.shape[2])


def fit_kernel(plane, own, rest, macro, right_e, right_p, wide):
    me, count = lax.axis_index("gx"), lax.axis_size("gx")
    core = lax.axis_index("vert") % 2
    lanes = macro.shape[1]
    cells = lanes // plane
    margin = SMOOTH * plane
    half = lanes // 2
    width = 2 * plane

    for first, left, right in ((0, own, rest), (1, rest, own)):

        @pl.when(core == first)
        def _():
            wide[:, :margin] = left[:, half:]
            wide[:, margin : margin + half] = left[:, :half]
            wide[:, margin + half : margin + lanes] = right[:, :half]
            wide[:, margin + lanes :] = right[:, half:]

    value = wide[...]
    total = value.shape[1]
    place = lax.broadcasted_iota(jnp.int32, (1, total), 1) + (me * lanes - margin)
    inside = (place >= 0) & (place < count * lanes)
    for _ in range(SMOOTH):
        rate = RATE / (1.0 + value[0:1] * value[0:1])
        rate = jnp.where(inside, rate, 0.0)
        value = value + rate * (pltpu.roll(value, plane, 1) + pltpu.roll(value, total - plane, 1) - 2.0 * value)
    value = value[:, margin : margin + lanes]
    wide[:, :lanes] = value
    macro[...] = value[: macro.shape[0]]

    @pl.loop(0, lanes // (2 * width))
    def _(i):
        at = pl.ds(pl.multiple_of(i * 2 * width, 2 * width), 2 * width)
        exponent, terms = fit_rows(wide[:, at])
        right_e[:, at] = stacked_right(exponent)
        right_p[:, at] = stacked_right(terms)


def join_kernel(plane, d, offset, sums, entering, left, spread, _, kept):
    vel = sums.shape[1]
    width = 2 * plane
    tiles, whole = width // LANES, plane // LANES
    pairs = sums.shape[2] // width
    rows = min(ROWS, vel)
    low = low_half(rows)

    def pair(i):
        p = i if d == 1 else pairs - 1 - i
        before = jnp.minimum(p + 1, pairs - 1) if d == 1 else jnp.maximum(p - 1, 0)
        there = jnp.where(i == pairs - 1, 0.0, 1.0)
        place = lambda q, t: pl.ds(pl.multiple_of(q * width + t * LANES, LANES), LANES)
        crossed = []
        for row in range(0, vel, rows):
            line = slice(row, row + rows)
            own = [sums[d, line, place(p, t)] for t in range(tiles)]
            past = [
                None if (t < whole) != (d == 1) and t != whole else there * sums[d, line, place(before, t)]
                for t in range(tiles)
            ]
            crossed.append(swap_cells(seen_before(own, past, d == 1, whole, low), whole, low))
        right = spread[:, pl.ds(pl.multiple_of(p * width, width), width)]
        reach = dot(left[d, offset : offset + vel, :], right)
        for n, row in enumerate(range(0, vel, rows)):
            line = slice(row, row + rows)
            for t in range(tiles):
                tile = slice(t * LANES, (t + 1) * LANES)
                value = sums[d, line, place(p, t)] + crossed[n][t] + entering[d, line, tile]
                kept[d, line, place(p, t)] = reach[line, tile] * value

    @pl.loop(0, pairs // GROUP)
    def _(i):
        for u in range(GROUP):
            pair(i * GROUP + u)


def edge_of(x, width):
    return jnp.where(lax.axis_index("vert") % 2 == 0, x[:, :width], x[:, x.shape[1] - width :])


def add_kernel(a, b, *refs):
    out = refs[-1]
    out[...] = a[...] + b[...]


def edge_kernel(a, b, *refs):
    out, edge = refs[-2:]
    out[...] = a[...] + b[...]
    edge[...] = edge_of(out, edge.shape[1])


def close_kernel(a, b, halo, more, *refs):
    out, lanes = refs[-1], a.shape[1]
    out[:, :lanes] = a[...] + b[...]
    out[:, lanes:] = halo[...] + more[...]


def finish_kernel(plane, parts, *refs):
    kept = refs[:parts]
    left_e, left_p, right_e, right_p, updated = refs[parts:]
    vel = kept[0].shape[1]
    width = 4 * plane
    block = min(vel, BLOCK)

    def body(*outs):
        at = pl.ds(pl.multiple_of(pl.program_id(0) * width, width), width)
        be, bp = right_e[:, at], right_p[:, at]
        for d in range(2):
            for c in range(parts):
                for row in range(0, vel, block):
                    there = slice(c * vel + row, c * vel + row + block)
                    equil = jnp.exp2(dot(left_e[d, there, :], be)) * dot(left_p[d, there, :], bp)
                    outs[d][there, :] = kept[c][d, row : row + block, at] + equil

    spec = lambda d: pl.BlockSpec((None, updated.shape[1], width), lambda i: (d, 0, i))
    pltpu.emit_pipeline(body, grid=(updated.shape[2] // width,), out_specs=[spec(0), spec(1)])(updated, updated)


def in_vmem(x):
    return pltpu.with_memory_space_constraint(x, pltpu.VMEM)


def per_device(dist, factors, velocity, weights, relax):
    _, vel, lanes = dist.shape
    cells = factors.shape[2]
    plane = lanes // cells
    count = lax.axis_size("gx")
    moments_n = weights.shape[0]
    k = 16
    pairs = cells // 2
    tiles, whole = 2 * plane // LANES, plane // LANES
    width = 2 * plane
    vel_part = vel // PARTS
    vmem = pl.BlockSpec(memory_space=pltpu.VMEM)
    anywhere = pl.BlockSpec(memory_space=pl.ANY)
    params = pltpu.CompilerParams(vmem_limit_bytes=12 * MIB)

    depth = -(-3 * cells // LANES) * LANES
    reach, gain, ends, spread = pl.pallas_call(
        lambda *refs: prepare_kernel(plane, PARTS, *refs),
        out_shape=[
            jax.ShapeDtypeStruct((2, cells, vel), f32),
            pltpu.VMEM((2, vel, depth), bf16),
            pltpu.VMEM((2 * PARTS, 8, LANES), f32),
            pltpu.VMEM((depth, lanes), bf16),
        ],
        in_specs=[vmem],
        out_specs=[vmem] * 4,
        compiler_params=params,
        name="prepare",
    )(jnp.swapaxes(factors, 1, 2))
    gain, ends, spread = in_vmem(gain), in_vmem(ends), in_vmem(spread)
    dist = pltpu.with_memory_space_constraint(dist, pltpu.HBM)

    payload = whole * vel_part + vel_part // 2 + 8
    swept, sent = [], []
    for part in range(PARTS):
        out = pl.pallas_call(
            lambda *refs, part=part: sweep_kernel(part, min(BLOCK, vel_part), plane, *refs),
            out_shape=[pltpu.VMEM((2, vel_part, lanes), f32)]
            + [jax.ShapeDtypeStruct((payload, LANES), f32)] * (count - 1),
            in_specs=[pl.BlockSpec(memory_space=pltpu.HBM), vmem, vmem, vmem],
            out_specs=[vmem] * count,
            compiler_params=params,
            name="sweep",
        )(dist, gain, ends, spread)
        swept.append(in_vmem(out[0]))
        sent.append(out[1:])

    padded = jnp.pad(jnp.moveaxis(weights, 1, 0), ((0, 0), (0, k - moments_n), (0, 0)))
    moments, *lhs = pl.pallas_call(
        lambda *refs: moment_kernel(plane, PARTS, *refs),
        out_shape=[jax.ShapeDtypeStruct((k, lanes), f32)]
        + [pltpu.VMEM((2, 2 * pairs * k, vel), bf16)] * 2,
        in_specs=[vmem] * (2 + PARTS),
        out_specs=[vmem] * 3,
        scratch_shapes=[pltpu.VMEM((2, pairs * k, vel), bf16)] * 2,
        compiler_params=params,
        name="moments",
    )(reach, padded, *swept)

    left_e, left_p, left_r = pl.pallas_call(
        table_kernel,
        out_shape=[pltpu.VMEM((2, vel, LANES), bf16)] * 2 + [pltpu.VMEM((2, vel, depth), bf16)],
        in_specs=[vmem] * 3 + [anywhere],
        out_specs=[vmem] * 3,
        compiler_params=params,
        name="tables",
    )(velocity[:, :, None, :], relax[:, None, :], reach, moments)

    entering = []
    for part in range(PARTS):
        last = part == PARTS - 1
        got = [
            lax.ppermute(sent[part][s - 1], "gx", [(i, i ^ s) for i in range(count)]) for s in range(1, count)
        ]
        out = [jax.ShapeDtypeStruct((k, lanes // 2), f32)] * 2 if last else [jax.ShapeDtypeStruct((k, lanes), f32)]
        found, *moments = pl.pallas_call(
            lambda *refs, part=part, last=last: correct_kernel(plane, part, last, *refs),
            out_shape=[pltpu.VMEM((2, vel_part, width), f32)] + out,
            in_specs=[vmem] * (3 + len(got)),
            out_specs=[vmem] * (1 + len(out)),
            scratch_shapes=[
                pltpu.VMEM((2, vel_part, (whole + 1) * LANES), f32),
                pltpu.VMEM((2 * pairs * k, (whole + 1) * LANES), f32),
            ],
            compiler_params=params,
            name="correct",
        )(*(moments if part else [moments]), *[in_vmem(x) for x in lhs], *got)
        entering.append(in_vmem(found))
    mine, other = moments

    size = lax.axis_size("vert")
    margin = SMOOTH * plane
    half = (k, lanes // 2)
    kept = list(swept)

    def join(part, d, after):
        kept[part] = pl.pallas_call(
            lambda *refs: join_kernel(plane, d, part * vel_part, *refs),
            out_shape=pltpu.VMEM(kept[part].shape, f32),
            in_specs=[vmem] * 4 + [anywhere],
            out_specs=vmem,
            input_output_aliases={0: 0},
            compiler_params=params,
            cost_estimate=pl.CostEstimate(
                flops=4 * dist.size * LANES // (2 * PARTS), bytes_accessed=4 * dist.size // PARTS, transcendentals=0
            ),
            name="join",
        )(in_vmem(kept[part]), entering[part], in_vmem(left_r), spread, after)
        return in_vmem(kept[part])

    def combine(kernel, out, *args):
        done = [x for x in args if x is not None]
        return pl.pallas_call(
            kernel,
            out_shape=[jax.ShapeDtypeStruct(x, f32) for x in out],
            in_specs=[vmem] * len(done),
            out_specs=[vmem] * len(out),
            compiler_params=params,
            name=kernel.__name__,
        )(*done)

    steps = [1]
    while 2 * steps[-1] < size:
        steps.append(2 * steps[-1])
    total, beside = mine, None
    chunks = [(part, d) for part in range(PARTS) for d in range(2)]
    for i, step in enumerate(steps[:-1]):
        got = lax.ppermute(total if i else other, "vert", [(v, v ^ step) for v in range(size)])
        if i:
            beside = join(*chunks.pop(0), total) if len(chunks) > 3 else None
        if i == len(steps) - 2:
            total, edge = combine(edge_kernel, [half, (k, margin)], total, got, beside)
        else:
            (total,) = combine(add_kernel, [half], total, got, beside)
    step = steps[-1]
    got = lax.ppermute(total, "vert", [(v, v ^ step) for v in range(size)])
    beyond = []
    for g in range(count - 1):
        for v in range(1, size, 2):
            near, far = g * size + v, (g + 1) * size + v - 1
            beyond += [(near, far), (far, near)]
    halo = lax.ppermute(edge, ("gx", "vert"), beyond)
    join(*chunks.pop(0), total)
    more = lax.ppermute(halo, "vert", [(v, v ^ step) for v in range(size)])
    while chunks:
        join(*chunks.pop(0), halo)
    (own,) = combine(close_kernel, [(k, lanes // 2 + margin)], total, got, halo, more, *[in_vmem(x) for x in kept])
    rest = lax.ppermute(own, "vert", [(v, v ^ 1) for v in range(size)])

    macro, right_e, right_p = pl.pallas_call(
        lambda *refs: fit_kernel(plane, *refs),
        out_shape=[jax.ShapeDtypeStruct((moments_n, lanes), f32)] + [pltpu.VMEM((LANES, lanes), bf16)] * 2,
        in_specs=[vmem] * 2,
        out_specs=[vmem] * 3,
        scratch_shapes=[pltpu.VMEM((k, lanes + 2 * margin), f32)],
        compiler_params=params,
        name="fit",
    )(own, rest)

    last = [*kept, left_e, left_p, right_e, right_p]
    updated = pl.pallas_call(
        lambda *refs: finish_kernel(plane, PARTS, *refs),
        out_shape=jax.ShapeDtypeStruct(dist.shape, f32),
        in_specs=[vmem] * len(last),
        out_specs=anywhere,
        compiler_params=params,
        name="finish",
    )(*[in_vmem(x) for x in last])
    return updated, macro


def solution(mesh):
    return jax.shard_map(
        per_device,
        mesh=mesh,
        in_specs=(
            P(None, "vert", "gx"),
            P(None, "vert", "gx"),
            P(None, None, "vert"),
            P(None, None, "vert"),
            P(None, "vert"),
        ),
        out_specs=(P(None, "vert", "gx"), P(None, "gx")),
        check_vma=False,
    )
```

time: 208 us -> 75.5 us (0.36)
  local copies, waits for them, and re-layouts: 61.8 us -> 0.95 us
  Pallas kernels: 104 us -> 53.5 us
  waiting for transfers between devices: 14.8 us -> 3.55 us
  other arithmetic: 7.49 us -> 0 us
    pallas_call x1, Pallas kernels: 48.5 us -> 10.7 us  [per_device(): pl.pallas_call(lambda *refs: finish_kernel(plane, PARTS, *refs), out_shap...]
    unnamed x34 -> x9, local copies, waits for them, and re-layouts: 37.5 us -> 0.93 us
    pallas_call x4 -> x15, Pallas kernels: 55 us -> 42.8 us  [the longest x4 15.8 us: join(): pl.pallas_call(lambda *refs: join_kernel(plane, d, part * vel_part, *refs...]
    another operation x16 -> x0, local copies, waits for them, and re-layouts: 9.94 us -> none  [the longest x9 7.95 us: per_device(): left_e = stacked_left(jnp.stack(base + [zero] * (k - len(base)), axis=-1))]
    mul x13 -> x0, local copies, waits for them, and re-layouts: 8.48 us -> none  [the longest x6 3.77 us: per_device(): base = base + [vx * vy, vx * vz, vy * vz, vx * vv, vy * vv, vz * vv]]
    ppermute x6, waiting for transfers between devices: 6.32 us -> 0.02 us  [per_device(): lax.ppermute(sent[part][s - 1], 'gx', [(i, i ^ s) for i in range(count)])]
    ppermute x6, waiting for transfers between devices: 8.49 us -> 3.54 us  [the longest x2 2.39 us: per_device(): lax.ppermute(total if i else other, 'vert', [(v, v ^ step) for v in range...]
    concatenate x4 -> x0, local copies, waits for them, and re-layouts: 4.26 us -> none  [the longest x2 3.31 us: stacked_left(): return jnp.concatenate([a, a, b, a, b, c], axis=-1)]
  transfers between devices with their start and end apart: 12 -> 12, of which waited for: 2 -> 3; matrix products, arithmetic and copies ran while one was open for 13% -> 0% of each run, Pallas kernels for 14% -> 41%
where the time goes in v2:
time: 75.5 us; the launch traced here: 75.3 us
  Pallas kernels  53.5 us (71%)
  starting transfers between devices  16.5 us (22%)
  waiting for transfers between devices  3.55 us (5%)
  local copies, waits for them, and re-layouts  0.95 us (1%)
  between operations  0.84 us (1%)
    pallas_call x4, Pallas kernels, join(): pl.pallas_call(lambda *refs: join_kernel(plane, d, part * vel_part, *refs...  15.8 us
    pallas_call x2, Pallas kernels, per_device(): pl.pallas_call(lambda *refs, part=part: sweep_kernel(part, min(BLOCK, vel...  11.4 us
    pallas_call x1, Pallas kernels, per_device(): pl.pallas_call(lambda *refs: finish_kernel(plane, PARTS, *refs), out_shap...  10.7 us
    pallas_call x1, Pallas kernels, per_device(): pl.pallas_call(lambda *refs: moment_kernel(plane, PARTS, *refs), out_shap...  8.2 us
    ppermute x6, starting transfers between devices, per_device(): lax.ppermute(sent[part][s - 1], 'gx', [(i, i ^ s) for i in range(count)])  8.12 us
    pallas_call x2, Pallas kernels, per_device(): pl.pallas_call(lambda *refs, part=part, last=last: correct_kernel(plane,...  3.25 us
    pallas_call x1, Pallas kernels, per_device(): pl.pallas_call(lambda *refs: fit_kernel(plane, *refs), out_shape=[jax.Sha...  3.02 us
    ppermute x1, starting transfers between devices, per_device(): got = lax.ppermute(total, 'vert', [(v, v ^ step) for v in range(size)])  2.81 us
  transfers between devices with their start and end apart: 12, of which 3 were waited for; matrix products, arithmetic and copies ran while one was open for 0% of the time, Pallas kernels for 41%

profile of v2, /device:TPU:0, one launch (start us, length us, event | category | flops | bytes accessed | tf_op | source)
XLA Modules:
  0.0 75.3 jit_solution(12996691528113050231)
XLA Ops:
  0.6 0.0 copy-start
  0.6 0.9 %copy-done = f32[2,512,32]{1,2,0:T(8,128)S(1)} copy-done((f32[2,512,32]{1,2,0:T(8,128)S(1)}, f32[2,512,32]{1,2,0:T(8,128)}, u32[]{:S(2)}) %copy-start) | copy-done | bytes 131096
  1.5 0.7 prepare.1
  2.3 5.7 %sweep.2 = (f32[2,256,6144]{2,1,0:T(8,128)S(1)}, f32[392,128]{1,0:T(8,128)S(1)}, f32[392,128]{1,0:T(8,128)S(1)}, f32[392,128]{1,0:T(8,128)S(1)}) custom-call(f32[2,512,6144]{2,1,0:T(8,128)} %refs_0_.3, bf16[2,512,128]{2,1,0:T(8,128)(2,1)S(1)} %get-tuple-element.30.refs_1_, f32[4,8,128]{2,1,0:T(8,128)S(1)} %get-tuple-element.31.refs_2_, ...), custom_call_target="tpu_custom_call" | custom-call | tf_op jit(solution)/shard_map/sweep/pallas_call | solution.py:549
  8.0 3.0 %collective-permute-start = (f32[392,128]{1,0:T(8,128)S(1)}, f32[392,128]{1,0:T(8,128)S(1)}, u32[]{:S(2)}, u32[]{:S(2)}) collective-permute-start(f32[392,128]{1,0:T(8,128)S(1)} %get-tuple-element.39), channel_id=1, source_target_pairs={{0,8},{8,0},{16,24},{24,16},{1,9},{9,1},{17,25},{25,17},{2,10},{10... | collective-permute-start | bytes 602120 | tf_op jit(solution)/shard_map/ppermute | solution.py:586
  11.0 1.5 %collective-permute-start.1 = (f32[392,128]{1,0:T(8,128)S(1)}, f32[392,128]{1,0:T(8,128)S(1)}, u32[]{:S(2)}, u32[]{:S(2)}) collective-permute-start(f32[392,128]{1,0:T(8,128)S(1)} %get-tuple-element.40), channel_id=1, source_target_pairs={{0,16},{8,24},{16,0},{24,8},{1,17},{9,25},{17,1},{25,9},{2,18},{10... | collective-permute-start | bytes 602120 | tf_op jit(solution)/shard_map/ppermute | solution.py:586
  12.5 0.0 copy-start.1
  12.5 0.0 collective-permute-start.2
  12.5 5.7 %sweep.3 = (f32[2,256,6144]{2,1,0:T(8,128)S(1)}, f32[392,128]{1,0:T(8,128)S(1)}, f32[392,128]{1,0:T(8,128)S(1)}, f32[392,128]{1,0:T(8,128)S(1)}) custom-call(f32[2,512,6144]{2,1,0:T(8,128)} %refs_0_.3, bf16[2,512,128]{2,1,0:T(8,128)(2,1)S(1)} %get-tuple-element.30.refs_1_, f32[4,8,128]{2,1,0:T(8,128)S(1)} %get-tuple-element.31.refs_2_, ...), custom_call_target="tpu_custom_call" | custom-call | tf_op jit(solution)/shard_map/sweep/pallas_call | solution.py:549
  18.2 2.0 %collective-permute-start.3 = (f32[392,128]{1,0:T(8,128)S(1)}, f32[392,128]{1,0:T(8,128)S(1)}, u32[]{:S(2)}, u32[]{:S(2)}) collective-permute-start(f32[392,128]{1,0:T(8,128)S(1)} %get-tuple-element.45), channel_id=1, source_target_pairs={{0,8},{8,0},{16,24},{24,16},{1,9},{9,1},{17,25},{25,17},{2,10},{10... | collective-permute-start | bytes 602120 | tf_op jit(solution)/shard_map/ppermute | solution.py:586
  20.2 1.5 %collective-permute-start.4 = (f32[392,128]{1,0:T(8,128)S(1)}, f32[392,128]{1,0:T(8,128)S(1)}, u32[]{:S(2)}, u32[]{:S(2)}) collective-permute-start(f32[392,128]{1,0:T(8,128)S(1)} %get-tuple-element.46), channel_id=1, source_target_pairs={{0,16},{8,24},{16,0},{24,8},{1,17},{9,25},{17,1},{25,9},{2,18},{10... | collective-permute-start | bytes 602120 | tf_op jit(solution)/shard_map/ppermute | solution.py:586
  21.7 0.0 collective-permute-done.refs_3_
  21.7 0.0 collective-permute-start.5
  21.8 0.0 copy-done.1
  21.8 0.0 copy-start.3
  21.8 0.0 copy-start.2
  21.8 8.2 %moments.1 = (f32[16,6144]{1,0:T(8,128)S(1)}, bf16[2,512,512]{2,1,0:T(8,128)(2,1)S(1)}, bf16[2,512,512]{2,1,0:T(8,128)(2,1)S(1)}) custom-call(f32[2,32,512]{2,1,0:T(8,128)S(1)} %get-tuple-element.34.refs_0_.reach, f32[2,16,512]{2,1,0:T(8,128)S(1)} %pad.4.refs_1_, f32[2,256,6144]{2,1,0:T(8,128)S(1)} %get-tuple-element.33.refs_2_.refs_0_, ...), custom_call_target="tpu_custom_call" | custom-call | tf_op jit(solution)/shard_map/moments/pallas_call | solution.py:562
  30.0 0.0 collective-permute-done.1.refs_4_
  30.0 0.0 collective-permute-done.2.refs_5_
  30.0 1.1 %correct.2 = (f32[2,256,384]{2,1,0:T(8,128)S(1)}, f32[16,6144]{1,0:T(8,128)S(1)}) custom-call(f32[16,6144]{1,0:T(8,128)S(1)} %get-tuple-element.36.refs_0_._, bf16[2,512,512]{2,1,0:T(8,128)(2,1)S(1)} %get-tuple-element.37.refs_1_, bf16[2,512,512]{2,1,0:T(8,128)(2,1)S(1)} %get-tuple-element.38.refs_2_, f32[392,128]{1,0:T(8,128)S(1)} %collective-permute-done.refs_3_, ...), custom_call_target="tpu_custom_call" | custom-call | tf_op jit(solution)/shard_map/correct/pallas_call | solution.py:589
  31.2 0.0 collective-permute-done.3.refs_3_
  31.2 0.0 collective-permute-done.4.refs_4_
  31.2 0.0 collective-permute-done.5.refs_5_
  31.2 2.1 %correct.3 = (f32[2,256,384]{2,1,0:T(8,128)S(1)}, f32[16,3072]{1,0:T(8,128)S(1)}, f32[16,3072]{1,0:T(8,128)S(1)}) custom-call(f32[16,6144]{1,0:T(8,128)S(1)} %get-tuple-element.44.refs_0_, bf16[2,512,512]{2,1,0:T(8,128)(2,1)S(1)} %get-tuple-element.37.refs_1_, bf16[2,512,512]{2,1,0:T(8,128)(2,1)S(1)} %get-tuple-element.38.refs_2_, ...), custom_call_target="tpu_custom_call" | custom-call | tf_op jit(solution)/shard_map/correct/pallas_call | solution.py:589
  33.3 0.0 collective-permute-start.6
  33.4 1.4 %collective-permute-done.6.b = f32[16,3072]{1,0:T(8,128)S(1)} collective-permute-done((f32[16,3072]{1,0:T(8,128)S(1)}, f32[16,3072]{1,0:T(8,128)S(1)}, u32[]{:S(2)}, u32[]{:S(2)}) %collective-permute-start.6) | collective-permute-done | bytes 196640 | tf_op jit(solution)/shard_map/ppermute | solution.py:641
  34.8 2.1 %collective-permute-start.7 = (f32[16,3072]{1,0:T(8,128)S(1)}, f32[16,3072]{1,0:T(8,128)S(1)}, u32[]{:S(2)}, u32[]{:S(2)}) collective-permute-start(f32[16,3072]{1,0:T(8,128)S(1)} %add_kernel.1.refs_4_.a), channel_id=1, source_target_pairs={{0,2},{1,3},{2,0},{3,1},{4,6},{5,7},{6,4},{7,5},{8,10},{9,11},{10,... | collective-permute-start | bytes 589832 | tf_op jit(solution)/shard_map/ppermute | solution.py:641
  36.9 0.0 copy-done.3
  36.9 0.0 copy-done.2
  36.9 0.3 tables.1
  37.2 3.9 %join.4.refs_0_ = f32[2,256,6144]{2,1,0:T(8,128)S(1)} custom-call(f32[2,256,6144]{2,1,0:T(8,128)S(1)} %get-tuple-element.33.refs_2_.refs_0_, f32[2,256,384]{2,1,0:T(8,128)S(1)} %get-tuple-element.42.refs_1_, bf16[2,512,128]{2,1,0:T(8,128)(2,1)S(1)} %get-tuple-element.43.refs_2_, ...), custom_call_target="tpu_custom_call", output_to_operand_aliasing={{}: (0, {})} | custom-call | flops 805306368 | bytes 12582912 | tf_op jit(solution)/shard_map/join/pallas_call | solution.py:610
  41.1 1.0 %collective-permute-done.7.b = f32[16,3072]{1,0:T(8,128)S(1)} collective-permute-done((f32[16,3072]{1,0:T(8,128)S(1)}, f32[16,3072]{1,0:T(8,128)S(1)}, u32[]{:S(2)}, u32[]{:S(2)}) %collective-permute-start.7) | collective-permute-done | bytes 196640 | tf_op jit(solution)/shard_map/ppermute | solution.py:641
  42.1 0.7 collective-permute-start.8
  42.8 2.8 %collective-permute-start.9 = (f32[16,3072]{1,0:T(8,128)S(1)}, f32[16,3072]{1,0:T(8,128)S(1)}, u32[]{:S(2)}, u32[]{:S(2)}) collective-permute-start(f32[16,3072]{1,0:T(8,128)S(1)} %get-tuple-element.50.refs_4_.a), channel_id=1, source_target_pairs={{0,4},{1,5},{2,6},{3,7},{4,0},{5,1},{6,2},{7,3},{8,12},{9,13},{10,... | collective-permute-start | bytes 589832 | tf_op jit(solution)/shard_map/ppermute | solution.py:649
  45.6 4.0 %join.5.refs_0_ = f32[2,256,6144]{2,1,0:T(8,128)S(1)} custom-call(f32[2,256,6144]{2,1,0:T(8,128)S(1)} %join.4.refs_0_, f32[2,256,384]{2,1,0:T(8,128)S(1)} %get-tuple-element.42.refs_1_, bf16[2,512,128]{2,1,0:T(8,128)(2,1)S(1)} %get-tuple-element.43.refs_2_, bf16[128,6144]{1,0:T(8,128)(2,1)S(1)} %get-tuple-element.32.refs_3_, ...), custom_call_target="tpu_custom_call", output_to_operand_aliasing={{}: (0, {})} | custom-call | flops 805306368 | bytes 12582912 | tf_op jit(solution)/shard_map/join/pallas_call | solution.py:610
  49.6 0.0 collective-permute-done.8.refs_4_.halo
  49.6 0.2 collective-permute-start.10
  49.8 4.0 %join.6.refs_0_ = f32[2,256,6144]{2,1,0:T(8,128)S(1)} custom-call(f32[2,256,6144]{2,1,0:T(8,128)S(1)} %get-tuple-element.35.refs_3_.refs_0_, f32[2,256,384]{2,1,0:T(8,128)S(1)} %get-tuple-element.51.refs_1_, bf16[2,512,128]{2,1,0:T(8,128)(2,1)S(1)} %get-tuple-element.43.refs_2_, ...), custom_call_target="tpu_custom_call", output_to_operand_aliasing={{}: (0, {})} | custom-call | flops 805306368 | bytes 12582912 | tf_op jit(solution)/shard_map/join/pallas_call | solution.py:610
  53.8 4.0 %join.7.refs_1_ = f32[2,256,6144]{2,1,0:T(8,128)S(1)} custom-call(f32[2,256,6144]{2,1,0:T(8,128)S(1)} %join.6.refs_0_, f32[2,256,384]{2,1,0:T(8,128)S(1)} %get-tuple-element.51.refs_1_, bf16[2,512,128]{2,1,0:T(8,128)(2,1)S(1)} %get-tuple-element.43.refs_2_, bf16[128,6144]{1,0:T(8,128)(2,1)S(1)} %get-tuple-element.32.refs_3_, ...), custom_call_target="tpu_custom_call", output_to_operand_aliasing={{}: (0, {})} | custom-call | flops 805306368 | bytes 12582912 | tf_op jit(solution)/shard_map/join/pallas_call | solution.py:610
  57.8 0.0 collective-permute-done.10.more
  57.8 0.0 collective-permute-done.9.b
  57.9 2.5 %collective-permute-start.11 = (f32[16,3840]{1,0:T(8,128)S(1)}, f32[16,3840]{1,0:T(8,128)S(1)}, u32[]{:S(2)}, u32[]{:S(2)}) collective-permute-start(f32[16,3840]{1,0:T(8,128)S(1)} %close_kernel.1.refs_0_), channel_id=1, source_target_pairs={{0,1},{1,0},{2,3},{3,2},{4,5},{5,4},{6,7},{7,6},{8,9},{9,8},{10,11... | collective-permute-start | bytes 737288 | tf_op jit(solution)/shard_map/ppermute | solution.py:661
  60.4 1.1 %collective-permute-done.11.refs_1_ = f32[16,3840]{1,0:T(8,128)S(1)} collective-permute-done((f32[16,3840]{1,0:T(8,128)S(1)}, f32[16,3840]{1,0:T(8,128)S(1)}, u32[]{:S(2)}, u32[]{:S(2)}) %collective-permute-start.11) | collective-permute-done | bytes 245792 | tf_op jit(solution)/shard_map/ppermute | solution.py:661
  61.6 3.0 %fit.1 = (f32[13,6144]{1,0:T(8,128)}, bf16[128,6144]{1,0:T(8,128)(2,1)S(1)}, bf16[128,6144]{1,0:T(8,128)(2,1)S(1)}) custom-call(f32[16,3840]{1,0:T(8,128)S(1)} %close_kernel.1.refs_0_, f32[16,3840]{1,0:T(8,128)S(1)} %collective-permute-done.11.refs_1_), custom_call_target="tpu_custom_call" | custom-call | tf_op jit(solution)/shard_map/fit/pallas_call | solution.py:663
  64.6 10.7 %finish.1 = f32[2,512,6144]{2,1,0:T(8,128)} custom-call(f32[2,256,6144]{2,1,0:T(8,128)S(1)} %join.5.refs_0_, f32[2,256,6144]{2,1,0:T(8,128)S(1)} %join.7.refs_1_, bf16[2,512,128]{2,1,0:T(8,128)(2,1)S(1)} %get-tuple-element.53.refs_2_, bf16[2,512,128]{2,1,0:T(8,128)(2,1)S(1)} %get-tuple-element.54.refs_3_, bf16[128,6144]{1,0:T(8,128)(2,1)S(1)} %get-tuple-element.55.refs_4_, ...), custom_call_target="tpu_custom_call" | custom-call | tf_op jit(solution)/shard_map/finish/pallas_call | solution.py:674
  (7 shorter events, 0.1 us)
Async XLA Ops:
  0.6 0.9 %copy-start = (f32[2,512,32]{1,2,0:T(8,128)S(1)}, f32[2,512,32]{1,2,0:T(8,128)}, u32[]{:S(2)}) copy-start(f32[2,512,32]{1,2,0:T(8,128)} %param.6) | copy-start | bytes 393220
  8.0 13.8 %collective-permute-start = (f32[392,128]{1,0:T(8,128)S(1)}, f32[392,128]{1,0:T(8,128)S(1)}, u32[]{:S(2)}, u32[]{:S(2)}) collective-permute-start(f32[392,128]{1,0:T(8,128)S(1)} %get-tuple-element.39), channel_id=1, source_target_pairs={{0,8},{8,0},{16,24},{24,16},{1,9},{9,1},{17,25},{25,17},{2,10},{10... | collective-permute-start | bytes 602120 | tf_op jit(solution)/shard_map/ppermute | solution.py:586
  11.0 19.0 %collective-permute-start.1 = (f32[392,128]{1,0:T(8,128)S(1)}, f32[392,128]{1,0:T(8,128)S(1)}, u32[]{:S(2)}, u32[]{:S(2)}) collective-permute-start(f32[392,128]{1,0:T(8,128)S(1)} %get-tuple-element.40), channel_id=1, source_target_pairs={{0,16},{8,24},{16,0},{24,8},{1,17},{9,25},{17,1},{25,9},{2,18},{10... | collective-permute-start | bytes 602120 | tf_op jit(solution)/shard_map/ppermute | solution.py:586
  12.5 9.3 %copy-start.1 = (f32[13,2,512]{2,1,0:T(2,128)S(1)}, f32[13,2,512]{2,1,0:T(2,128)}, u32[]{:S(2)}) copy-start(f32[13,2,512]{2,1,0:T(2,128)} %param.8) | copy-start | bytes 159748
  12.5 17.5 %collective-permute-start.2 = (f32[392,128]{1,0:T(8,128)S(1)}, f32[392,128]{1,0:T(8,128)S(1)}, u32[]{:S(2)}, u32[]{:S(2)}) collective-permute-start(f32[392,128]{1,0:T(8,128)S(1)} %get-tuple-element.41), channel_id=1, source_target_pairs={{0,24},{8,16},{16,8},{24,0},{1,25},{9,17},{17,9},{25,1},{2,26},{10... | collective-permute-start | bytes 602120 | tf_op jit(solution)/shard_map/ppermute | solution.py:586
  18.2 13.0 %collective-permute-start.3 = (f32[392,128]{1,0:T(8,128)S(1)}, f32[392,128]{1,0:T(8,128)S(1)}, u32[]{:S(2)}, u32[]{:S(2)}) collective-permute-start(f32[392,128]{1,0:T(8,128)S(1)} %get-tuple-element.45), channel_id=1, source_target_pairs={{0,8},{8,0},{16,24},{24,16},{1,9},{9,1},{17,25},{25,17},{2,10},{10... | collective-permute-start | bytes 602120 | tf_op jit(solution)/shard_map/ppermute | solution.py:586
  20.2 11.0 %collective-permute-start.4 = (f32[392,128]{1,0:T(8,128)S(1)}, f32[392,128]{1,0:T(8,128)S(1)}, u32[]{:S(2)}, u32[]{:S(2)}) collective-permute-start(f32[392,128]{1,0:T(8,128)S(1)} %get-tuple-element.46), channel_id=1, source_target_pairs={{0,16},{8,24},{16,0},{24,8},{1,17},{9,25},{17,1},{25,9},{2,18},{10... | collective-permute-start | bytes 602120 | tf_op jit(solution)/shard_map/ppermute | solution.py:586
  21.7 9.4 %collective-permute-start.5 = (f32[392,128]{1,0:T(8,128)S(1)}, f32[392,128]{1,0:T(8,128)S(1)}, u32[]{:S(2)}, u32[]{:S(2)}) collective-permute-start(f32[392,128]{1,0:T(8,128)S(1)} %get-tuple-element.47), channel_id=1, source_target_pairs={{0,24},{8,16},{16,8},{24,0},{1,25},{9,17},{17,9},{25,1},{2,26},{10... | collective-permute-start | bytes 602120 | tf_op jit(solution)/shard_map/ppermute | solution.py:586
  21.8 15.1 %copy-start.3 = (f32[2,512]{1,0:T(2,128)S(1)}, f32[2,512]{1,0:T(2,128)}, u32[]{:S(2)}) copy-start(f32[2,512]{1,0:T(2,128)} %param.9) | copy-start | bytes 12292
  21.8 15.1 %copy-start.2 = (f32[3,2,512]{2,1,0:T(2,128)S(1)}, f32[3,2,512]{2,1,0:T(2,128)}, u32[]{:S(2)}) copy-start(f32[3,2,512]{2,1,0:T(2,128)} %param.7) | copy-start | bytes 36868
  33.3 1.4 %collective-permute-start.6 = (f32[16,3072]{1,0:T(8,128)S(1)}, f32[16,3072]{1,0:T(8,128)S(1)}, u32[]{:S(2)}, u32[]{:S(2)}) collective-permute-start(f32[16,3072]{1,0:T(8,128)S(1)} %get-tuple-element.49), channel_id=1, source_target_pairs={{0,1},{1,0},{2,3},{3,2},{4,5},{5,4},{6,7},{7,6},{8,9},{9,8},{10,11... | collective-permute-start | bytes 589832 | tf_op jit(solution)/shard_map/ppermute | solution.py:641
  34.8 7.3 %collective-permute-start.7 = (f32[16,3072]{1,0:T(8,128)S(1)}, f32[16,3072]{1,0:T(8,128)S(1)}, u32[]{:S(2)}, u32[]{:S(2)}) collective-permute-start(f32[16,3072]{1,0:T(8,128)S(1)} %add_kernel.1.refs_4_.a), channel_id=1, source_target_pairs={{0,2},{1,3},{2,0},{3,1},{4,6},{5,7},{6,4},{7,5},{8,10},{9,11},{10,... | collective-permute-start | bytes 589832 | tf_op jit(solution)/shard_map/ppermute | solution.py:641
  42.1 7.4 %collective-permute-start.8 = (f32[16,768]{1,0:T(8,128)S(1)}, f32[16,768]{1,0:T(8,128)S(1)}, u32[]{:S(2)}, u32[]{:S(2)}) collective-permute-start(f32[16,768]{1,0:T(8,128)S(1)} %get-tuple-element.52), channel_id=1, source_target_pairs={{1,8},{8,1},{3,10},{10,3},{5,12},{12,5},{7,14},{14,7},{9,16},{16,9... | collective-permute-start | bytes 147464 | tf_op jit(solution)/shard_map/ppermute | solution.py:655
  42.8 15.0 %collective-permute-start.9 = (f32[16,3072]{1,0:T(8,128)S(1)}, f32[16,3072]{1,0:T(8,128)S(1)}, u32[]{:S(2)}, u32[]{:S(2)}) collective-permute-start(f32[16,3072]{1,0:T(8,128)S(1)} %get-tuple-element.50.refs_4_.a), channel_id=1, source_target_pairs={{0,4},{1,5},{2,6},{3,7},{4,0},{5,1},{6,2},{7,3},{8,12},{9,13},{10,... | collective-permute-start | bytes 589832 | tf_op jit(solution)/shard_map/ppermute | solution.py:649
  49.6 8.2 %collective-permute-start.10 = (f32[16,768]{1,0:T(8,128)S(1)}, f32[16,768]{1,0:T(8,128)S(1)}, u32[]{:S(2)}, u32[]{:S(2)}) collective-permute-start(f32[16,768]{1,0:T(8,128)S(1)} %collective-permute-done.8.refs_4_.halo), channel_id=1, source_target_pairs={{0,4},{1,5},{2,6},{3,7},{4,0},{5,1},{6,2},{7,3},{8,12},{9,13},{10,... | collective-permute-start | bytes 147464 | tf_op jit(solution)/shard_map/ppermute | solution.py:657
  57.9 3.7 %collective-permute-start.11 = (f32[16,3840]{1,0:T(8,128)S(1)}, f32[16,3840]{1,0:T(8,128)S(1)}, u32[]{:S(2)}, u32[]{:S(2)}) collective-permute-start(f32[16,3840]{1,0:T(8,128)S(1)} %close_kernel.1.refs_0_), channel_id=1, source_target_pairs={{0,1},{1,0},{2,3},{3,2},{4,5},{5,4},{6,7},{7,6},{8,9},{9,8},{10,11... | collective-permute-start | bytes 737288 | tf_op jit(solution)/shard_map/ppermute | solution.py:661

commit v3 on v2

--- a/solution.py
+++ b/solution.py
@@ -81,7 +81,7 @@
     return full, turned[whole]
 
 
-def prepare_kernel(plane, parts, factors, reach, gain, ends, spread):
+def prepare(plane, parts, factors, reach, gain, ends, spread):
     cells, vel = factors.shape[1], factors.shape[2]
     depth = spread.shape[0]
     lane = lax.broadcasted_iota(jnp.int32, (8, LANES), 1)
@@ -121,62 +121,70 @@
     return jnp.concatenate(terms, axis=0).T.astype(bf16)
 
 
-def sweep_kernel(part, rows, plane, dist, gain, ends, spread, *rest):
-    swept, sent = rest[0], rest[1:]
-    count = len(sent) + 1
+def sweep_kernel(part, rows, plane, parts, count, *refs):
+    if part == 0:
+        dist, factors, swept, *sent = refs[: 2 + count]
+        reach, gain, ends, spread, blocks, arrived, table, read = refs[2 + count :]
+    else:
+        dist, gain, ends, spread, swept, *sent = refs[: 4 + count]
+        blocks, arrived = refs[4 + count :]
     me = lax.axis_index("gx")
     vel = swept.shape[1]
     pairs = swept.shape[2] // plane // 2
     whole = plane // LANES
     width = 2 * plane
-    offset = part * (vel // rows)
     low = low_half(rows)
     some = min(ROWS, rows)
-
-    def body(ref):
-        step = pl.program_id(0)
-        row = pl.multiple_of(step // 2 * rows, rows)
-
-        def one(d):
-            table = gain[d, pl.ds(pl.multiple_of(part * vel + row, rows), rows), :]
-
-            def gains(p):
-                return dot(table, spread[:, p * width : (p + 1) * width])
-
-            def load(p, t):
-                return ref[:, p * width + t * LANES : p * width + (t + 1) * LANES]
-
-            def store(p, t, value):
-                swept[d, pl.ds(row, rows), p * width + t * LANES : p * width + (t + 1) * LANES] = value
-
-            values = sweep_rows(rows, load, store, gains, d == 1, pairs, plane)
-            full, half = packed_last(values, d == 1, whole, low)
-            both = [
-                jnp.where(low[: some // 2], half[n : n + some // 2], turn(half[n + some // 2 : n + some]))
-                for n in range(0, rows, some)
-            ]
-            for s in range(1, count):
-                out = sent[s - 1]
-
-                @pl.when(((me ^ s) > me) == (d == 0))
-                def _():
-                    for w in range(whole):
-                        out[pl.ds(pl.multiple_of(w * vel + row, rows), rows), :] = full[w]
-                    for n, packed in enumerate(both):
-                        out[pl.ds(pl.multiple_of(whole * vel + (row + n * some) // 2, some // 2), some // 2), :] = packed
-
-        for d in range(2):
-            pl.when(step % 2 == d)(lambda d=d: one(d))
-
-    pltpu.emit_pipeline(
-        body,
-        grid=(2 * vel // rows,),
-        in_specs=[
-            pl.BlockSpec(
-                (None, rows, dist.shape[2]), lambda i: (i % 2, i // 2 + offset, 0), pipeline_mode=pl.Buffered(3)
-            )
-        ],
-    )(dist)
+    steps = [(d, row) for row in range(0, vel, rows) for d in range(2)]
+    slots = blocks.shape[0]
+
+    def fetch(i):
+        d, row = steps[i]
+        at = part * vel + row
+        return pltpu.make_async_copy(dist.at[d, at : at + rows, :], blocks.at[i % slots], arrived.at[i % slots])
+
+    if part == 0:
+        first = pltpu.make_async_copy(factors, table, read)
+        first.start()
+    for i in range(min(slots, len(steps))):
+        fetch(i).start()
+    if part == 0:
+        first.wait()
+        prepare(plane, parts, table, reach, gain, ends, spread)
+
+    for i, (d, row) in enumerate(steps):
+        fetch(i).wait()
+        ref = blocks.at[i % slots]
+        left = gain[d, part * vel + row : part * vel + row + rows, :]
+
+        def gains(p):
+            return dot(left, spread[:, p * width : (p + 1) * width])
+
+        def load(p, t):
+            return ref[:, p * width + t * LANES : p * width + (t + 1) * LANES]
+
+        def store(p, t, value):
+            swept[d, row : row + rows, p * width + t * LANES : p * width + (t + 1) * LANES] = value
+
+        values = sweep_rows(rows, load, store, gains, d == 1, pairs, plane)
+        if i + slots < len(steps):
+            fetch(i + slots).start()
+        full, half = packed_last(values, d == 1, whole, low)
+        both = [
+            jnp.where(low[: some // 2], half[n : n + some // 2], turn(half[n + some // 2 : n + some]))
+            for n in range(0, rows, some)
+        ]
+        for s in range(1, count):
+            out = sent[s - 1]
+
+            @pl.when(((me ^ s) > me) == (d == 0))
+            def _():
+                for w in range(whole):
+                    out[w * vel + row : w * vel + row + rows, :] = full[w]
+                for n, packed in enumerate(both):
+                    at = whole * vel + (row + n * some) // 2
+                    out[at : at + some // 2, :] = packed
+
     tail = whole * vel + vel // 2
     for s in range(1, count):
         sent[s - 1][tail : tail + 8, :] = jnp.where((me ^ s) > me, ends[2 * part], ends[2 * part + 1])
@@ -211,8 +219,7 @@
         tiles = [x[:, t : t + LANES] for t in range(0, width, LANES)]
         return jnp.concatenate(swap_cells(tiles, whole, low), axis=1)
 
-    @pl.loop(0, pairs)
-    def _(p):
+    def pair(p):
         at = pl.ds(pl.multiple_of(p * width, width), width)
         ahead = jnp.minimum(p + 1, pairs - 1)
         behind = jnp.maximum(p - 1, 0)
@@ -238,10 +245,15 @@
                 out[:, pl.ds(pl.multiple_of(behind * width, width), width)] += moved
         out[:, at] += here
 
+    @pl.loop(0, pairs // 2)
+    def _(i):
+        for u in range(2):
+            pair(2 * i + u)
+
 
 def correct_kernel(plane, part, last, moments, high_lhs, rest_lhs, *refs):
     count = lax.axis_size("gx")
-    refs_c, refs = refs[: count - 1], refs[count - 1 :]
+    refs_c, refs = refs[: count - 1], refs[count:]
     entering, outs, (natural, work) = refs[0], refs[1:-2], refs[-2:]
     me = lax.axis_index("gx")
     core = lax.axis_index("vert") % 2
@@ -303,40 +315,41 @@
             work[...] += total
     half_pairs = pairs // 2
     width = 2 * plane
-    for p in range(pairs):
-        first, second = ([work[(2 * p + i) * k : (2 * p + i + 1) * k, t : t + LANES] for t in range(0, (whole + 1) * LANES, LANES)] for i in range(2))
+
+    def corrected(p):
+        first, second = (
+            [work[(2 * p + i) * k : (2 * p + i + 1) * k, t : t + LANES] for t in range(0, (whole + 1) * LANES, LANES)]
+            for i in range(2)
+        )
         turned = [turn(x) for x in second]
         term = first[:whole] + [jnp.where(low, first[whole], turned[0])]
         term += [jnp.where(low, turned[w], turned[w + 1]) for w in range(whole)]
-        value = moments[:, p * width : (p + 1) * width] + jnp.concatenate(term, axis=1)
-        if not last:
-            outs[0][:, p * width : (p + 1) * width] = value
-            continue
-        mine, other = outs
-        inner = slice((p % half_pairs) * width, (p % half_pairs + 1) * width)
-
-        @pl.when(core == p // half_pairs)
+        return moments[:, p * width : (p + 1) * width] + jnp.concatenate(term, axis=1)
+
+    if not last:
+        for p in range(pairs):
+            outs[0][:, p * width : (p + 1) * width] = corrected(p)
+        return
+    for n in range(2):
+
+        @pl.when(core == n)
         def _():
-            mine[:, inner] = value
-
-        @pl.when(core != p // half_pairs)
-        def _():
-            other[:, inner] = value
+            for p in range(pairs):
+                out = outs[(p // half_pairs) ^ n]
+                out[:, p % half_pairs * width : (p % half_pairs + 1) * width] = corrected(p)
 
 
 def fit_rows(m):
-    density = 1.0 + 0.5 * jnp.tanh(m[0:1])
-    u = [0.5 * jnp.tanh(m[j : j + 1]) for j in (1, 2, 3)]
-    inverse = 1.0 / (1.0 + 0.5 * jnp.tanh(m[4:5]))
-    s = [0.2 * jnp.tanh(m[j : j + 1]) for j in range(5, 10)]
-    q = [0.2 * jnp.tanh(m[j : j + 1]) for j in range(10, 13)]
+    density = 1.0 + 0.5 * jnp.tanh(m[0])
+    u = [0.5 * jnp.tanh(m[j]) for j in (1, 2, 3)]
+    inverse = 1.0 / (1.0 + 0.5 * jnp.tanh(m[4]))
+    s = [0.2 * jnp.tanh(m[j]) for j in range(5, 10)]
+    q = [0.2 * jnp.tanh(m[j]) for j in range(10, 13)]
     h = 0.5 * inverse
     uu = u[0] * u[0] + u[1] * u[1] + u[2] * u[2]
     qu = q[0] * u[0] + q[1] * u[1] + q[2] * u[2]
     e = h * 1.4426950408889634
-    zero = jnp.zeros_like(e)
     exponent = [-e * uu, 2.0 * e * u[0], 2.0 * e * u[1], 2.0 * e * u[2], -e, -e, -e]
-    exponent = exponent + [zero] * (16 - len(exponent))
     a = h * uu - 2.5
     xx, yy, zz = 0.5 * s[3], 0.5 * s[4], -0.5 * (s[3] + s[4])
     xy, xz, yz = s[0], s[1], s[2]
@@ -363,8 +376,7 @@
         by * (h * q[1]),
         by * (h * q[2]),
     ]
-    terms = terms + [zero] * (16 - len(terms))
-    return jnp.concatenate(exponent, axis=0), jnp.concatenate(terms, axis=0)
+    return exponent, terms
 
 
 def stacked_right(x):
@@ -390,42 +402,54 @@
         left_r[d, :, :] = turned_thirds(reach[d] * (1.0 - fraction), left_r.shape[2])
 
 
-def fit_kernel(plane, own, rest, macro, right_e, right_p, wide):
+def fit_kernel(plane, own, rest, macro, right_e, right_p, tiles, turned, fitted):
     me, count = lax.axis_index("gx"), lax.axis_size("gx")
     core = lax.axis_index("vert") % 2
     lanes = macro.shape[1]
-    cells = lanes // plane
-    margin = SMOOTH * plane
-    half = lanes // 2
-    width = 2 * plane
+    margin = SMOOTH * plane // LANES
+    inner = lanes // LANES
+    half = inner // 2
+    k = own.shape[0]
+    number = inner + 2 * margin
+    whole = plane // LANES
+    low = low_half(k)
+    tile = lambda t: slice(t % number * k, t % number * k + k)
+    column = lambda t: slice(t * LANES, (t + 1) * LANES)
 
     for first, left, right in ((0, own, rest), (1, rest, own)):
 
         @pl.when(core == first)
         def _():
-            wide[:, :margin] = left[:, half:]
-            wide[:, margin : margin + half] = left[:, :half]
-            wide[:, margin + half : margin + lanes] = right[:, :half]
-            wide[:, margin + lanes :] = right[:, half:]
-
-    value = wide[...]
-    total = value.shape[1]
-    place = lax.broadcasted_iota(jnp.int32, (1, total), 1) + (me * lanes - margin)
-    inside = (place >= 0) & (place < count * lanes)
+            for t in range(margin):
+                tiles[tile(t), :] = left[:, column(half + t)]
+                tiles[tile(margin + inner + t), :] = right[:, column(half + t)]
+            for t in range(half):
+                tiles[tile(margin + t), :] = left[:, column(t)]
+                tiles[tile(margin + half + t), :] = right[:, column(t)]
+
+    before = jnp.where(me > 0, RATE, 0.0)
+    after = jnp.where(me < count - 1, RATE, 0.0)
     for _ in range(SMOOTH):
-        rate = RATE / (1.0 + value[0:1] * value[0:1])
-        rate = jnp.where(inside, rate, 0.0)
-        value = value + rate * (pltpu.roll(value, plane, 1) + pltpu.roll(value, total - plane, 1) - 2.0 * value)
-    value = value[:, margin : margin + lanes]
-    wide[:, :lanes] = value
-    macro[...] = value[: macro.shape[0]]
-
-    @pl.loop(0, lanes // (2 * width))
-    def _(i):
-        at = pl.ds(pl.multiple_of(i * 2 * width, 2 * width), 2 * width)
-        exponent, terms = fit_rows(wide[:, at])
-        right_e[:, at] = stacked_right(exponent)
-        right_p[:, at] = stacked_right(terms)
+        for t in range(number):
+            turned[tile(t), :] = turn(tiles[tile(t), :])
+        for t in range(number):
+            value = tiles[tile(t), :]
+            behind = jnp.where(low, turned[tile(t - whole - 1), :], turned[tile(t - whole), :])
+            ahead = jnp.where(low, turned[tile(t + whole), :], turned[tile(t + whole + 1), :])
+            rate = (before if t < margin else after if t >= margin + inner else RATE) / (1.0 + value[0:1] * value[0:1])
+            tiles[tile(t), :] = value + rate * (behind + ahead - 2.0 * value)
+
+    fitted[...] = jnp.zeros(fitted.shape, f32)
+    some = 8
+    for t in range(0, inner, some):
+        values = [tiles[pl.ds((margin + t) * k + j, some, stride=k), :] for j in range(macro.shape[0])]
+        for n, group in enumerate(fit_rows(values)):
+            for j, value in enumerate(group):
+                fitted[pl.ds((n * inner + t) * k + j, some, stride=k), :] = value
+    for t in range(inner):
+        macro[:, column(t)] = tiles[tile(margin + t), :][: macro.shape[0]]
+        for n, right in enumerate((right_e, right_p)):
+            right[:, column(t)] = stacked_right(fitted[(n * inner + t) * k : (n * inner + t + 1) * k, :])
 
 
 def join_kernel(plane, d, offset, sums, entering, left, spread, _, kept):
@@ -491,7 +515,7 @@
     left_e, left_p, right_e, right_p, updated = refs[parts:]
     vel = kept[0].shape[1]
     width = 4 * plane
-    block = min(vel, BLOCK)
+    block = min(vel, 2 * BLOCK)
 
     def body(*outs):
         at = pl.ds(pl.multiple_of(pl.program_id(0) * width, width), width)
@@ -527,36 +551,36 @@
     params = pltpu.CompilerParams(vmem_limit_bytes=12 * MIB)
 
     depth = -(-3 * cells // LANES) * LANES
-    reach, gain, ends, spread = pl.pallas_call(
-        lambda *refs: prepare_kernel(plane, PARTS, *refs),
-        out_shape=[
-            jax.ShapeDtypeStruct((2, cells, vel), f32),
-            pltpu.VMEM((2, vel, depth), bf16),
-            pltpu.VMEM((2 * PARTS, 8, LANES), f32),
-            pltpu.VMEM((depth, lanes), bf16),
-        ],
-        in_specs=[vmem],
-        out_specs=[vmem] * 4,
-        compiler_params=params,
-        name="prepare",
-    )(jnp.swapaxes(factors, 1, 2))
-    gain, ends, spread = in_vmem(gain), in_vmem(ends), in_vmem(spread)
+    rows = min(BLOCK, vel_part)
+    payload = whole * vel_part + vel_part // 2 + 8
+    hbm = pl.BlockSpec(memory_space=pltpu.HBM)
     dist = pltpu.with_memory_space_constraint(dist, pltpu.HBM)
-
-    payload = whole * vel_part + vel_part // 2 + 8
+    table = pltpu.with_memory_space_constraint(jnp.swapaxes(factors, 1, 2), pltpu.HBM)
+    shared = [
+        jax.ShapeDtypeStruct((2, cells, vel), f32),
+        pltpu.VMEM((2, vel, depth), bf16),
+        pltpu.VMEM((2 * PARTS, 8, LANES), f32),
+        pltpu.VMEM((depth, lanes), bf16),
+    ]
     swept, sent = [], []
     for part in range(PARTS):
-        out = pl.pallas_call(
-            lambda *refs, part=part: sweep_kernel(part, min(BLOCK, vel_part), plane, *refs),
+        out, *leaving = pl.pallas_call(
+            lambda *refs, part=part: sweep_kernel(part, rows, plane, PARTS, count, *refs),
             out_shape=[pltpu.VMEM((2, vel_part, lanes), f32)]
-            + [jax.ShapeDtypeStruct((payload, LANES), f32)] * (count - 1),
-            in_specs=[pl.BlockSpec(memory_space=pltpu.HBM), vmem, vmem, vmem],
-            out_specs=[vmem] * count,
+            + [jax.ShapeDtypeStruct((payload, LANES), f32)] * (count - 1)
+            + ([] if part else shared),
+            in_specs=[hbm] + ([vmem] * 3 if part else [hbm]),
+            out_specs=[vmem] * (count + (0 if part else len(shared))),
+            scratch_shapes=[pltpu.VMEM((3, rows, lanes), f32), pltpu.SemaphoreType.DMA((3,))]
+            + ([] if part else [pltpu.VMEM((2, cells, vel), f32), pltpu.SemaphoreType.DMA(())]),
             compiler_params=params,
             name="sweep",
-        )(dist, gain, ends, spread)
-        swept.append(in_vmem(out[0]))
-        sent.append(out[1:])
+        )(dist, *([gain, ends, spread] if part else [table]))
+        if part == 0:
+            leaving, (reach, gain, ends, spread) = leaving[: count - 1], leaving[count - 1 :]
+            gain, ends, spread = in_vmem(gain), in_vmem(ends), in_vmem(spread)
+        swept.append(in_vmem(out))
+        sent.append(leaving)
 
     padded = jnp.pad(jnp.moveaxis(weights, 1, 0), ((0, 0), (0, k - moments_n), (0, 0)))
     moments, *lhs = pl.pallas_call(
@@ -589,7 +613,7 @@
         found, *moments = pl.pallas_call(
             lambda *refs, part=part, last=last: correct_kernel(plane, part, last, *refs),
             out_shape=[pltpu.VMEM((2, vel_part, width), f32)] + out,
-            in_specs=[vmem] * (3 + len(got)),
+            in_specs=[vmem] * (3 + len(got)) + [anywhere],
             out_specs=[vmem] * (1 + len(out)),
             scratch_shapes=[
                 pltpu.VMEM((2, vel_part, (whole + 1) * LANES), f32),
@@ -597,7 +621,7 @@
             ],
             compiler_params=params,
             name="correct",
-        )(*(moments if part else [moments]), *[in_vmem(x) for x in lhs], *got)
+        )(*(moments if part else [moments]), *[in_vmem(x) for x in lhs], *got, left_r)
         entering.append(in_vmem(found))
     mine, other = moments
 
@@ -655,17 +679,19 @@
     halo = lax.ppermute(edge, ("gx", "vert"), beyond)
     join(*chunks.pop(0), total)
     more = lax.ppermute(halo, "vert", [(v, v ^ step) for v in range(size)])
-    while chunks:
+    while len(chunks) > 1:
         join(*chunks.pop(0), halo)
     (own,) = combine(close_kernel, [(k, lanes // 2 + margin)], total, got, halo, more, *[in_vmem(x) for x in kept])
     rest = lax.ppermute(own, "vert", [(v, v ^ 1) for v in range(size)])
+    join(*chunks.pop(0), own)
 
     macro, right_e, right_p = pl.pallas_call(
         lambda *refs: fit_kernel(plane, *refs),
         out_shape=[jax.ShapeDtypeStruct((moments_n, lanes), f32)] + [pltpu.VMEM((LANES, lanes), bf16)] * 2,
         in_specs=[vmem] * 2,
         out_specs=[vmem] * 3,
-        scratch_shapes=[pltpu.VMEM((k, lanes + 2 * margin), f32)],
+        scratch_shapes=[pltpu.VMEM(((lanes + 2 * margin) // LANES * k, LANES), f32)] * 2
+        + [pltpu.VMEM((2 * lanes // LANES * k, LANES), f32)],
         compiler_params=params,
         name="fit",
     )(own, rest)

time: 75.5 us -> 70.4 us (0.932)
  Pallas kernels: 53.5 us -> 49.6 us
  local copies, waits for them, and re-layouts: 0.95 us -> 0.05 us
    pallas_call x1, Pallas kernels: 8.2 us -> 6.62 us  [per_device(): pl.pallas_call(lambda *refs: moment_kernel(plane, PARTS, *refs), out_shap...]
    ppermute x1, waiting for transfers between devices: 1.14 us -> 0.01 us  [per_device(): rest = lax.ppermute(own, 'vert', [(v, v ^ 1) for v in range(size)])]
    pallas_call x2, Pallas kernels: 3.25 us -> 2.29 us  [per_device(): pl.pallas_call(lambda *refs, part=part, last=last: correct_kernel(plane,...]
    pallas_call x1, Pallas kernels: 3.02 us -> 2.11 us  [per_device(): pl.pallas_call(lambda *refs: fit_kernel(plane, *refs), out_shape=[jax.Sha...]
    unnamed x9 -> x7, local copies, waits for them, and re-layouts: 0.93 us -> 0.03 us
    pallas_call x1, Pallas kernels: 10.7 us -> 9.89 us  [per_device(): pl.pallas_call(lambda *refs: finish_kernel(plane, PARTS, *refs), out_shap...]
    ppermute x1, waiting for transfers between devices: 0.01 us -> 0.77 us  [per_device(): more = lax.ppermute(halo, 'vert', [(v, v ^ step) for v in range(size)])]
    pallas_call x3 -> x2, Pallas kernels: 12.1 us -> 12.5 us  [per_device(): pl.pallas_call(lambda *refs, part=part: sweep_kernel(part, rows, plane, P...]
  transfers between devices with their start and end apart: 12 -> 12, of which waited for: 3 -> 4; matrix products, arithmetic and copies ran while one was open for 0% -> 0% of each run, Pallas kernels for 41% -> 42%
where the time goes in v3:
time: 70.4 us; the launch traced here: 70.2 us
  Pallas kernels  49.6 us (70%)
  starting transfers between devices  15.8 us (22%)
  waiting for transfers between devices  3.92 us (6%)
  between operations  0.83 us (1%)
    pallas_call x4, Pallas kernels, join(): pl.pallas_call(lambda *refs: join_kernel(plane, d, part * vel_part, *refs...  15.8 us
    pallas_call x2, Pallas kernels, per_device(): pl.pallas_call(lambda *refs, part=part: sweep_kernel(part, rows, plane, P...  12.5 us
    pallas_call x1, Pallas kernels, per_device(): pl.pallas_call(lambda *refs: finish_kernel(plane, PARTS, *refs), out_shap...  9.89 us
    ppermute x6, starting transfers between devices, per_device(): lax.ppermute(sent[part][s - 1], 'gx', [(i, i ^ s) for i in range(count)])  8.1 us
    pallas_call x1, Pallas kernels, per_device(): pl.pallas_call(lambda *refs: moment_kernel(plane, PARTS, *refs), out_shap...  6.62 us
    ppermute x2, waiting for transfers between devices, per_device(): lax.ppermute(total if i else other, 'vert', [(v, v ^ step) for v in range...  2.77 us
    ppermute x1, starting transfers between devices, per_device(): got = lax.ppermute(total, 'vert', [(v, v ^ step) for v in range(size)])  2.76 us
    pallas_call x2, Pallas kernels, per_device(): pl.pallas_call(lambda *refs, part=part, last=last: correct_kernel(plane,...  2.29 us
  transfers between devices with their start and end apart: 12, of which 4 were waited for; matrix products, arithmetic and copies ran while one was open for 0% of the time, Pallas kernels for 42%

profile of v3, /device:TPU:0, one launch (start us, length us, event | category | flops | bytes accessed | tf_op | source)
XLA Modules:
  0.0 70.2 jit_solution(11243015906327422336)
XLA Ops:
  0.6 6.8 %sweep.2 = (f32[2,256,6144]{2,1,0:T(8,128)S(1)}, f32[392,128]{1,0:T(8,128)S(1)}, f32[392,128]{1,0:T(8,128)S(1)}, f32[392,128]{1,0:T(8,128)S(1)}, f32[2,32,512]{2...) custom-call(f32[2,512,6144]{2,1,0:T(8,128)} %refs_0_.3, ...), custom_call_target="tpu_custom_call" | custom-call | tf_op jit(solution)/shard_map/sweep/pallas_call | solution.py:567
  7.4 3.0 %collective-permute-start = (f32[392,128]{1,0:T(8,128)S(1)}, f32[392,128]{1,0:T(8,128)S(1)}, u32[]{:S(2)}, u32[]{:S(2)}) collective-permute-start(f32[392,128]{1,0:T(8,128)S(1)} %get-tuple-element.39), channel_id=1, source_target_pairs={{0,8},{8,0},{16,24},{24,16},{1,9},{9,1},{17,25},{25,17},{2,10},{10... | collective-permute-start | bytes 602120 | tf_op jit(solution)/shard_map/ppermute | solution.py:610
  10.5 1.5 %collective-permute-start.1 = (f32[392,128]{1,0:T(8,128)S(1)}, f32[392,128]{1,0:T(8,128)S(1)}, u32[]{:S(2)}, u32[]{:S(2)}) collective-permute-start(f32[392,128]{1,0:T(8,128)S(1)} %get-tuple-element.40), channel_id=1, source_target_pairs={{0,16},{8,24},{16,0},{24,8},{1,17},{9,25},{17,1},{25,9},{2,18},{10... | collective-permute-start | bytes 602120 | tf_op jit(solution)/shard_map/ppermute | solution.py:610
  12.0 0.0 collective-permute-start.2
  12.0 0.0 copy-start.2
  12.0 0.0 copy-start.1
  12.0 0.0 copy-start
  12.0 5.7 %sweep.3 = (f32[2,256,6144]{2,1,0:T(8,128)S(1)}, f32[392,128]{1,0:T(8,128)S(1)}, f32[392,128]{1,0:T(8,128)S(1)}, f32[392,128]{1,0:T(8,128)S(1)}) custom-call(f32[2,512,6144]{2,1,0:T(8,128)} %refs_0_.3, bf16[2,512,128]{2,1,0:T(8,128)(2,1)S(1)} %get-tuple-element.32.refs_1_, f32[4,8,128]{2,1,0:T(8,128)S(1)} %get-tuple-element.33.refs_2_, ...), custom_call_target="tpu_custom_call" | custom-call | tf_op jit(solution)/shard_map/sweep/pallas_call | solution.py:567
  17.7 2.0 %collective-permute-start.3 = (f32[392,128]{1,0:T(8,128)S(1)}, f32[392,128]{1,0:T(8,128)S(1)}, u32[]{:S(2)}, u32[]{:S(2)}) collective-permute-start(f32[392,128]{1,0:T(8,128)S(1)} %get-tuple-element.45), channel_id=1, source_target_pairs={{0,8},{8,0},{16,24},{24,16},{1,9},{9,1},{17,25},{25,17},{2,10},{10... | collective-permute-start | bytes 602120 | tf_op jit(solution)/shard_map/ppermute | solution.py:610
  19.7 1.5 %collective-permute-start.4 = (f32[392,128]{1,0:T(8,128)S(1)}, f32[392,128]{1,0:T(8,128)S(1)}, u32[]{:S(2)}, u32[]{:S(2)}) collective-permute-start(f32[392,128]{1,0:T(8,128)S(1)} %get-tuple-element.46), channel_id=1, source_target_pairs={{0,16},{8,24},{16,0},{24,8},{1,17},{9,25},{17,1},{25,9},{2,18},{10... | collective-permute-start | bytes 602120 | tf_op jit(solution)/shard_map/ppermute | solution.py:610
  21.3 0.0 collective-permute-done.refs_3_
  21.3 0.0 collective-permute-start.5
  21.3 0.0 copy-done.2
  21.3 0.0 copy-done.1
  21.3 0.0 copy-done
  21.4 6.6 %moments.1 = (f32[16,6144]{1,0:T(8,128)S(1)}, bf16[2,512,512]{2,1,0:T(8,128)(2,1)S(1)}, bf16[2,512,512]{2,1,0:T(8,128)(2,1)S(1)}) custom-call(f32[2,32,512]{2,1,0:T(8,128)S(1)} %get-tuple-element.31.refs_0_.reach, f32[2,16,512]{2,1,0:T(8,128)S(1)} %pad.4.refs_1_, f32[2,256,6144]{2,1,0:T(8,128)S(1)} %get-tuple-element.30.refs_2_.refs_0_, ...), custom_call_target="tpu_custom_call" | custom-call | tf_op jit(solution)/shard_map/moments/pallas_call | solution.py:586
  28.0 0.3 tables.1
  28.3 0.0 collective-permute-done.1.refs_4_
  28.3 0.0 collective-permute-done.2.refs_5_
  28.3 1.1 %correct.2 = (f32[2,256,384]{2,1,0:T(8,128)S(1)}, f32[16,6144]{1,0:T(8,128)S(1)}) custom-call(f32[16,6144]{1,0:T(8,128)S(1)} %get-tuple-element.36._.refs_0_, bf16[2,512,512]{2,1,0:T(8,128)(2,1)S(1)} %get-tuple-element.37.refs_1_, bf16[2,512,512]{2,1,0:T(8,128)(2,1)S(1)} %get-tuple-element.38.refs_2_, f32[392,128]{1,0:T(8,128)S(1)} %collective-permute-done.refs_3_, ...), custom_call_target="tpu_custom_call" | custom-call | tf_op jit(solution)/shard_map/correct/pallas_call | solution.py:613
  29.4 0.0 collective-permute-done.3.refs_3_
  29.4 0.4 collective-permute-done.4.refs_4_
  29.8 0.0 collective-permute-done.5.refs_5_
  29.8 1.2 %correct.3 = (f32[2,256,384]{2,1,0:T(8,128)S(1)}, f32[16,3072]{1,0:T(8,128)S(1)}, f32[16,3072]{1,0:T(8,128)S(1)}) custom-call(f32[16,6144]{1,0:T(8,128)S(1)} %get-tuple-element.44.refs_0_, bf16[2,512,512]{2,1,0:T(8,128)(2,1)S(1)} %get-tuple-element.37.refs_1_, bf16[2,512,512]{2,1,0:T(8,128)(2,1)S(1)} %get-tuple-element.38.refs_2_, ...), custom_call_target="tpu_custom_call" | custom-call | tf_op jit(solution)/shard_map/correct/pallas_call | solution.py:613
  31.0 0.1 collective-permute-start.6
  31.1 1.4 %collective-permute-done.6.b = f32[16,3072]{1,0:T(8,128)S(1)} collective-permute-done((f32[16,3072]{1,0:T(8,128)S(1)}, f32[16,3072]{1,0:T(8,128)S(1)}, u32[]{:S(2)}, u32[]{:S(2)}) %collective-permute-start.6) | collective-permute-done | bytes 196640 | tf_op jit(solution)/shard_map/ppermute | solution.py:665
  32.5 1.7 %collective-permute-start.7 = (f32[16,3072]{1,0:T(8,128)S(1)}, f32[16,3072]{1,0:T(8,128)S(1)}, u32[]{:S(2)}, u32[]{:S(2)}) collective-permute-start(f32[16,3072]{1,0:T(8,128)S(1)} %add_kernel.1.refs_4_.a), channel_id=1, source_target_pairs={{0,2},{1,3},{2,0},{3,1},{4,6},{5,7},{6,4},{7,5},{8,10},{9,11},{10,... | collective-permute-start | bytes 589832 | tf_op jit(solution)/shard_map/ppermute | solution.py:665
  34.3 3.9 %join.4.refs_0_ = f32[2,256,6144]{2,1,0:T(8,128)S(1)} custom-call(f32[2,256,6144]{2,1,0:T(8,128)S(1)} %get-tuple-element.30.refs_2_.refs_0_, f32[2,256,384]{2,1,0:T(8,128)S(1)} %get-tuple-element.43.refs_1_, bf16[2,512,128]{2,1,0:T(8,128)(2,1)S(1)} %get-tuple-element.42.refs_6_.refs_2_, ...), custom_call_target="tpu_custom_call", output_to_operand_aliasing={{}: (0, {})} | custom-call | flops 805306368 | bytes 12582912 | tf_op jit(solution)/shard_map/join/pallas_call | solution.py:634
  38.2 1.3 %collective-permute-done.7.b = f32[16,3072]{1,0:T(8,128)S(1)} collective-permute-done((f32[16,3072]{1,0:T(8,128)S(1)}, f32[16,3072]{1,0:T(8,128)S(1)}, u32[]{:S(2)}, u32[]{:S(2)}) %collective-permute-start.7) | collective-permute-done | bytes 196640 | tf_op jit(solution)/shard_map/ppermute | solution.py:665
  39.6 2.8 %collective-permute-start.9 = (f32[16,3072]{1,0:T(8,128)S(1)}, f32[16,3072]{1,0:T(8,128)S(1)}, u32[]{:S(2)}, u32[]{:S(2)}) collective-permute-start(f32[16,3072]{1,0:T(8,128)S(1)} %get-tuple-element.50.refs_4_.a), channel_id=1, source_target_pairs={{0,4},{1,5},{2,6},{3,7},{4,0},{5,1},{6,2},{7,3},{8,12},{9,13},{10,... | collective-permute-start | bytes 589832 | tf_op jit(solution)/shard_map/ppermute | solution.py:673
  42.3 0.8 %collective-permute-start.8 = (f32[16,768]{1,0:T(8,128)S(1)}, f32[16,768]{1,0:T(8,128)S(1)}, u32[]{:S(2)}, u32[]{:S(2)}) collective-permute-start(f32[16,768]{1,0:T(8,128)S(1)} %get-tuple-element.52), channel_id=1, source_target_pairs={{1,8},{8,1},{3,10},{10,3},{5,12},{12,5},{7,14},{14,7},{9,16},{16,9... | collective-permute-start | bytes 147464 | tf_op jit(solution)/shard_map/ppermute | solution.py:679
  43.2 4.0 %join.5.refs_0_ = f32[2,256,6144]{2,1,0:T(8,128)S(1)} custom-call(f32[2,256,6144]{2,1,0:T(8,128)S(1)} %join.4.refs_0_, f32[2,256,384]{2,1,0:T(8,128)S(1)} %get-tuple-element.43.refs_1_, bf16[2,512,128]{2,1,0:T(8,128)(2,1)S(1)} %get-tuple-element.42.refs_6_.refs_2_, bf16[128,6144]{1,0:T(8,128)(2,1)S(1)} %get-tuple-element.34.refs_3_, ...), custom_call_target="tpu_custom_call", output_to_operand_aliasing={{}: (0, {})} | custom-call | flops 805306368 | bytes 12582912 | tf_op jit(solution)/shard_map/join/pallas_call | solution.py:634
  47.1 0.0 collective-permute-done.8.refs_4_.halo
  47.1 0.3 collective-permute-start.10
  47.4 4.0 %join.6.refs_1_.refs_0_ = f32[2,256,6144]{2,1,0:T(8,128)S(1)} custom-call(f32[2,256,6144]{2,1,0:T(8,128)S(1)} %get-tuple-element.35.refs_3_.refs_0_, f32[2,256,384]{2,1,0:T(8,128)S(1)} %get-tuple-element.51.refs_1_, bf16[2,512,128]{2,1,0:T(8,128)(2,1)S(1)} %get-tuple-element.42.refs_6_.refs_2_, ...), custom_call_target="tpu_custom_call", output_to_operand_aliasing={{}: (0, {})} | custom-call | flops 805306368 | bytes 12582912 | tf_op jit(solution)/shard_map/join/pallas_call | solution.py:634
  51.4 0.8 %collective-permute-done.10.more = f32[16,768]{1,0:T(8,128)S(1)} collective-permute-done((f32[16,768]{1,0:T(8,128)S(1)}, f32[16,768]{1,0:T(8,128)S(1)}, u32[]{:S(2)}, u32[]{:S(2)}) %collective-permute-start.10) | collective-permute-done | bytes 49184 | tf_op jit(solution)/shard_map/ppermute | solution.py:681
  52.2 0.0 collective-permute-done.9.b
  52.2 2.0 %collective-permute-start.11 = (f32[16,3840]{1,0:T(8,128)S(1)}, f32[16,3840]{1,0:T(8,128)S(1)}, u32[]{:S(2)}, u32[]{:S(2)}) collective-permute-start(f32[16,3840]{1,0:T(8,128)S(1)} %close_kernel.1.refs_4_.refs_0_), channel_id=1, source_target_pairs={{0,1},{1,0},{2,3},{3,2},{4,5},{5,4},{6,7},{7,6},{8,9},{9,8},{10,11... | collective-permute-start | bytes 737288 | tf_op jit(solution)/shard_map/ppermute | solution.py:685
  54.2 4.0 %join.7.refs_1_ = f32[2,256,6144]{2,1,0:T(8,128)S(1)} custom-call(f32[2,256,6144]{2,1,0:T(8,128)S(1)} %join.6.refs_1_.refs_0_, f32[2,256,384]{2,1,0:T(8,128)S(1)} %get-tuple-element.51.refs_1_, bf16[2,512,128]{2,1,0:T(8,128)(2,1)S(1)} %get-tuple-element.42.refs_6_.refs_2_, ...), custom_call_target="tpu_custom_call", output_to_operand_aliasing={{}: (0, {})} | custom-call | flops 805306368 | bytes 12582912 | tf_op jit(solution)/shard_map/join/pallas_call | solution.py:634
  58.2 0.0 collective-permute-done.11.refs_1_
  58.2 2.1 %fit.1 = (f32[13,6144]{1,0:T(8,128)}, bf16[128,6144]{1,0:T(8,128)(2,1)S(1)}, bf16[128,6144]{1,0:T(8,128)(2,1)S(1)}) custom-call(f32[16,3840]{1,0:T(8,128)S(1)} %close_kernel.1.refs_4_.refs_0_, f32[16,3840]{1,0:T(8,128)S(1)} %collective-permute-done.11.refs_1_), custom_call_target="tpu_custom_call" | custom-call | tf_op jit(solution)/shard_map/fit/pallas_call | solution.py:688
  60.4 9.9 %finish.1 = f32[2,512,6144]{2,1,0:T(8,128)} custom-call(f32[2,256,6144]{2,1,0:T(8,128)S(1)} %join.5.refs_0_, f32[2,256,6144]{2,1,0:T(8,128)S(1)} %join.7.refs_1_, bf16[2,512,128]{2,1,0:T(8,128)(2,1)S(1)} %get-tuple-element.53.refs_2_, bf16[2,512,128]{2,1,0:T(8,128)(2,1)S(1)} %get-tuple-element.54.refs_3_, bf16[128,6144]{1,0:T(8,128)(2,1)S(1)} %get-tuple-element.55.refs_4_, ...), custom_call_target="tpu_custom_call" | custom-call | tf_op jit(solution)/shard_map/finish/pallas_call | solution.py:700
  (7 shorter events, 0.1 us)
Async XLA Ops:
  7.4 13.8 %collective-permute-start = (f32[392,128]{1,0:T(8,128)S(1)}, f32[392,128]{1,0:T(8,128)S(1)}, u32[]{:S(2)}, u32[]{:S(2)}) collective-permute-start(f32[392,128]{1,0:T(8,128)S(1)} %get-tuple-element.39), channel_id=1, source_target_pairs={{0,8},{8,0},{16,24},{24,16},{1,9},{9,1},{17,25},{25,17},{2,10},{10... | collective-permute-start | bytes 602120 | tf_op jit(solution)/shard_map/ppermute | solution.py:610
  10.5 17.9 %collective-permute-start.1 = (f32[392,128]{1,0:T(8,128)S(1)}, f32[392,128]{1,0:T(8,128)S(1)}, u32[]{:S(2)}, u32[]{:S(2)}) collective-permute-start(f32[392,128]{1,0:T(8,128)S(1)} %get-tuple-element.40), channel_id=1, source_target_pairs={{0,16},{8,24},{16,0},{24,8},{1,17},{9,25},{17,1},{25,9},{2,18},{10... | collective-permute-start | bytes 602120 | tf_op jit(solution)/shard_map/ppermute | solution.py:610
  12.0 16.3 %collective-permute-start.2 = (f32[392,128]{1,0:T(8,128)S(1)}, f32[392,128]{1,0:T(8,128)S(1)}, u32[]{:S(2)}, u32[]{:S(2)}) collective-permute-start(f32[392,128]{1,0:T(8,128)S(1)} %get-tuple-element.41), channel_id=1, source_target_pairs={{0,24},{8,16},{16,8},{24,0},{1,25},{9,17},{17,9},{25,1},{2,26},{10... | collective-permute-start | bytes 602120 | tf_op jit(solution)/shard_map/ppermute | solution.py:610
  12.0 9.3 %copy-start.2 = (f32[2,512]{1,0:T(2,128)S(1)}, f32[2,512]{1,0:T(2,128)}, u32[]{:S(2)}) copy-start(f32[2,512]{1,0:T(2,128)} %param.9) | copy-start | bytes 12292
  12.0 9.3 %copy-start.1 = (f32[3,2,512]{2,1,0:T(2,128)S(1)}, f32[3,2,512]{2,1,0:T(2,128)}, u32[]{:S(2)}) copy-start(f32[3,2,512]{2,1,0:T(2,128)} %param.7) | copy-start | bytes 36868
  12.0 9.3 %copy-start = (f32[13,2,512]{2,1,0:T(2,128)S(1)}, f32[13,2,512]{2,1,0:T(2,128)}, u32[]{:S(2)}) copy-start(f32[13,2,512]{2,1,0:T(2,128)} %param.8) | copy-start | bytes 159748
  17.7 11.7 %collective-permute-start.3 = (f32[392,128]{1,0:T(8,128)S(1)}, f32[392,128]{1,0:T(8,128)S(1)}, u32[]{:S(2)}, u32[]{:S(2)}) collective-permute-start(f32[392,128]{1,0:T(8,128)S(1)} %get-tuple-element.45), channel_id=1, source_target_pairs={{0,8},{8,0},{16,24},{24,16},{1,9},{9,1},{17,25},{25,17},{2,10},{10... | collective-permute-start | bytes 602120 | tf_op jit(solution)/shard_map/ppermute | solution.py:610
  19.7 10.1 %collective-permute-start.4 = (f32[392,128]{1,0:T(8,128)S(1)}, f32[392,128]{1,0:T(8,128)S(1)}, u32[]{:S(2)}, u32[]{:S(2)}) collective-permute-start(f32[392,128]{1,0:T(8,128)S(1)} %get-tuple-element.46), channel_id=1, source_target_pairs={{0,16},{8,24},{16,0},{24,8},{1,17},{9,25},{17,1},{25,9},{2,18},{10... | collective-permute-start | bytes 602120 | tf_op jit(solution)/shard_map/ppermute | solution.py:610
  21.3 8.5 %collective-permute-start.5 = (f32[392,128]{1,0:T(8,128)S(1)}, f32[392,128]{1,0:T(8,128)S(1)}, u32[]{:S(2)}, u32[]{:S(2)}) collective-permute-start(f32[392,128]{1,0:T(8,128)S(1)} %get-tuple-element.47), channel_id=1, source_target_pairs={{0,24},{8,16},{16,8},{24,0},{1,25},{9,17},{17,9},{25,1},{2,26},{10... | collective-permute-start | bytes 602120 | tf_op jit(solution)/shard_map/ppermute | solution.py:610
  31.0 1.5 %collective-permute-start.6 = (f32[16,3072]{1,0:T(8,128)S(1)}, f32[16,3072]{1,0:T(8,128)S(1)}, u32[]{:S(2)}, u32[]{:S(2)}) collective-permute-start(f32[16,3072]{1,0:T(8,128)S(1)} %get-tuple-element.49), channel_id=1, source_target_pairs={{0,1},{1,0},{2,3},{3,2},{4,5},{5,4},{6,7},{7,6},{8,9},{9,8},{10,11... | collective-permute-start | bytes 589832 | tf_op jit(solution)/shard_map/ppermute | solution.py:665
  32.5 7.0 %collective-permute-start.7 = (f32[16,3072]{1,0:T(8,128)S(1)}, f32[16,3072]{1,0:T(8,128)S(1)}, u32[]{:S(2)}, u32[]{:S(2)}) collective-permute-start(f32[16,3072]{1,0:T(8,128)S(1)} %add_kernel.1.refs_4_.a), channel_id=1, source_target_pairs={{0,2},{1,3},{2,0},{3,1},{4,6},{5,7},{6,4},{7,5},{8,10},{9,11},{10,... | collective-permute-start | bytes 589832 | tf_op jit(solution)/shard_map/ppermute | solution.py:665
  39.6 12.6 %collective-permute-start.9 = (f32[16,3072]{1,0:T(8,128)S(1)}, f32[16,3072]{1,0:T(8,128)S(1)}, u32[]{:S(2)}, u32[]{:S(2)}) collective-permute-start(f32[16,3072]{1,0:T(8,128)S(1)} %get-tuple-element.50.refs_4_.a), channel_id=1, source_target_pairs={{0,4},{1,5},{2,6},{3,7},{4,0},{5,1},{6,2},{7,3},{8,12},{9,13},{10,... | collective-permute-start | bytes 589832 | tf_op jit(solution)/shard_map/ppermute | solution.py:673
  42.3 4.8 %collective-permute-start.8 = (f32[16,768]{1,0:T(8,128)S(1)}, f32[16,768]{1,0:T(8,128)S(1)}, u32[]{:S(2)}, u32[]{:S(2)}) collective-permute-start(f32[16,768]{1,0:T(8,128)S(1)} %get-tuple-element.52), channel_id=1, source_target_pairs={{1,8},{8,1},{3,10},{10,3},{5,12},{12,5},{7,14},{14,7},{9,16},{16,9... | collective-permute-start | bytes 147464 | tf_op jit(solution)/shard_map/ppermute | solution.py:679
  47.1 5.1 %collective-permute-start.10 = (f32[16,768]{1,0:T(8,128)S(1)}, f32[16,768]{1,0:T(8,128)S(1)}, u32[]{:S(2)}, u32[]{:S(2)}) collective-permute-start(f32[16,768]{1,0:T(8,128)S(1)} %collective-permute-done.8.refs_4_.halo), channel_id=1, source_target_pairs={{0,4},{1,5},{2,6},{3,7},{4,0},{5,1},{6,2},{7,3},{8,12},{9,13},{10,... | collective-permute-start | bytes 147464 | tf_op jit(solution)/shard_map/ppermute | solution.py:681
  52.2 6.0 %collective-permute-start.11 = (f32[16,3840]{1,0:T(8,128)S(1)}, f32[16,3840]{1,0:T(8,128)S(1)}, u32[]{:S(2)}, u32[]{:S(2)}) collective-permute-start(f32[16,3840]{1,0:T(8,128)S(1)} %close_kernel.1.refs_4_.refs_0_), channel_id=1, source_target_pairs={{0,1},{1,0},{2,3},{3,2},{4,5},{5,4},{6,7},{7,6},{8,9},{9,8},{10,11... | collective-permute-start | bytes 737288 | tf_op jit(solution)/shard_map/ppermute | solution.py:685

commit v4 on v3

--- a/solution.py
+++ b/solution.py
@@ -45,16 +45,24 @@
 
 def swap_cells(pair, whole, low):
     tiles = len(pair)
-    turned = [turn(t) for t in pair]
-    return [
-        jnp.where(low, turned[(t + whole) % tiles], turned[(t + whole + 1) % tiles])
-        for t in range(tiles)
-    ]
-
-
-def seen_before(new, old, backward, whole, low):
+    return [turn(jnp.where(low, pair[(t + whole + 1) % tiles], pair[(t + whole) % tiles])) for t in range(tiles)]
+
+
+def other_cell(new, old, backward, whole, low):
+    tiles = len(new)
     first, second = (old, new) if backward else (new, old)
-    return first[:whole] + [jnp.where(low, first[whole], second[whole])] + second[whole + 1 :]
+    upper = first[:whole] + second[whole:]
+    lower = first[: whole + 1] + second[whole + 1 :]
+    return [turn(jnp.where(low, lower[(t + whole + 1) % tiles], upper[(t + whole) % tiles])) for t in range(tiles)]
+
+
+def eights(rows):
+    return -(-rows // 8) * 8
+
+
+def packed_rows(t, tiles, moments):
+    rest = moments - 8
+    return slice(8 * t, 8 * t + 8), slice(8 * tiles + rest * t, 8 * tiles + rest * (t + 1))
 
 
 def sweep_rows(rows, load, store, gains, backward, pairs, plane):
@@ -68,7 +76,7 @@
         sums = [old[t] + gain[:, t * LANES : (t + 1) * LANES] * load(p, t) for t in range(tiles)]
         for t in range(tiles):
             store(p, t, sums[t])
-    crossed = swap_cells(seen_before(sums, old, backward, whole, low), whole, low)
+    crossed = other_cell(sums, old, backward, whole, low)
     return [sums[t] + crossed[t] for t in range(tiles)]
 
 
@@ -103,14 +111,20 @@
                 at = c * (vel // parts) + 8 * j
                 tile = jnp.where(lane == j, jnp.broadcast_to(column[at : at + 8, 0:1], (8, LANES)), tile)
             ends[2 * c + d, :, :] = tile
-    row = lax.broadcasted_iota(jnp.int32, (cells, 4 * LANES), 0) * plane
-    for at in range(0, spread.shape[1], 4 * LANES):
-        place = lax.broadcasted_iota(jnp.int32, (cells, 4 * LANES), 1) + at
-        own = jnp.where((place >= row) & (place < row + plane), 1.0, 0.0).astype(bf16)
+    row = lax.broadcasted_iota(jnp.int32, (cells, LANES), 0)
+    low = low_half(cells)
+    number = 2 * plane // LANES
+    for t in range(spread.shape[1] // LANES):
+        cell = t // number * 2
+        middle = plane // LANES
+        at = t % number
+        one = cell if at < middle else cell + 1 if at > middle else jnp.where(low, cell, cell + 1)
+        own = jnp.where(row == one, 1.0, 0.0).astype(bf16)
+        column = slice(t * LANES, (t + 1) * LANES)
         for i in range(3):
-            spread[i * cells : (i + 1) * cells, at : at + 4 * LANES] = own
+            spread[i * cells : (i + 1) * cells, column] = own
         if depth > 3 * cells:
-            spread[3 * cells :, at : at + 4 * LANES] = jnp.zeros((depth - 3 * cells, 4 * LANES), bf16)
+            spread[3 * cells :, column] = jnp.zeros((depth - 3 * cells, LANES), bf16)
 
 
 def turned_thirds(x, depth):
@@ -245,13 +259,13 @@
                 out[:, pl.ds(pl.multiple_of(behind * width, width), width)] += moved
         out[:, at] += here
 
-    @pl.loop(0, pairs // 2)
+    @pl.loop(0, pairs // GROUP)
     def _(i):
-        for u in range(2):
-            pair(2 * i + u)
-
-
-def correct_kernel(plane, part, last, moments, high_lhs, rest_lhs, *refs):
+        for u in range(GROUP):
+            pair(GROUP * i + u)
+
+
+def correct_kernel(plane, part, last, number, moments, high_lhs, rest_lhs, *refs):
     count = lax.axis_size("gx")
     refs_c, refs = refs[: count - 1], refs[count:]
     entering, outs, (natural, work) = refs[0], refs[1:-2], refs[-2:]
@@ -330,13 +344,18 @@
         for p in range(pairs):
             outs[0][:, p * width : (p + 1) * width] = corrected(p)
         return
+    half_tiles = half_pairs * width // LANES
     for n in range(2):
 
         @pl.when(core == n)
         def _():
             for p in range(pairs):
                 out = outs[(p // half_pairs) ^ n]
-                out[:, p % half_pairs * width : (p % half_pairs + 1) * width] = corrected(p)
+                value = corrected(p)
+                for t in range(width // LANES):
+                    head, tail = packed_rows(p % half_pairs * (width // LANES) + t, half_tiles, number)
+                    out[head, :] = value[:8, t * LANES : (t + 1) * LANES]
+                    out[tail, :] = value[8:number, t * LANES : (t + 1) * LANES]
 
 
 def fit_rows(m):
@@ -402,30 +421,38 @@
         left_r[d, :, :] = turned_thirds(reach[d] * (1.0 - fraction), left_r.shape[2])
 
 
-def fit_kernel(plane, own, rest, macro, right_e, right_p, tiles, turned, fitted):
+def fit_kernel(plane, k, own, rest, macro, right_e, right_p, tiles, turned, fitted):
     me, count = lax.axis_index("gx"), lax.axis_size("gx")
     core = lax.axis_index("vert") % 2
     lanes = macro.shape[1]
     margin = SMOOTH * plane // LANES
     inner = lanes // LANES
     half = inner // 2
-    k = own.shape[0]
     number = inner + 2 * margin
     whole = plane // LANES
     low = low_half(k)
     tile = lambda t: slice(t % number * k, t % number * k + k)
     column = lambda t: slice(t * LANES, (t + 1) * LANES)
 
+    count_of = macro.shape[0]
+    outside = eights(half * count_of)
+
+    def place(t, ref, offset, of, size):
+        at = t * k
+        for piece, row in zip(packed_rows(of, size, count_of), (at, at + 8)):
+            some = piece.stop - piece.start
+            tiles[row : row + some, :] = ref[offset + piece.start : offset + piece.stop, :]
+
     for first, left, right in ((0, own, rest), (1, rest, own)):
 
         @pl.when(core == first)
         def _():
             for t in range(margin):
-                tiles[tile(t), :] = left[:, column(half + t)]
-                tiles[tile(margin + inner + t), :] = right[:, column(half + t)]
+                place(t, left, outside, t, margin)
+                place(margin + inner + t, right, outside, t, margin)
             for t in range(half):
-                tiles[tile(margin + t), :] = left[:, column(t)]
-                tiles[tile(margin + half + t), :] = right[:, column(t)]
+                place(margin + t, left, 0, t, half)
+                place(margin + half + t, right, 0, t, half)
 
     before = jnp.where(me > 0, RATE, 0.0)
     after = jnp.where(me < count - 1, RATE, 0.0)
@@ -452,7 +479,7 @@
             right[:, column(t)] = stacked_right(fitted[(n * inner + t) * k : (n * inner + t + 1) * k, :])
 
 
-def join_kernel(plane, d, offset, sums, entering, left, spread, _, kept):
+def join_kernel(plane, d, offset, span, sums, entering, left, spread, _, kept):
     vel = sums.shape[1]
     width = 2 * plane
     tiles, whole = width // LANES, plane // LANES
@@ -473,7 +500,7 @@
                 None if (t < whole) != (d == 1) and t != whole else there * sums[d, line, place(before, t)]
                 for t in range(tiles)
             ]
-            crossed.append(swap_cells(seen_before(own, past, d == 1, whole, low), whole, low))
+            crossed.append(other_cell(own, past, d == 1, whole, low))
         right = spread[:, pl.ds(pl.multiple_of(p * width, width), width)]
         reach = dot(left[d, offset : offset + vel, :], right)
         for n, row in enumerate(range(0, vel, rows)):
@@ -483,31 +510,35 @@
                 value = sums[d, line, place(p, t)] + crossed[n][t] + entering[d, line, tile]
                 kept[d, line, place(p, t)] = reach[line, tile] * value
 
-    @pl.loop(0, pairs // GROUP)
+    @pl.loop(*span)
     def _(i):
         for u in range(GROUP):
             pair(i * GROUP + u)
 
 
-def edge_of(x, width):
-    return jnp.where(lax.axis_index("vert") % 2 == 0, x[:, :width], x[:, x.shape[1] - width :])
-
-
 def add_kernel(a, b, *refs):
     out = refs[-1]
     out[...] = a[...] + b[...]
 
 
-def edge_kernel(a, b, *refs):
+def edge_kernel(margin, number, a, b, *refs):
     out, edge = refs[-2:]
     out[...] = a[...] + b[...]
-    edge[...] = edge_of(out, edge.shape[1])
+    first = lax.axis_index("vert") % 2 == 0
+    tiles = out.shape[0] // number
+    rest = number - 8
+    for start, size, into in ((0, 8, 0), (8 * tiles, rest, 8 * margin)):
+        low = out[start : start + size * margin, :]
+        high = out[start + size * (tiles - margin) : start + size * tiles, :]
+        edge[into : into + size * margin, :] = jnp.where(first, low, high)
+    if edge.shape[0] > number * margin:
+        edge[number * margin :, :] = jnp.zeros((edge.shape[0] - number * margin, LANES), f32)
 
 
 def close_kernel(a, b, halo, more, *refs):
-    out, lanes = refs[-1], a.shape[1]
-    out[:, :lanes] = a[...] + b[...]
-    out[:, lanes:] = halo[...] + more[...]
+    out, rows = refs[-1], a.shape[0]
+    out[:rows, :] = a[...] + b[...]
+    out[rows:, :] = halo[...] + more[...]
 
 
 def finish_kernel(plane, parts, *refs):
@@ -603,15 +634,38 @@
         name="tables",
     )(velocity[:, :, None, :], relax[:, None, :], reach, moments)
 
+    margin = SMOOTH * plane // LANES
+    half = (eights(lanes // 2 // LANES * moments_n), LANES)
+    side = (eights(margin * moments_n), LANES)
+    kept = list(swept)
+
+    def join(part, d, start, stop, after):
+        span = tuple(x * (pairs // GROUP) // 4 for x in (start, stop))
+        kept[part] = pl.pallas_call(
+            lambda *refs: join_kernel(plane, d, part * vel_part, span, *refs),
+            out_shape=pltpu.VMEM(kept[part].shape, f32),
+            in_specs=[vmem] * 4 + [anywhere],
+            out_specs=vmem,
+            input_output_aliases={0: 0},
+            compiler_params=params,
+            cost_estimate=pl.CostEstimate(
+                flops=dist.size * LANES * (stop - start) // (2 * PARTS),
+                bytes_accessed=dist.size * (stop - start) // PARTS,
+                transcendentals=0,
+            ),
+            name="join",
+        )(in_vmem(kept[part]), entering[part], in_vmem(left_r), spread, after)
+        return in_vmem(kept[part])
+
     entering = []
     for part in range(PARTS):
         last = part == PARTS - 1
         got = [
             lax.ppermute(sent[part][s - 1], "gx", [(i, i ^ s) for i in range(count)]) for s in range(1, count)
         ]
-        out = [jax.ShapeDtypeStruct((k, lanes // 2), f32)] * 2 if last else [jax.ShapeDtypeStruct((k, lanes), f32)]
+        out = [jax.ShapeDtypeStruct(half, f32)] * 2 if last else [jax.ShapeDtypeStruct((k, lanes), f32)]
         found, *moments = pl.pallas_call(
-            lambda *refs, part=part, last=last: correct_kernel(plane, part, last, *refs),
+            lambda *refs, part=part, last=last: correct_kernel(plane, part, last, moments_n, *refs),
             out_shape=[pltpu.VMEM((2, vel_part, width), f32)] + out,
             in_specs=[vmem] * (3 + len(got)) + [anywhere],
             out_specs=[vmem] * (1 + len(out)),
@@ -621,30 +675,13 @@
             ],
             compiler_params=params,
             name="correct",
-        )(*(moments if part else [moments]), *[in_vmem(x) for x in lhs], *got, left_r)
+        )(*(moments if part else [moments]), *[in_vmem(x) for x in lhs], *got, early if part else left_r)
         entering.append(in_vmem(found))
+        if not last:
+            early = join(part, 0, 0, 2, found)
     mine, other = moments
 
     size = lax.axis_size("vert")
-    margin = SMOOTH * plane
-    half = (k, lanes // 2)
-    kept = list(swept)
-
-    def join(part, d, after):
-        kept[part] = pl.pallas_call(
-            lambda *refs: join_kernel(plane, d, part * vel_part, *refs),
-            out_shape=pltpu.VMEM(kept[part].shape, f32),
-            in_specs=[vmem] * 4 + [anywhere],
-            out_specs=vmem,
-            input_output_aliases={0: 0},
-            compiler_params=params,
-            cost_estimate=pl.CostEstimate(
-                flops=4 * dist.size * LANES // (2 * PARTS), bytes_accessed=4 * dist.size // PARTS, transcendentals=0
-            ),
-            name="join",
-        )(in_vmem(kept[part]), entering[part], in_vmem(left_r), spread, after)
-        return in_vmem(kept[part])
-
     def combine(kernel, out, *args):
         done = [x for x in args if x is not None]
         return pl.pallas_call(
@@ -653,20 +690,22 @@
             in_specs=[vmem] * len(done),
             out_specs=[vmem] * len(out),
             compiler_params=params,
-            name=kernel.__name__,
+            name="add",
         )(*done)
 
     steps = [1]
     while 2 * steps[-1] < size:
         steps.append(2 * steps[-1])
     total, beside = mine, None
-    chunks = [(part, d) for part in range(PARTS) for d in range(2)]
     for i, step in enumerate(steps[:-1]):
         got = lax.ppermute(total if i else other, "vert", [(v, v ^ step) for v in range(size)])
-        if i:
-            beside = join(*chunks.pop(0), total) if len(chunks) > 3 else None
+        if i == 1:
+            join(0, 0, 2, 4, total)
+            beside = join(0, 1, 0, 2, total)
         if i == len(steps) - 2:
-            total, edge = combine(edge_kernel, [half, (k, margin)], total, got, beside)
+            total, edge = combine(
+                lambda *refs: edge_kernel(margin, moments_n, *refs), [half, side], total, got, beside
+            )
         else:
             (total,) = combine(add_kernel, [half], total, got, beside)
     step = steps[-1]
@@ -677,20 +716,20 @@
             near, far = g * size + v, (g + 1) * size + v - 1
             beyond += [(near, far), (far, near)]
     halo = lax.ppermute(edge, ("gx", "vert"), beyond)
-    join(*chunks.pop(0), total)
+    join(1, 0, 0, 4, total)
     more = lax.ppermute(halo, "vert", [(v, v ^ step) for v in range(size)])
-    while len(chunks) > 1:
-        join(*chunks.pop(0), halo)
-    (own,) = combine(close_kernel, [(k, lanes // 2 + margin)], total, got, halo, more, *[in_vmem(x) for x in kept])
+    join(0, 1, 2, 4, halo)
+    join(1, 1, 0, 2, halo)
+    (own,) = combine(close_kernel, [(half[0] + side[0], LANES)], total, got, halo, more, *[in_vmem(x) for x in kept])
     rest = lax.ppermute(own, "vert", [(v, v ^ 1) for v in range(size)])
-    join(*chunks.pop(0), own)
+    join(1, 1, 2, 4, own)
 
     macro, right_e, right_p = pl.pallas_call(
-        lambda *refs: fit_kernel(plane, *refs),
+        lambda *refs: fit_kernel(plane, k, *refs),
         out_shape=[jax.ShapeDtypeStruct((moments_n, lanes), f32)] + [pltpu.VMEM((LANES, lanes), bf16)] * 2,
         in_specs=[vmem] * 2,
         out_specs=[vmem] * 3,
-        scratch_shapes=[pltpu.VMEM(((lanes + 2 * margin) // LANES * k, LANES), f32)] * 2
+        scratch_shapes=[pltpu.VMEM((((lanes // LANES) + 2 * margin) * k, LANES), f32)] * 2
         + [pltpu.VMEM((2 * lanes // LANES * k, LANES), f32)],
         compiler_params=params,
         name="fit",

time: 70.4 us -> 68.3 us (0.970)
  Pallas kernels: 49.6 us -> 48.4 us
  waiting for transfers between devices: 3.92 us -> 2.9 us
    ppermute x2, waiting for transfers between devices: 2.77 us -> 2 us  [per_device(): lax.ppermute(total if i else other, 'vert', [(v, v ^ step) for v in range...]
    pallas_call x5 -> x8, Pallas kernels: 17.9 us -> 17.2 us  [the longest x7 15.1 us: join(): pl.pallas_call(lambda *refs: join_kernel(plane, d, part * vel_part, span,...]
  transfers between devices with their start and end apart: 12 -> 12, of which waited for: 4 -> 3; matrix products, arithmetic and copies ran while one was open for 0% -> 0% of each run, Pallas kernels for 42% -> 41%
where the time goes in v4:
time: 68.3 us; the launch traced here: 68.2 us
  Pallas kernels  48.4 us (71%)
  starting transfers between devices  15.9 us (23%)
  waiting for transfers between devices  2.9 us (4%)
  between operations  0.86 us (1%)
    pallas_call x7, Pallas kernels, join(): pl.pallas_call(lambda *refs: join_kernel(plane, d, part * vel_part, span,...  15.1 us
    pallas_call x2, Pallas kernels, per_device(): pl.pallas_call(lambda *refs, part=part: sweep_kernel(part, rows, plane, P...  12.5 us
    pallas_call x1, Pallas kernels, per_device(): pl.pallas_call(lambda *refs: finish_kernel(plane, PARTS, *refs), out_shap...  9.9 us
    ppermute x6, starting transfers between devices, per_device(): lax.ppermute(sent[part][s - 1], 'gx', [(i, i ^ s) for i in range(count)])  8.1 us
    pallas_call x1, Pallas kernels, per_device(): pl.pallas_call(lambda *refs: moment_kernel(plane, PARTS, *refs), out_shap...  5.96 us
    ppermute x1, starting transfers between devices, per_device(): got = lax.ppermute(total, 'vert', [(v, v ^ step) for v in range(size)])  2.83 us
    pallas_call x2, Pallas kernels, per_device(): pl.pallas_call(lambda *refs, part=part, last=last: correct_kernel(plane,...  2.49 us
    ppermute x2, starting transfers between devices, per_device(): lax.ppermute(total if i else other, 'vert', [(v, v ^ step) for v in range...  2.15 us
  transfers between devices with their start and end apart: 12, of which 3 were waited for; matrix products, arithmetic and copies ran while one was open for 0% of the time, Pallas kernels for 41%

profile of v4, /device:TPU:0, one launch (start us, length us, event | category | flops | bytes accessed | tf_op | source)
XLA Modules:
  0.0 68.2 jit_solution(2630081187263671717)
XLA Ops:
  0.6 6.8 %sweep.2 = (f32[2,256,6144]{2,1,0:T(8,128)S(1)}, f32[392,128]{1,0:T(8,128)S(1)}, f32[392,128]{1,0:T(8,128)S(1)}, f32[392,128]{1,0:T(8,128)S(1)}, f32[2,32,512]{2...) custom-call(f32[2,512,6144]{2,1,0:T(8,128)} %refs_0_.3, ...), custom_call_target="tpu_custom_call" | custom-call | tf_op jit(solution)/shard_map/sweep/pallas_call | solution.py:598
  7.4 3.0 %collective-permute-start = (f32[392,128]{1,0:T(8,128)S(1)}, f32[392,128]{1,0:T(8,128)S(1)}, u32[]{:S(2)}, u32[]{:S(2)}) collective-permute-start(f32[392,128]{1,0:T(8,128)S(1)} %get-tuple-element.39), channel_id=1, source_target_pairs={{0,8},{8,0},{16,24},{24,16},{1,9},{9,1},{17,25},{25,17},{2,10},{10... | collective-permute-start | bytes 602120 | tf_op jit(solution)/shard_map/ppermute | solution.py:664
  10.4 1.5 %collective-permute-start.1 = (f32[392,128]{1,0:T(8,128)S(1)}, f32[392,128]{1,0:T(8,128)S(1)}, u32[]{:S(2)}, u32[]{:S(2)}) collective-permute-start(f32[392,128]{1,0:T(8,128)S(1)} %get-tuple-element.40), channel_id=1, source_target_pairs={{0,16},{8,24},{16,0},{24,8},{1,17},{9,25},{17,1},{25,9},{2,18},{10... | collective-permute-start | bytes 602120 | tf_op jit(solution)/shard_map/ppermute | solution.py:664
  11.9 0.0 collective-permute-start.2
  11.9 0.0 copy-start.2
  11.9 0.0 copy-start.1
  11.9 0.0 copy-start
  12.0 5.7 %sweep.3 = (f32[2,256,6144]{2,1,0:T(8,128)S(1)}, f32[392,128]{1,0:T(8,128)S(1)}, f32[392,128]{1,0:T(8,128)S(1)}, f32[392,128]{1,0:T(8,128)S(1)}) custom-call(f32[2,512,6144]{2,1,0:T(8,128)} %refs_0_.3, bf16[2,512,128]{2,1,0:T(8,128)(2,1)S(1)} %get-tuple-element.32.refs_1_, f32[4,8,128]{2,1,0:T(8,128)S(1)} %get-tuple-element.33.refs_2_, ...), custom_call_target="tpu_custom_call" | custom-call | tf_op jit(solution)/shard_map/sweep/pallas_call | solution.py:598
  17.7 2.0 %collective-permute-start.3 = (f32[392,128]{1,0:T(8,128)S(1)}, f32[392,128]{1,0:T(8,128)S(1)}, u32[]{:S(2)}, u32[]{:S(2)}) collective-permute-start(f32[392,128]{1,0:T(8,128)S(1)} %get-tuple-element.45), channel_id=1, source_target_pairs={{0,8},{8,0},{16,24},{24,16},{1,9},{9,1},{17,25},{25,17},{2,10},{10... | collective-permute-start | bytes 602120 | tf_op jit(solution)/shard_map/ppermute | solution.py:664
  19.7 1.5 %collective-permute-start.4 = (f32[392,128]{1,0:T(8,128)S(1)}, f32[392,128]{1,0:T(8,128)S(1)}, u32[]{:S(2)}, u32[]{:S(2)}) collective-permute-start(f32[392,128]{1,0:T(8,128)S(1)} %get-tuple-element.46), channel_id=1, source_target_pairs={{0,16},{8,24},{16,0},{24,8},{1,17},{9,25},{17,1},{25,9},{2,18},{10... | collective-permute-start | bytes 602120 | tf_op jit(solution)/shard_map/ppermute | solution.py:664
  21.2 0.0 collective-permute-done.refs_3_
  21.2 0.0 collective-permute-start.5
  21.2 0.0 copy-done.2
  21.3 0.0 copy-done.1
  21.3 0.0 copy-done
  21.3 6.0 %moments.1 = (f32[16,6144]{1,0:T(8,128)S(1)}, bf16[2,512,512]{2,1,0:T(8,128)(2,1)S(1)}, bf16[2,512,512]{2,1,0:T(8,128)(2,1)S(1)}) custom-call(f32[2,32,512]{2,1,0:T(8,128)S(1)} %get-tuple-element.31.refs_0_.reach, f32[2,16,512]{2,1,0:T(8,128)S(1)} %pad.4.refs_1_, f32[2,256,6144]{2,1,0:T(8,128)S(1)} %get-tuple-element.30.refs_2_.refs_0_, ...), custom_call_target="tpu_custom_call" | custom-call | tf_op jit(solution)/shard_map/moments/pallas_call | solution.py:617
  27.3 0.3 tables.1
  27.6 0.0 collective-permute-done.1.refs_4_
  27.6 0.0 collective-permute-done.2.refs_5_
  27.6 1.1 %correct.2 = (f32[2,256,384]{2,1,0:T(8,128)S(1)}, f32[16,6144]{1,0:T(8,128)S(1)}) custom-call(f32[16,6144]{1,0:T(8,128)S(1)} %get-tuple-element.36._.refs_0_, bf16[2,512,512]{2,1,0:T(8,128)(2,1)S(1)} %get-tuple-element.37.refs_1_, bf16[2,512,512]{2,1,0:T(8,128)(2,1)S(1)} %get-tuple-element.38.refs_2_, f32[392,128]{1,0:T(8,128)S(1)} %collective-permute-done.refs_3_, ...), custom_call_target="tpu_custom_call" | custom-call | tf_op jit(solution)/shard_map/correct/pallas_call | solution.py:667
  28.8 1.9 %join.7.refs_6_.refs_0_ = f32[2,256,6144]{2,1,0:T(8,128)S(1)} custom-call(f32[2,256,6144]{2,1,0:T(8,128)S(1)} %get-tuple-element.30.refs_2_.refs_0_, f32[2,256,384]{2,1,0:T(8,128)S(1)} %get-tuple-element.43.refs_1_.refs_4_, bf16[2,512,128]{2,1,0:T(8,128)(2,1)S(1)} %get-tuple-element.42.refs_6_.refs_2_, ...), custom_call_target="tpu_custom_call", output_to_operand_aliasing={{}: (0, {})} | custom-call | flops 402653184 | bytes 6291456 | tf_op jit(solution)/shard_map/join/pallas_call | solution.py:644
  30.6 0.0 collective-permute-done.3.refs_3_
  30.6 0.0 collective-permute-done.4.refs_4_
  30.7 0.0 collective-permute-done.5.refs_5_
  30.7 1.4 %correct.3 = (f32[2,256,384]{2,1,0:T(8,128)S(1)}, f32[312,128]{1,0:T(8,128)S(1)}, f32[312,128]{1,0:T(8,128)S(1)}) custom-call(f32[16,6144]{1,0:T(8,128)S(1)} %get-tuple-element.44.refs_0_, bf16[2,512,512]{2,1,0:T(8,128)(2,1)S(1)} %get-tuple-element.37.refs_1_, bf16[2,512,512]{2,1,0:T(8,128)(2,1)S(1)} %get-tuple-element.38.refs_2_, ...), custom_call_target="tpu_custom_call" | custom-call | tf_op jit(solution)/shard_map/correct/pallas_call | solution.py:667
  32.0 0.1 collective-permute-start.6
  32.1 1.4 %collective-permute-done.6.b = f32[312,128]{1,0:T(8,128)S(1)} collective-permute-done((f32[312,128]{1,0:T(8,128)S(1)}, f32[312,128]{1,0:T(8,128)S(1)}, u32[]{:S(2)}, u32[]{:S(2)}) %collective-permute-start.6) | collective-permute-done | bytes 159776 | tf_op jit(solution)/shard_map/ppermute | solution.py:701
  33.5 2.1 %collective-permute-start.7 = (f32[312,128]{1,0:T(8,128)S(1)}, f32[312,128]{1,0:T(8,128)S(1)}, u32[]{:S(2)}, u32[]{:S(2)}) collective-permute-start(f32[312,128]{1,0:T(8,128)S(1)} %add.5.refs_4_.refs_0_), channel_id=1, source_target_pairs={{0,2},{1,3},{2,0},{3,1},{4,6},{5,7},{6,4},{7,5},{8,10},{9,11},{10,... | collective-permute-start | bytes 479240 | tf_op jit(solution)/shard_map/ppermute | solution.py:701
  35.6 1.9 %join.8.refs_0_ = f32[2,256,6144]{2,1,0:T(8,128)S(1)} custom-call(f32[2,256,6144]{2,1,0:T(8,128)S(1)} %join.7.refs_6_.refs_0_, f32[2,256,384]{2,1,0:T(8,128)S(1)} %get-tuple-element.43.refs_1_.refs_4_, bf16[2,512,128]{2,1,0:T(8,128)(2,1)S(1)} %get-tuple-element.42.refs_6_.refs_2_, ...), custom_call_target="tpu_custom_call", output_to_operand_aliasing={{}: (0, {})} | custom-call | flops 402653184 | bytes 6291456 | tf_op jit(solution)/shard_map/join/pallas_call | solution.py:644
  37.5 1.9 %join.9.refs_2_.refs_0_ = f32[2,256,6144]{2,1,0:T(8,128)S(1)} custom-call(f32[2,256,6144]{2,1,0:T(8,128)S(1)} %join.8.refs_0_, f32[2,256,384]{2,1,0:T(8,128)S(1)} %get-tuple-element.43.refs_1_.refs_4_, bf16[2,512,128]{2,1,0:T(8,128)(2,1)S(1)} %get-tuple-element.42.refs_6_.refs_2_, ...), custom_call_target="tpu_custom_call", output_to_operand_aliasing={{}: (0, {})} | custom-call | flops 402653184 | bytes 6291456 | tf_op jit(solution)/shard_map/join/pallas_call | solution.py:644
  39.4 0.6 collective-permute-done.7.refs_1_
  40.0 2.8 %collective-permute-start.9 = (f32[312,128]{1,0:T(8,128)S(1)}, f32[312,128]{1,0:T(8,128)S(1)}, u32[]{:S(2)}, u32[]{:S(2)}) collective-permute-start(f32[312,128]{1,0:T(8,128)S(1)} %get-tuple-element.52.refs_4_.a), channel_id=1, source_target_pairs={{0,4},{1,5},{2,6},{3,7},{4,0},{5,1},{6,2},{7,3},{8,12},{9,13},{10,... | collective-permute-start | bytes 479240 | tf_op jit(solution)/shard_map/ppermute | solution.py:712
  42.9 0.7 collective-permute-start.8
  43.5 3.7 %join.11.refs_0_ = f32[2,256,6144]{2,1,0:T(8,128)S(1)} custom-call(f32[2,256,6144]{2,1,0:T(8,128)S(1)} %get-tuple-element.35.refs_3_.refs_0_, f32[2,256,384]{2,1,0:T(8,128)S(1)} %get-tuple-element.51.refs_1_, bf16[2,512,128]{2,1,0:T(8,128)(2,1)S(1)} %get-tuple-element.42.refs_6_.refs_2_, ...), custom_call_target="tpu_custom_call", output_to_operand_aliasing={{}: (0, {})} | custom-call | flops 805306368 | bytes 12582912 | tf_op jit(solution)/shard_map/join/pallas_call | solution.py:644
  47.3 0.0 collective-permute-done.8.refs_4_.halo
  47.3 0.2 collective-permute-start.10
  47.5 1.9 %join.10.refs_0_ = f32[2,256,6144]{2,1,0:T(8,128)S(1)} custom-call(f32[2,256,6144]{2,1,0:T(8,128)S(1)} %join.9.refs_2_.refs_0_, f32[2,256,384]{2,1,0:T(8,128)S(1)} %get-tuple-element.43.refs_1_.refs_4_, bf16[2,512,128]{2,1,0:T(8,128)(2,1)S(1)} %get-tuple-element.42.refs_6_.refs_2_, ...), custom_call_target="tpu_custom_call", output_to_operand_aliasing={{}: (0, {})} | custom-call | flops 402653184 | bytes 6291456 | tf_op jit(solution)/shard_map/join/pallas_call | solution.py:644
  49.4 1.9 %join.12.refs_1_.refs_0_ = f32[2,256,6144]{2,1,0:T(8,128)S(1)} custom-call(f32[2,256,6144]{2,1,0:T(8,128)S(1)} %join.11.refs_0_, f32[2,256,384]{2,1,0:T(8,128)S(1)} %get-tuple-element.51.refs_1_, bf16[2,512,128]{2,1,0:T(8,128)(2,1)S(1)} %get-tuple-element.42.refs_6_.refs_2_, ...), custom_call_target="tpu_custom_call", output_to_operand_aliasing={{}: (0, {})} | custom-call | flops 402653184 | bytes 6291456 | tf_op jit(solution)/shard_map/join/pallas_call | solution.py:644
  51.4 0.9 %collective-permute-done.10.more = f32[80,128]{1,0:T(8,128)S(1)} collective-permute-done((f32[80,128]{1,0:T(8,128)S(1)}, f32[80,128]{1,0:T(8,128)S(1)}, u32[]{:S(2)}, u32[]{:S(2)}) %collective-permute-start.10) | collective-permute-done | bytes 40992 | tf_op jit(solution)/shard_map/ppermute | solution.py:720
  52.3 0.0 collective-permute-done.9.b
  52.3 1.9 %collective-permute-start.11 = (f32[392,128]{1,0:T(8,128)S(1)}, f32[392,128]{1,0:T(8,128)S(1)}, u32[]{:S(2)}, u32[]{:S(2)}) collective-permute-start(f32[392,128]{1,0:T(8,128)S(1)} %add.7.refs_4_.refs_0_), channel_id=1, source_target_pairs={{0,1},{1,0},{2,3},{3,2},{4,5},{5,4},{6,7},{7,6},{8,9},{9,8},{10,11... | collective-permute-start | bytes 602120 | tf_op jit(solution)/shard_map/ppermute | solution.py:724
  54.2 1.9 %join.13.refs_1_ = f32[2,256,6144]{2,1,0:T(8,128)S(1)} custom-call(f32[2,256,6144]{2,1,0:T(8,128)S(1)} %join.12.refs_1_.refs_0_, f32[2,256,384]{2,1,0:T(8,128)S(1)} %get-tuple-element.51.refs_1_, bf16[2,512,128]{2,1,0:T(8,128)(2,1)S(1)} %get-tuple-element.42.refs_6_.refs_2_, ...), custom_call_target="tpu_custom_call", output_to_operand_aliasing={{}: (0, {})} | custom-call | flops 402653184 | bytes 6291456 | tf_op jit(solution)/shard_map/join/pallas_call | solution.py:644
  56.2 0.0 collective-permute-done.11.refs_1_
  56.2 2.1 %fit.1 = (f32[13,6144]{1,0:T(8,128)}, bf16[128,6144]{1,0:T(8,128)(2,1)S(1)}, bf16[128,6144]{1,0:T(8,128)(2,1)S(1)}) custom-call(f32[392,128]{1,0:T(8,128)S(1)} %add.7.refs_4_.refs_0_, f32[392,128]{1,0:T(8,128)S(1)} %collective-permute-done.11.refs_1_), custom_call_target="tpu_custom_call" | custom-call | tf_op jit(solution)/shard_map/fit/pallas_call | solution.py:727
  58.3 9.9 %finish.1 = f32[2,512,6144]{2,1,0:T(8,128)} custom-call(f32[2,256,6144]{2,1,0:T(8,128)S(1)} %join.10.refs_0_, f32[2,256,6144]{2,1,0:T(8,128)S(1)} %join.13.refs_1_, bf16[2,512,128]{2,1,0:T(8,128)(2,1)S(1)} %get-tuple-element.53.refs_2_, bf16[2,512,128]{2,1,0:T(8,128)(2,1)S(1)} %get-tuple-element.54.refs_3_, bf16[128,6144]{1,0:T(8,128)(2,1)S(1)} %get-tuple-element.55.refs_4_, ...), custom_call_target="tpu_custom_call" | custom-call | tf_op jit(solution)/shard_map/finish/pallas_call | solution.py:739
  (7 shorter events, 0.1 us)
Async XLA Ops:
  7.4 13.8 %collective-permute-start = (f32[392,128]{1,0:T(8,128)S(1)}, f32[392,128]{1,0:T(8,128)S(1)}, u32[]{:S(2)}, u32[]{:S(2)}) collective-permute-start(f32[392,128]{1,0:T(8,128)S(1)} %get-tuple-element.39), channel_id=1, source_target_pairs={{0,8},{8,0},{16,24},{24,16},{1,9},{9,1},{17,25},{25,17},{2,10},{10... | collective-permute-start | bytes 602120 | tf_op jit(solution)/shard_map/ppermute | solution.py:664
  10.4 17.2 %collective-permute-start.1 = (f32[392,128]{1,0:T(8,128)S(1)}, f32[392,128]{1,0:T(8,128)S(1)}, u32[]{:S(2)}, u32[]{:S(2)}) collective-permute-start(f32[392,128]{1,0:T(8,128)S(1)} %get-tuple-element.40), channel_id=1, source_target_pairs={{0,16},{8,24},{16,0},{24,8},{1,17},{9,25},{17,1},{25,9},{2,18},{10... | collective-permute-start | bytes 602120 | tf_op jit(solution)/shard_map/ppermute | solution.py:664
  11.9 15.7 %collective-permute-start.2 = (f32[392,128]{1,0:T(8,128)S(1)}, f32[392,128]{1,0:T(8,128)S(1)}, u32[]{:S(2)}, u32[]{:S(2)}) collective-permute-start(f32[392,128]{1,0:T(8,128)S(1)} %get-tuple-element.41), channel_id=1, source_target_pairs={{0,24},{8,16},{16,8},{24,0},{1,25},{9,17},{17,9},{25,1},{2,26},{10... | collective-permute-start | bytes 602120 | tf_op jit(solution)/shard_map/ppermute | solution.py:664
  11.9 9.3 %copy-start.2 = (f32[2,512]{1,0:T(2,128)S(1)}, f32[2,512]{1,0:T(2,128)}, u32[]{:S(2)}) copy-start(f32[2,512]{1,0:T(2,128)} %param.9) | copy-start | bytes 12292
  11.9 9.3 %copy-start.1 = (f32[3,2,512]{2,1,0:T(2,128)S(1)}, f32[3,2,512]{2,1,0:T(2,128)}, u32[]{:S(2)}) copy-start(f32[3,2,512]{2,1,0:T(2,128)} %param.7) | copy-start | bytes 36868
  11.9 9.3 %copy-start = (f32[13,2,512]{2,1,0:T(2,128)S(1)}, f32[13,2,512]{2,1,0:T(2,128)}, u32[]{:S(2)}) copy-start(f32[13,2,512]{2,1,0:T(2,128)} %param.8) | copy-start | bytes 159748
  17.7 13.0 %collective-permute-start.3 = (f32[392,128]{1,0:T(8,128)S(1)}, f32[392,128]{1,0:T(8,128)S(1)}, u32[]{:S(2)}, u32[]{:S(2)}) collective-permute-start(f32[392,128]{1,0:T(8,128)S(1)} %get-tuple-element.45), channel_id=1, source_target_pairs={{0,8},{8,0},{16,24},{24,16},{1,9},{9,1},{17,25},{25,17},{2,10},{10... | collective-permute-start | bytes 602120 | tf_op jit(solution)/shard_map/ppermute | solution.py:664
  19.7 11.0 %collective-permute-start.4 = (f32[392,128]{1,0:T(8,128)S(1)}, f32[392,128]{1,0:T(8,128)S(1)}, u32[]{:S(2)}, u32[]{:S(2)}) collective-permute-start(f32[392,128]{1,0:T(8,128)S(1)} %get-tuple-element.46), channel_id=1, source_target_pairs={{0,16},{8,24},{16,0},{24,8},{1,17},{9,25},{17,1},{25,9},{2,18},{10... | collective-permute-start | bytes 602120 | tf_op jit(solution)/shard_map/ppermute | solution.py:664
  21.2 9.4 %collective-permute-start.5 = (f32[392,128]{1,0:T(8,128)S(1)}, f32[392,128]{1,0:T(8,128)S(1)}, u32[]{:S(2)}, u32[]{:S(2)}) collective-permute-start(f32[392,128]{1,0:T(8,128)S(1)} %get-tuple-element.47), channel_id=1, source_target_pairs={{0,24},{8,16},{16,8},{24,0},{1,25},{9,17},{17,9},{25,1},{2,26},{10... | collective-permute-start | bytes 602120 | tf_op jit(solution)/shard_map/ppermute | solution.py:664
  32.0 1.5 %collective-permute-start.6 = (f32[312,128]{1,0:T(8,128)S(1)}, f32[312,128]{1,0:T(8,128)S(1)}, u32[]{:S(2)}, u32[]{:S(2)}) collective-permute-start(f32[312,128]{1,0:T(8,128)S(1)} %get-tuple-element.49), channel_id=1, source_target_pairs={{0,1},{1,0},{2,3},{3,2},{4,5},{5,4},{6,7},{7,6},{8,9},{9,8},{10,11... | collective-permute-start | bytes 479240 | tf_op jit(solution)/shard_map/ppermute | solution.py:701
  33.5 6.5 %collective-permute-start.7 = (f32[312,128]{1,0:T(8,128)S(1)}, f32[312,128]{1,0:T(8,128)S(1)}, u32[]{:S(2)}, u32[]{:S(2)}) collective-permute-start(f32[312,128]{1,0:T(8,128)S(1)} %add.5.refs_4_.refs_0_), channel_id=1, source_target_pairs={{0,2},{1,3},{2,0},{3,1},{4,6},{5,7},{6,4},{7,5},{8,10},{9,11},{10,... | collective-permute-start | bytes 479240 | tf_op jit(solution)/shard_map/ppermute | solution.py:701
  40.0 12.2 %collective-permute-start.9 = (f32[312,128]{1,0:T(8,128)S(1)}, f32[312,128]{1,0:T(8,128)S(1)}, u32[]{:S(2)}, u32[]{:S(2)}) collective-permute-start(f32[312,128]{1,0:T(8,128)S(1)} %get-tuple-element.52.refs_4_.a), channel_id=1, source_target_pairs={{0,4},{1,5},{2,6},{3,7},{4,0},{5,1},{6,2},{7,3},{8,12},{9,13},{10,... | collective-permute-start | bytes 479240 | tf_op jit(solution)/shard_map/ppermute | solution.py:712
  42.9 4.4 %collective-permute-start.8 = (f32[80,128]{1,0:T(8,128)S(1)}, f32[80,128]{1,0:T(8,128)S(1)}, u32[]{:S(2)}, u32[]{:S(2)}) collective-permute-start(f32[80,128]{1,0:T(8,128)S(1)} %get-tuple-element.50), channel_id=1, source_target_pairs={{1,8},{8,1},{3,10},{10,3},{5,12},{12,5},{7,14},{14,7},{9,16},{16,9... | collective-permute-start | bytes 122888 | tf_op jit(solution)/shard_map/ppermute | solution.py:718
  47.3 5.0 %collective-permute-start.10 = (f32[80,128]{1,0:T(8,128)S(1)}, f32[80,128]{1,0:T(8,128)S(1)}, u32[]{:S(2)}, u32[]{:S(2)}) collective-permute-start(f32[80,128]{1,0:T(8,128)S(1)} %collective-permute-done.8.refs_4_.halo), channel_id=1, source_target_pairs={{0,4},{1,5},{2,6},{3,7},{4,0},{5,1},{6,2},{7,3},{8,12},{9,13},{10,... | collective-permute-start | bytes 122888 | tf_op jit(solution)/shard_map/ppermute | solution.py:720
  52.3 3.9 %collective-permute-start.11 = (f32[392,128]{1,0:T(8,128)S(1)}, f32[392,128]{1,0:T(8,128)S(1)}, u32[]{:S(2)}, u32[]{:S(2)}) collective-permute-start(f32[392,128]{1,0:T(8,128)S(1)} %add.7.refs_4_.refs_0_), channel_id=1, source_target_pairs={{0,1},{1,0},{2,3},{3,2},{4,5},{5,4},{6,7},{7,6},{8,9},{9,8},{10,11... | collective-permute-start | bytes 602120 | tf_op jit(solution)/shard_map/ppermute | solution.py:724

commit v5 on v4

--- a/solution.py
+++ b/solution.py
@@ -259,10 +259,10 @@
                 out[:, pl.ds(pl.multiple_of(behind * width, width), width)] += moved
         out[:, at] += here
 
-    @pl.loop(0, pairs // GROUP)
+    @pl.loop(0, pairs // (2 * GROUP))
     def _(i):
-        for u in range(GROUP):
-            pair(GROUP * i + u)
+        for u in range(2 * GROUP):
+            pair(2 * GROUP * i + u)
 
 
 def correct_kernel(plane, part, last, number, moments, high_lhs, rest_lhs, *refs):

time: 68.3 us -> 67.9 us (level)
  no operation moved by 1% of the time
where the time goes in v5:
time: 67.9 us; the launch traced here: 67.7 us
  Pallas kernels  48 us (71%)
  starting transfers between devices  15.9 us (23%)
  waiting for transfers between devices  2.89 us (4%)
  between operations  0.86 us (1%)
    pallas_call x7, Pallas kernels, join(): pl.pallas_call(lambda *refs: join_kernel(plane, d, part * vel_part, span,...  15.2 us
    pallas_call x2, Pallas kernels, per_device(): pl.pallas_call(lambda *refs, part=part: sweep_kernel(part, rows, plane, P...  12.6 us
    pallas_call x1, Pallas kernels, per_device(): pl.pallas_call(lambda *refs: finish_kernel(plane, PARTS, *refs), out_shap...  9.9 us
    ppermute x6, starting transfers between devices, per_device(): lax.ppermute(sent[part][s - 1], 'gx', [(i, i ^ s) for i in range(count)])  8.13 us
    pallas_call x1, Pallas kernels, per_device(): pl.pallas_call(lambda *refs: moment_kernel(plane, PARTS, *refs), out_shap...  5.56 us
    ppermute x1, starting transfers between devices, per_device(): got = lax.ppermute(total, 'vert', [(v, v ^ step) for v in range(size)])  2.81 us
    pallas_call x2, Pallas kernels, per_device(): pl.pallas_call(lambda *refs, part=part, last=last: correct_kernel(plane,...  2.31 us
    ppermute x2, starting transfers between devices, per_device(): lax.ppermute(total if i else other, 'vert', [(v, v ^ step) for v in range...  2.11 us
  transfers between devices with their start and end apart: 12, of which 3 were waited for; matrix products, arithmetic and copies ran while one was open for 0% of the time, Pallas kernels for 41%

profile of v5, /device:TPU:0, one launch (start us, length us, event | category | flops | bytes accessed | tf_op | source)
XLA Modules:
  0.0 67.7 jit_solution(3126893290269040587)
XLA Ops:
  0.6 6.8 %sweep.2 = (f32[2,256,6144]{2,1,0:T(8,128)S(1)}, f32[392,128]{1,0:T(8,128)S(1)}, f32[392,128]{1,0:T(8,128)S(1)}, f32[392,128]{1,0:T(8,128)S(1)}, f32[2,32,512]{2...) custom-call(f32[2,512,6144]{2,1,0:T(8,128)} %refs_0_.3, ...), custom_call_target="tpu_custom_call" | custom-call | tf_op jit(solution)/shard_map/sweep/pallas_call | solution.py:598
  7.4 3.0 %collective-permute-start = (f32[392,128]{1,0:T(8,128)S(1)}, f32[392,128]{1,0:T(8,128)S(1)}, u32[]{:S(2)}, u32[]{:S(2)}) collective-permute-start(f32[392,128]{1,0:T(8,128)S(1)} %get-tuple-element.39), channel_id=1, source_target_pairs={{0,8},{8,0},{16,24},{24,16},{1,9},{9,1},{17,25},{25,17},{2,10},{10... | collective-permute-start | bytes 602120 | tf_op jit(solution)/shard_map/ppermute | solution.py:664
  10.4 1.5 %collective-permute-start.1 = (f32[392,128]{1,0:T(8,128)S(1)}, f32[392,128]{1,0:T(8,128)S(1)}, u32[]{:S(2)}, u32[]{:S(2)}) collective-permute-start(f32[392,128]{1,0:T(8,128)S(1)} %get-tuple-element.40), channel_id=1, source_target_pairs={{0,16},{8,24},{16,0},{24,8},{1,17},{9,25},{17,1},{25,9},{2,18},{10... | collective-permute-start | bytes 602120 | tf_op jit(solution)/shard_map/ppermute | solution.py:664
  11.9 0.0 collective-permute-start.2
  11.9 0.0 copy-start.2
  11.9 0.0 copy-start.1
  11.9 0.0 copy-start
  12.0 5.9 %sweep.3 = (f32[2,256,6144]{2,1,0:T(8,128)S(1)}, f32[392,128]{1,0:T(8,128)S(1)}, f32[392,128]{1,0:T(8,128)S(1)}, f32[392,128]{1,0:T(8,128)S(1)}) custom-call(f32[2,512,6144]{2,1,0:T(8,128)} %refs_0_.3, bf16[2,512,128]{2,1,0:T(8,128)(2,1)S(1)} %get-tuple-element.32.refs_1_, f32[4,8,128]{2,1,0:T(8,128)S(1)} %get-tuple-element.33.refs_2_, ...), custom_call_target="tpu_custom_call" | custom-call | tf_op jit(solution)/shard_map/sweep/pallas_call | solution.py:598
  17.8 2.0 %collective-permute-start.3 = (f32[392,128]{1,0:T(8,128)S(1)}, f32[392,128]{1,0:T(8,128)S(1)}, u32[]{:S(2)}, u32[]{:S(2)}) collective-permute-start(f32[392,128]{1,0:T(8,128)S(1)} %get-tuple-element.45), channel_id=1, source_target_pairs={{0,8},{8,0},{16,24},{24,16},{1,9},{9,1},{17,25},{25,17},{2,10},{10... | collective-permute-start | bytes 602120 | tf_op jit(solution)/shard_map/ppermute | solution.py:664
  19.9 1.6 %collective-permute-start.4 = (f32[392,128]{1,0:T(8,128)S(1)}, f32[392,128]{1,0:T(8,128)S(1)}, u32[]{:S(2)}, u32[]{:S(2)}) collective-permute-start(f32[392,128]{1,0:T(8,128)S(1)} %get-tuple-element.46), channel_id=1, source_target_pairs={{0,16},{8,24},{16,0},{24,8},{1,17},{9,25},{17,1},{25,9},{2,18},{10... | collective-permute-start | bytes 602120 | tf_op jit(solution)/shard_map/ppermute | solution.py:664
  21.4 0.0 collective-permute-done.refs_3_
  21.4 0.0 collective-permute-start.5
  21.4 0.0 copy-done.2
  21.4 0.0 copy-done.1
  21.5 0.0 copy-done
  21.5 5.6 %moments.1 = (f32[16,6144]{1,0:T(8,128)S(1)}, bf16[2,512,512]{2,1,0:T(8,128)(2,1)S(1)}, bf16[2,512,512]{2,1,0:T(8,128)(2,1)S(1)}) custom-call(f32[2,32,512]{2,1,0:T(8,128)S(1)} %get-tuple-element.31.refs_0_.reach, f32[2,16,512]{2,1,0:T(8,128)S(1)} %pad.4.refs_1_, f32[2,256,6144]{2,1,0:T(8,128)S(1)} %get-tuple-element.30.refs_2_.refs_0_, ...), custom_call_target="tpu_custom_call" | custom-call | tf_op jit(solution)/shard_map/moments/pallas_call | solution.py:617
  27.1 0.3 tables.1
  27.4 0.0 collective-permute-done.1.refs_4_
  27.4 0.0 collective-permute-done.2.refs_5_
  27.4 1.1 %correct.2 = (f32[2,256,384]{2,1,0:T(8,128)S(1)}, f32[16,6144]{1,0:T(8,128)S(1)}) custom-call(f32[16,6144]{1,0:T(8,128)S(1)} %get-tuple-element.36._.refs_0_, bf16[2,512,512]{2,1,0:T(8,128)(2,1)S(1)} %get-tuple-element.37.refs_1_, bf16[2,512,512]{2,1,0:T(8,128)(2,1)S(1)} %get-tuple-element.38.refs_2_, f32[392,128]{1,0:T(8,128)S(1)} %collective-permute-done.refs_3_, ...), custom_call_target="tpu_custom_call" | custom-call | tf_op jit(solution)/shard_map/correct/pallas_call | solution.py:667
  28.5 1.9 %join.7.refs_6_.refs_0_ = f32[2,256,6144]{2,1,0:T(8,128)S(1)} custom-call(f32[2,256,6144]{2,1,0:T(8,128)S(1)} %get-tuple-element.30.refs_2_.refs_0_, f32[2,256,384]{2,1,0:T(8,128)S(1)} %get-tuple-element.43.refs_1_.refs_4_, bf16[2,512,128]{2,1,0:T(8,128)(2,1)S(1)} %get-tuple-element.42.refs_6_.refs_2_, ...), custom_call_target="tpu_custom_call", output_to_operand_aliasing={{}: (0, {})} | custom-call | flops 402653184 | bytes 6291456 | tf_op jit(solution)/shard_map/join/pallas_call | solution.py:644
  30.4 0.0 collective-permute-done.3.refs_3_
  30.4 0.0 collective-permute-done.4.refs_4_
  30.4 0.0 collective-permute-done.5.refs_5_
  30.4 1.2 %correct.3 = (f32[2,256,384]{2,1,0:T(8,128)S(1)}, f32[312,128]{1,0:T(8,128)S(1)}, f32[312,128]{1,0:T(8,128)S(1)}) custom-call(f32[16,6144]{1,0:T(8,128)S(1)} %get-tuple-element.44.refs_0_, bf16[2,512,512]{2,1,0:T(8,128)(2,1)S(1)} %get-tuple-element.37.refs_1_, bf16[2,512,512]{2,1,0:T(8,128)(2,1)S(1)} %get-tuple-element.38.refs_2_, ...), custom_call_target="tpu_custom_call" | custom-call | tf_op jit(solution)/shard_map/correct/pallas_call | solution.py:667
  31.6 0.1 collective-permute-start.6
  31.7 1.4 %collective-permute-done.6.b = f32[312,128]{1,0:T(8,128)S(1)} collective-permute-done((f32[312,128]{1,0:T(8,128)S(1)}, f32[312,128]{1,0:T(8,128)S(1)}, u32[]{:S(2)}, u32[]{:S(2)}) %collective-permute-start.6) | collective-permute-done | bytes 159776 | tf_op jit(solution)/shard_map/ppermute | solution.py:701
  33.1 2.0 %collective-permute-start.7 = (f32[312,128]{1,0:T(8,128)S(1)}, f32[312,128]{1,0:T(8,128)S(1)}, u32[]{:S(2)}, u32[]{:S(2)}) collective-permute-start(f32[312,128]{1,0:T(8,128)S(1)} %add.5.refs_4_.refs_0_), channel_id=1, source_target_pairs={{0,2},{1,3},{2,0},{3,1},{4,6},{5,7},{6,4},{7,5},{8,10},{9,11},{10,... | collective-permute-start | bytes 479240 | tf_op jit(solution)/shard_map/ppermute | solution.py:701
  35.2 1.9 %join.8.refs_0_ = f32[2,256,6144]{2,1,0:T(8,128)S(1)} custom-call(f32[2,256,6144]{2,1,0:T(8,128)S(1)} %join.7.refs_6_.refs_0_, f32[2,256,384]{2,1,0:T(8,128)S(1)} %get-tuple-element.43.refs_1_.refs_4_, bf16[2,512,128]{2,1,0:T(8,128)(2,1)S(1)} %get-tuple-element.42.refs_6_.refs_2_, ...), custom_call_target="tpu_custom_call", output_to_operand_aliasing={{}: (0, {})} | custom-call | flops 402653184 | bytes 6291456 | tf_op jit(solution)/shard_map/join/pallas_call | solution.py:644
  37.0 1.9 %join.9.refs_2_.refs_0_ = f32[2,256,6144]{2,1,0:T(8,128)S(1)} custom-call(f32[2,256,6144]{2,1,0:T(8,128)S(1)} %join.8.refs_0_, f32[2,256,384]{2,1,0:T(8,128)S(1)} %get-tuple-element.43.refs_1_.refs_4_, bf16[2,512,128]{2,1,0:T(8,128)(2,1)S(1)} %get-tuple-element.42.refs_6_.refs_2_, ...), custom_call_target="tpu_custom_call", output_to_operand_aliasing={{}: (0, {})} | custom-call | flops 402653184 | bytes 6291456 | tf_op jit(solution)/shard_map/join/pallas_call | solution.py:644
  39.0 0.6 collective-permute-done.7.refs_1_
  39.6 2.8 %collective-permute-start.9 = (f32[312,128]{1,0:T(8,128)S(1)}, f32[312,128]{1,0:T(8,128)S(1)}, u32[]{:S(2)}, u32[]{:S(2)}) collective-permute-start(f32[312,128]{1,0:T(8,128)S(1)} %get-tuple-element.52.refs_4_.a), channel_id=1, source_target_pairs={{0,4},{1,5},{2,6},{3,7},{4,0},{5,1},{6,2},{7,3},{8,12},{9,13},{10,... | collective-permute-start | bytes 479240 | tf_op jit(solution)/shard_map/ppermute | solution.py:712
  42.4 0.7 collective-permute-start.8
  43.1 3.7 %join.11.refs_0_ = f32[2,256,6144]{2,1,0:T(8,128)S(1)} custom-call(f32[2,256,6144]{2,1,0:T(8,128)S(1)} %get-tuple-element.35.refs_3_.refs_0_, f32[2,256,384]{2,1,0:T(8,128)S(1)} %get-tuple-element.51.refs_1_, bf16[2,512,128]{2,1,0:T(8,128)(2,1)S(1)} %get-tuple-element.42.refs_6_.refs_2_, ...), custom_call_target="tpu_custom_call", output_to_operand_aliasing={{}: (0, {})} | custom-call | flops 805306368 | bytes 12582912 | tf_op jit(solution)/shard_map/join/pallas_call | solution.py:644
  46.8 0.0 collective-permute-done.8.refs_4_.halo
  46.8 0.2 collective-permute-start.10
  47.1 1.9 %join.10.refs_0_ = f32[2,256,6144]{2,1,0:T(8,128)S(1)} custom-call(f32[2,256,6144]{2,1,0:T(8,128)S(1)} %join.9.refs_2_.refs_0_, f32[2,256,384]{2,1,0:T(8,128)S(1)} %get-tuple-element.43.refs_1_.refs_4_, bf16[2,512,128]{2,1,0:T(8,128)(2,1)S(1)} %get-tuple-element.42.refs_6_.refs_2_, ...), custom_call_target="tpu_custom_call", output_to_operand_aliasing={{}: (0, {})} | custom-call | flops 402653184 | bytes 6291456 | tf_op jit(solution)/shard_map/join/pallas_call | solution.py:644
  49.0 1.9 %join.12.refs_1_.refs_0_ = f32[2,256,6144]{2,1,0:T(8,128)S(1)} custom-call(f32[2,256,6144]{2,1,0:T(8,128)S(1)} %join.11.refs_0_, f32[2,256,384]{2,1,0:T(8,128)S(1)} %get-tuple-element.51.refs_1_, bf16[2,512,128]{2,1,0:T(8,128)(2,1)S(1)} %get-tuple-element.42.refs_6_.refs_2_, ...), custom_call_target="tpu_custom_call", output_to_operand_aliasing={{}: (0, {})} | custom-call | flops 402653184 | bytes 6291456 | tf_op jit(solution)/shard_map/join/pallas_call | solution.py:644
  50.9 0.9 %collective-permute-done.10.more = f32[80,128]{1,0:T(8,128)S(1)} collective-permute-done((f32[80,128]{1,0:T(8,128)S(1)}, f32[80,128]{1,0:T(8,128)S(1)}, u32[]{:S(2)}, u32[]{:S(2)}) %collective-permute-start.10) | collective-permute-done | bytes 40992 | tf_op jit(solution)/shard_map/ppermute | solution.py:720
  51.8 0.0 collective-permute-done.9.b
  51.8 2.0 %collective-permute-start.11 = (f32[392,128]{1,0:T(8,128)S(1)}, f32[392,128]{1,0:T(8,128)S(1)}, u32[]{:S(2)}, u32[]{:S(2)}) collective-permute-start(f32[392,128]{1,0:T(8,128)S(1)} %add.7.refs_4_.refs_0_), channel_id=1, source_target_pairs={{0,1},{1,0},{2,3},{3,2},{4,5},{5,4},{6,7},{7,6},{8,9},{9,8},{10,11... | collective-permute-start | bytes 602120 | tf_op jit(solution)/shard_map/ppermute | solution.py:724
  53.8 1.9 %join.13.refs_1_ = f32[2,256,6144]{2,1,0:T(8,128)S(1)} custom-call(f32[2,256,6144]{2,1,0:T(8,128)S(1)} %join.12.refs_1_.refs_0_, f32[2,256,384]{2,1,0:T(8,128)S(1)} %get-tuple-element.51.refs_1_, bf16[2,512,128]{2,1,0:T(8,128)(2,1)S(1)} %get-tuple-element.42.refs_6_.refs_2_, ...), custom_call_target="tpu_custom_call", output_to_operand_aliasing={{}: (0, {})} | custom-call | flops 402653184 | bytes 6291456 | tf_op jit(solution)/shard_map/join/pallas_call | solution.py:644
  55.7 0.0 collective-permute-done.11.refs_1_
  55.7 2.1 %fit.1 = (f32[13,6144]{1,0:T(8,128)}, bf16[128,6144]{1,0:T(8,128)(2,1)S(1)}, bf16[128,6144]{1,0:T(8,128)(2,1)S(1)}) custom-call(f32[392,128]{1,0:T(8,128)S(1)} %add.7.refs_4_.refs_0_, f32[392,128]{1,0:T(8,128)S(1)} %collective-permute-done.11.refs_1_), custom_call_target="tpu_custom_call" | custom-call | tf_op jit(solution)/shard_map/fit/pallas_call | solution.py:727
  57.8 9.9 %finish.1 = f32[2,512,6144]{2,1,0:T(8,128)} custom-call(f32[2,256,6144]{2,1,0:T(8,128)S(1)} %join.10.refs_0_, f32[2,256,6144]{2,1,0:T(8,128)S(1)} %join.13.refs_1_, bf16[2,512,128]{2,1,0:T(8,128)(2,1)S(1)} %get-tuple-element.53.refs_2_, bf16[2,512,128]{2,1,0:T(8,128)(2,1)S(1)} %get-tuple-element.54.refs_3_, bf16[128,6144]{1,0:T(8,128)(2,1)S(1)} %get-tuple-element.55.refs_4_, ...), custom_call_target="tpu_custom_call" | custom-call | tf_op jit(solution)/shard_map/finish/pallas_call | solution.py:739
  (7 shorter events, 0.1 us)
Async XLA Ops:
  7.4 14.0 %collective-permute-start = (f32[392,128]{1,0:T(8,128)S(1)}, f32[392,128]{1,0:T(8,128)S(1)}, u32[]{:S(2)}, u32[]{:S(2)}) collective-permute-start(f32[392,128]{1,0:T(8,128)S(1)} %get-tuple-element.39), channel_id=1, source_target_pairs={{0,8},{8,0},{16,24},{24,16},{1,9},{9,1},{17,25},{25,17},{2,10},{10... | collective-permute-start | bytes 602120 | tf_op jit(solution)/shard_map/ppermute | solution.py:664
  10.4 17.0 %collective-permute-start.1 = (f32[392,128]{1,0:T(8,128)S(1)}, f32[392,128]{1,0:T(8,128)S(1)}, u32[]{:S(2)}, u32[]{:S(2)}) collective-permute-start(f32[392,128]{1,0:T(8,128)S(1)} %get-tuple-element.40), channel_id=1, source_target_pairs={{0,16},{8,24},{16,0},{24,8},{1,17},{9,25},{17,1},{25,9},{2,18},{10... | collective-permute-start | bytes 602120 | tf_op jit(solution)/shard_map/ppermute | solution.py:664
  11.9 15.5 %collective-permute-start.2 = (f32[392,128]{1,0:T(8,128)S(1)}, f32[392,128]{1,0:T(8,128)S(1)}, u32[]{:S(2)}, u32[]{:S(2)}) collective-permute-start(f32[392,128]{1,0:T(8,128)S(1)} %get-tuple-element.41), channel_id=1, source_target_pairs={{0,24},{8,16},{16,8},{24,0},{1,25},{9,17},{17,9},{25,1},{2,26},{10... | collective-permute-start | bytes 602120 | tf_op jit(solution)/shard_map/ppermute | solution.py:664
  11.9 9.5 %copy-start.2 = (f32[2,512]{1,0:T(2,128)S(1)}, f32[2,512]{1,0:T(2,128)}, u32[]{:S(2)}) copy-start(f32[2,512]{1,0:T(2,128)} %param.9) | copy-start | bytes 12292
  11.9 9.5 %copy-start.1 = (f32[3,2,512]{2,1,0:T(2,128)S(1)}, f32[3,2,512]{2,1,0:T(2,128)}, u32[]{:S(2)}) copy-start(f32[3,2,512]{2,1,0:T(2,128)} %param.7) | copy-start | bytes 36868
  11.9 9.5 %copy-start = (f32[13,2,512]{2,1,0:T(2,128)S(1)}, f32[13,2,512]{2,1,0:T(2,128)}, u32[]{:S(2)}) copy-start(f32[13,2,512]{2,1,0:T(2,128)} %param.8) | copy-start | bytes 159748
  17.8 12.6 %collective-permute-start.3 = (f32[392,128]{1,0:T(8,128)S(1)}, f32[392,128]{1,0:T(8,128)S(1)}, u32[]{:S(2)}, u32[]{:S(2)}) collective-permute-start(f32[392,128]{1,0:T(8,128)S(1)} %get-tuple-element.45), channel_id=1, source_target_pairs={{0,8},{8,0},{16,24},{24,16},{1,9},{9,1},{17,25},{25,17},{2,10},{10... | collective-permute-start | bytes 602120 | tf_op jit(solution)/shard_map/ppermute | solution.py:664
  19.9 10.6 %collective-permute-start.4 = (f32[392,128]{1,0:T(8,128)S(1)}, f32[392,128]{1,0:T(8,128)S(1)}, u32[]{:S(2)}, u32[]{:S(2)}) collective-permute-start(f32[392,128]{1,0:T(8,128)S(1)} %get-tuple-element.46), channel_id=1, source_target_pairs={{0,16},{8,24},{16,0},{24,8},{1,17},{9,25},{17,1},{25,9},{2,18},{10... | collective-permute-start | bytes 602120 | tf_op jit(solution)/shard_map/ppermute | solution.py:664
  21.4 9.0 %collective-permute-start.5 = (f32[392,128]{1,0:T(8,128)S(1)}, f32[392,128]{1,0:T(8,128)S(1)}, u32[]{:S(2)}, u32[]{:S(2)}) collective-permute-start(f32[392,128]{1,0:T(8,128)S(1)} %get-tuple-element.47), channel_id=1, source_target_pairs={{0,24},{8,16},{16,8},{24,0},{1,25},{9,17},{17,9},{25,1},{2,26},{10... | collective-permute-start | bytes 602120 | tf_op jit(solution)/shard_map/ppermute | solution.py:664
  31.6 1.5 %collective-permute-start.6 = (f32[312,128]{1,0:T(8,128)S(1)}, f32[312,128]{1,0:T(8,128)S(1)}, u32[]{:S(2)}, u32[]{:S(2)}) collective-permute-start(f32[312,128]{1,0:T(8,128)S(1)} %get-tuple-element.49), channel_id=1, source_target_pairs={{0,1},{1,0},{2,3},{3,2},{4,5},{5,4},{6,7},{7,6},{8,9},{9,8},{10,11... | collective-permute-start | bytes 479240 | tf_op jit(solution)/shard_map/ppermute | solution.py:701
  33.1 6.5 %collective-permute-start.7 = (f32[312,128]{1,0:T(8,128)S(1)}, f32[312,128]{1,0:T(8,128)S(1)}, u32[]{:S(2)}, u32[]{:S(2)}) collective-permute-start(f32[312,128]{1,0:T(8,128)S(1)} %add.5.refs_4_.refs_0_), channel_id=1, source_target_pairs={{0,2},{1,3},{2,0},{3,1},{4,6},{5,7},{6,4},{7,5},{8,10},{9,11},{10,... | collective-permute-start | bytes 479240 | tf_op jit(solution)/shard_map/ppermute | solution.py:701
  39.6 12.2 %collective-permute-start.9 = (f32[312,128]{1,0:T(8,128)S(1)}, f32[312,128]{1,0:T(8,128)S(1)}, u32[]{:S(2)}, u32[]{:S(2)}) collective-permute-start(f32[312,128]{1,0:T(8,128)S(1)} %get-tuple-element.52.refs_4_.a), channel_id=1, source_target_pairs={{0,4},{1,5},{2,6},{3,7},{4,0},{5,1},{6,2},{7,3},{8,12},{9,13},{10,... | collective-permute-start | bytes 479240 | tf_op jit(solution)/shard_map/ppermute | solution.py:712
  42.4 4.4 %collective-permute-start.8 = (f32[80,128]{1,0:T(8,128)S(1)}, f32[80,128]{1,0:T(8,128)S(1)}, u32[]{:S(2)}, u32[]{:S(2)}) collective-permute-start(f32[80,128]{1,0:T(8,128)S(1)} %get-tuple-element.50), channel_id=1, source_target_pairs={{1,8},{8,1},{3,10},{10,3},{5,12},{12,5},{7,14},{14,7},{9,16},{16,9... | collective-permute-start | bytes 122888 | tf_op jit(solution)/shard_map/ppermute | solution.py:718
  46.8 5.0 %collective-permute-start.10 = (f32[80,128]{1,0:T(8,128)S(1)}, f32[80,128]{1,0:T(8,128)S(1)}, u32[]{:S(2)}, u32[]{:S(2)}) collective-permute-start(f32[80,128]{1,0:T(8,128)S(1)} %collective-permute-done.8.refs_4_.halo), channel_id=1, source_target_pairs={{0,4},{1,5},{2,6},{3,7},{4,0},{5,1},{6,2},{7,3},{8,12},{9,13},{10,... | collective-permute-start | bytes 122888 | tf_op jit(solution)/shard_map/ppermute | solution.py:720
  51.8 3.9 %collective-permute-start.11 = (f32[392,128]{1,0:T(8,128)S(1)}, f32[392,128]{1,0:T(8,128)S(1)}, u32[]{:S(2)}, u32[]{:S(2)}) collective-permute-start(f32[392,128]{1,0:T(8,128)S(1)} %add.7.refs_4_.refs_0_), channel_id=1, source_target_pairs={{0,1},{1,0},{2,3},{3,2},{4,5},{5,4},{6,7},{7,6},{8,9},{9,8},{10,11... | collective-permute-start | bytes 602120 | tf_op jit(solution)/shard_map/ppermute | solution.py:724
